TPU v7x, 32 devices: a whole 2x2x4 slice. The times are simulated.
32 devices in a mesh: path: 8 (over z, y), fsdp: 4 (over x, core).
Axes of the slice: x: 2, y: 2, z: 4, core: 2. Of those that a mesh axis runs over, the one named last changes fastest.
Arguments:
- tokens: bfloat16 [8, 1024, 4096], P('path', 'fsdp'), may hold values from -6 to 6
- cotangent: bfloat16 [8, 1024, 256], P('path', 'fsdp'), may hold values from -6 to 6
- module_table: int32 [8, 1], replicated, may hold values from 0 to 7
- module_weights: bfloat16 [8, 4096, 256], P(None, 'fsdp'), may hold values from -6 to 6
- momentum: float32 [8, 4096, 256], P(None, 'fsdp'), may hold values from -6 to 6
Outputs:
- new_weights: bfloat16 [8, 4096, 256], P(None, 'fsdp')
- new_momentum: float32 [8, 4096, 256], P(None, 'fsdp')
Inputs may be any that keep to these rules, and one draw needn't show every extreme that they name: `module_table`: every module is taken by at least one path.
All inputs are finite; a program needn't handle non-finite values.
Results may differ from a plain program's by a relative error of at most 0.0034.
Values may be sent and summed in bfloat16 or wider, within the bound.
No kernel may reach another device: no remote copies, remote signals or barrier semaphores. Data moves between devices by JAX's collectives and lax.ppermute only.
A program may use at most 64 MiB of HBM per device.

v0:
```python
import math

import jax
import jax.numpy as jnp
from jax import lax
from jax.sharding import PartitionSpec as P


def outer_update(weights, moment, average):
    new_moment = 0.9 * moment + average
    new_weights = (weights.astype(jnp.float32) - 0.7 * (average + 0.9 * new_moment)).astype(
        jnp.bfloat16
    )
    return (new_weights, new_moment)


def body(tokens, cotangent, module_table, module_weights, momentum):
    local_tokens = tokens[0]
    upstream = cotangent[0].astype(jnp.float32)
    tok_rows = local_tokens.shape[0]
    width = local_tokens.shape[1]
    module_count = module_weights.shape[0]
    path_id = lax.axis_index("path")
    choices_col = module_table[:, 0]
    module = lax.dynamic_index_in_dim(choices_col, path_id, 0, keepdims=False)
    shard_weights = lax.dynamic_index_in_dim(module_weights, module, 0, keepdims=False)
    columns = local_tokens
    latent = jnp.dot(
        columns,
        lax.all_gather(shard_weights, "fsdp", axis=0, tiled=True),
        preferred_element_type=jnp.float32,
    )
    inverse_rms = lax.rsqrt(jnp.mean(latent * latent, axis=-1, keepdims=True) + 1e-06)
    normed = latent * inverse_rms
    latent_cotangent = (
        inverse_rms * (upstream - normed * jnp.mean(upstream * normed, axis=-1, keepdims=True))
    ).astype(jnp.bfloat16)
    columns = local_tokens
    gradient = lax.psum_scatter(
        lax.dot_general(
            columns, latent_cotangent, (((0,), (0,)), ((), ())), preferred_element_type=jnp.float32
        ),
        "fsdp",
        scatter_dimension=0,
        tiled=True,
    )
    path_tokens = tok_rows * lax.axis_size("fsdp")
    delta = gradient * math.sqrt(width / path_tokens)
    module_ids = jnp.arange(module_count, dtype=jnp.int32)
    picked = (module_ids == module).astype(jnp.float32)
    counts = jnp.sum((choices_col[:, None] == module_ids[None, :]).astype(jnp.float32), axis=0)
    summand = picked[:, None, None] * delta[None]
    summed = lax.psum(summand, "path")
    average = summed / counts[:, None, None]
    new_weights, new_moment = outer_update(module_weights, momentum, average)
    return (new_weights, new_moment)


def solution(mesh):
    return jax.shard_map(
        body,
        mesh=mesh,
        in_specs=(
            P("path", "fsdp", None),
            P("path", "fsdp", None),
            P(),
            P(None, "fsdp", None),
            P(None, "fsdp", None),
        ),
        out_specs=(P(None, "fsdp", None), P(None, "fsdp", None)),
        check_vma=False,
    )
```

profile of v0, /device:TPU:0, one launch (start us, length us, event | category | flops | bytes accessed | tf_op | source)
XLA Modules:
  0.0 385.7 jit_solution(16930801982664747659)
XLA Ops:
  7.2 0.0 copy-start
  7.2 0.0 all-gather.3.cloned.1.call-start
  7.2 1.4 constant_dynamic-slice_fusion.1
  10.6 1.9 constant_dynamic-slice_fusion
  12.4 0.0 all-gather.3.cloned.1.call-update
  12.4 0.0 reduce-scatter.2.cloned.1.call-start
  12.5 1.0 copy.9
  13.5 24.4 %all-gather.3.cloned.1.call-done = bf16[1,4096,256]{2,1,0:T(8,128)(2,1)} async-done(((bf16[1,1024,256]{2,1,0:T(8,128)(2,1)}), bf16[1,4096,256]{2,1,0:T(8,128)(2,1)}) %all-gather.3.cloned.1.call-update) | async-done | bytes 2097168 | tf_op jit(solution)/shard_map/all_gather | solution.py:30
  37.9 0.0 copy-done
  37.9 2.4 multiply_reduce_fusion
  40.3 0.1 fusion.4
  40.3 2.7 convolution_bitcast_fusion
  43.1 0.0 reduce-scatter.2.cloned.1.call-update
  43.1 0.0 all-reduce.2.cloned.1.call-start
  43.1 0.7 compare_convert_fusion
  43.8 44.0 %reduce-scatter.2.cloned.1.call-done = f32[1024,256]{0,1:T(8,128)} async-done(((f32[4096,256]{0,1:T(8,128)}), f32[1024,256]{0,1:T(8,128)}) %reduce-scatter.2.cloned.1.call-update) | async-done | bytes 1048592 | tf_op jit(solution)/shard_map/reduce_scatter | solution.py:39
  87.8 2.3 broadcast_multiply_fusion.1
  90.1 1.6 copy.10
  91.6 0.0 copy-start.1
  91.6 4.2 %broadcast_multiply_fusion = f32[8,1024,256]{2,1,0:T(8,128)} fusion(f32[1024,256]{1,0:T(8,128)S(1)} %copy.10, f32[8]{0:T(128)S(1)} %compare_convert_fusion), kind=kLoop, calls=%fused_computation.4 | loop fusion | flops 2097152 | bytes 9437216 | tf_op jit(solution)/shard_map/mul | solution.py:52
  95.8 0.0 all-reduce.2.cloned.1.call-update
  95.8 0.0 copy-done.1
  95.9 0.1 convert_reduce_fusion
  95.9 270.5 %all-reduce.2.cloned.1.call-done = f32[8,1024,256]{2,1,0:T(8,128)} async-done(((f32[8,1024,256]{2,1,0:T(8,128)}), f32[8,1024,256]{2,1,0:T(8,128)}) %all-reduce.2.cloned.1.call-update) | async-done | bytes 8388624 | tf_op jit(solution)/shard_map/psum | solution.py:53
  366.4 12.8 %subtract_convert_fusion = (bf16[8,1024,256]{2,1,0:T(8,128)(2,1)}, f32[8,1024,256]{2,1,0:T(8,128)}) fusion(bf16[8,1024,256]{2,1,0:T(8,128)(2,1)} %param.8, f32[8,1024,256]{2,1,0:T(8,128)} %all-reduce.2.cloned.1.call-done, f32[8]{0:T(128)S(1)} %convert_reduce_fusion, f32[8,1024,256]{2,1,0:T(8,128)} %param.9), kind=kLoop, calls=%fused_computation | loop fusion | flops 18874368 | bytes 33554464 | tf_op jit(solution)/shard_map/convert_element_type | solution.py:11
  (2 shorter events, 0.0 us)
Async XLA Ops:
  7.2 30.7 %copy-start = (bf16[1,256,4096]{2,1,0:T(8,128)(2,1)S(1)}, bf16[1,256,4096]{2,1,0:T(8,128)(2,1)}, u32[]{:S(2)}) copy-start(bf16[1,256,4096]{2,1,0:T(8,128)(2,1)} %param.5) | copy-start | bytes 6291460
  7.2 30.7 %all-gather.3.cloned.1.call-start = ((), (), s32[]{:S(2)}) async-start(), calls=%async_computation.3 | async-start | bytes 2621440 | tf_op jit(solution)/shard_map/all_gather | solution.py:30
  12.4 75.3 %reduce-scatter.2.cloned.1.call-start = ((), (), s32[]{:S(2)}) async-start(), calls=%async_computation.1 | async-start | bytes 5242880 | tf_op jit(solution)/shard_map/reduce_scatter | solution.py:39
  43.1 323.3 %all-reduce.2.cloned.1.call-start = ((), (), s32[]{:S(2)}) async-start(), calls=%async_computation.2 | async-start | bytes 16777216 | tf_op jit(solution)/shard_map/psum | solution.py:53
  91.6 4.2 %copy-start.1 = (s32[8,1]{0,1:T(1,128)S(1)}, s32[8,1]{0,1:T(1,128)}, u32[]{:S(2)}) copy-start(s32[8,1]{0,1:T(1,128)} %param.7) | copy-start | bytes 100
Sparse Core Ops, SparseCore 0:
  12.6 25.2 all-gather.2
  43.2 44.4 reduce-scatter.1
  96.0 270.3 all-reduce.1
where the time goes:
time: 386 us
  waiting for transfers between devices  339 us (88%)
  other arithmetic  20.1 us (5%)
  between operations  15.7 us (4%)
  local copies, waits for them, and re-layouts  5.83 us (2%)
  matrix products  5.09 us (1%)
    psum x1, waiting for transfers between devices, body(): summed = lax.psum(summand, 'path')  270 us
    reduce_scatter x1, waiting for transfers between devices, body(): lax.psum_scatter(lax.dot_general(columns, latent_cotangent, (((0,), (0,))...  44 us
    all_gather x1, waiting for transfers between devices, body(): lax.all_gather(shard_weights, 'fsdp', axis=0, tiled=True)  24.4 us
    convert_element_type x1, other arithmetic, outer_update(): (weights.astype(jnp.float32) - 0.7 * (average + 0.9 * new_moment)).astype...  12.8 us
  transfers between devices with their start and end apart: 3, of which 3 were waited for; matrix products, arithmetic and copies ran while one was open for 0% of the time, Pallas kernels for 0%

commit v1 on v0

v1 whole, which is shorter than its diff:
```python
import math

import jax
import jax.numpy as jnp
import numpy as np
from jax import lax
from jax.experimental import pallas as pl
from jax.experimental.pallas import tpu as pltpu
from jax.sharding import PartitionSpec as P

CHAINS = 2


def outer_update(weights, moment, average):
    new_moment = 0.9 * moment + average
    new_weights = (weights.astype(jnp.float32) - 0.7 * (average + 0.9 * new_moment)).astype(
        jnp.bfloat16
    )
    return (new_weights, new_moment)


def ring_order(paths):
    return [p for p in range(0, paths, 2)] + [p for p in range(paths - 1, 0, -2)]


def ring_plan(paths, shards):
    order = ring_order(paths)
    place = {p: i for i, p in enumerate(order)}
    pairs = []
    source = np.zeros((paths, 2, paths), np.int32)
    for p in range(paths):
        for f in range(shards):
            way = 1 if f % 2 == 0 else -1
            pairs.append((p * shards + f, order[(place[p] + way) % paths] * shards + f))
        for core in range(2):
            way = 1 if core == 0 else -1
            for step in range(paths):
                source[p, core, step] = order[(place[p] - way * step) % paths]
    return pairs, source


def apply_kernel(index_ref, block_ref, weights_ref, moment_ref, *rest):
    new_weights_ref, new_moment_ref = rest[-2:]
    average = block_ref[...].astype(jnp.float32)
    new_weights, new_moment = outer_update(weights_ref[0], moment_ref[0], average)
    new_weights_ref[0] = new_weights
    new_moment_ref[0] = new_moment


def apply_block(modules, step, chain, block, weights, moment, outs):
    rows, width = block.shape
    tile = min(rows, 256)
    tiles = rows // tile

    def spot(i, index):
        return (index[0], chain * tiles + i, 0)

    module = lax.dynamic_slice_in_dim(modules, step, 1)
    spec = pl.BlockSpec((1, tile, width), spot)
    in_specs = [pl.BlockSpec((tile, width), lambda i, index: (i, 0)), spec, spec]
    args = [block, weights, moment]
    aliases = {}
    if outs is not None:
        in_specs += [pl.BlockSpec(memory_space=pl.ANY)] * 2
        args += list(outs)
        aliases = {4: 0, 5: 1}
    return pl.pallas_call(
        apply_kernel,
        grid_spec=pltpu.PrefetchScalarGridSpec(
            num_scalar_prefetch=1, grid=(tiles,), in_specs=in_specs, out_specs=[spec, spec]
        ),
        out_shape=[
            jax.ShapeDtypeStruct(weights.shape, weights.dtype),
            jax.ShapeDtypeStruct(moment.shape, moment.dtype),
        ],
        input_output_aliases=aliases,
        cost_estimate=pl.CostEstimate(
            flops=6 * rows * width, bytes_accessed=14 * rows * width, transcendentals=0
        ),
        name="apply_block",
    )(module, *args)


def body(tokens, cotangent, module_table, module_weights, momentum):
    paths, shards = lax.axis_size("path"), lax.axis_size("fsdp")
    chips = shards // 2
    path_id, shard_id = lax.axis_index("path"), lax.axis_index("fsdp")
    core, chip = shard_id % 2, shard_id // 2
    tok_rows, width = tokens.shape[1:]
    module_count, rows, features = module_weights.shape
    step_size = math.sqrt(width / (tok_rows * shards))
    choices = module_table[:, 0]
    module = lax.dynamic_index_in_dim(choices, path_id, 0, keepdims=False)

    to_core = [(i, i ^ 1) for i in range(shards)]

    def to_chip(step):
        return [(i, (i + 2 * step) % shards) for i in range(shards)]

    own_weights = lax.dynamic_index_in_dim(module_weights, module, 0, keepdims=False)
    blocks = [own_weights] + [
        lax.ppermute(own_weights, "fsdp", to_chip(s)) for s in range(1, chips)
    ]
    split = tokens[0].reshape(tok_rows, chips, 2, rows)
    kept = lax.dynamic_index_in_dim(split, core, 2, keepdims=False)
    given = lax.dynamic_index_in_dim(split, 1 - core, 2, keepdims=False)
    taken = lax.ppermute(given, "fsdp", to_core)
    first = core == 0
    columns = jnp.where(
        first, jnp.concatenate([kept, taken]), jnp.concatenate([taken, kept])
    )
    other_up = lax.ppermute(cotangent[0], "fsdp", to_core)
    upstream = jnp.where(
        first,
        jnp.concatenate([cotangent[0], other_up]),
        jnp.concatenate([other_up, cotangent[0]]),
    ).astype(jnp.float32)

    def chip_columns(index):
        return lax.dynamic_index_in_dim(columns, index, 1, keepdims=False)

    partial = sum(
        jnp.dot(
            chip_columns((chip - s) % chips), blocks[s], preferred_element_type=jnp.float32
        )
        for s in range(chips)
    )
    latent = partial + lax.ppermute(partial, "fsdp", to_core)
    inverse_rms = lax.rsqrt(jnp.mean(latent * latent, axis=-1, keepdims=True) + 1e-06)
    normed = latent * inverse_rms
    latent_cotangent = (
        inverse_rms * (upstream - normed * jnp.mean(upstream * normed, axis=-1, keepdims=True))
    ).astype(jnp.bfloat16)

    def gradient(index, chain, chains):
        part = lax.dynamic_slice_in_dim(
            chip_columns(index), chain * (rows // chains), rows // chains, 1
        )
        return lax.dot_general(
            part, latent_cotangent, (((0,), (0,)), ((), ())), preferred_element_type=jnp.float32
        )

    def path_delta(chain, chains):
        total = gradient(chip, chain, chains)
        for s in range(1, chips):
            there = gradient((chip + s) % chips, chain, chains).astype(jnp.bfloat16)
            total = total + lax.ppermute(there, "fsdp", to_chip(s)).astype(jnp.float32)
        return total * step_size

    if paths != module_count:
        module_ids = jnp.arange(module_count, dtype=jnp.int32)
        picked = (module_ids == module).astype(jnp.float32)
        counts = jnp.sum((choices[:, None] == module_ids[None, :]).astype(jnp.float32), axis=0)
        summed = lax.psum(picked[:, None, None] * path_delta(0, 1)[None], "path")
        return outer_update(module_weights, momentum, summed / counts[:, None, None])

    pairs, source = ring_plan(paths, shards)
    sources = jnp.asarray(source).reshape(paths * 2, paths)
    mine = lax.dynamic_index_in_dim(sources, path_id * 2 + core, 0, keepdims=False)
    modules = jnp.sum(
        jnp.where(mine[:, None] == jnp.arange(paths)[None, :], choices[None, :], 0), axis=1
    ).astype(jnp.int32)
    held = [path_delta(c, CHAINS).astype(jnp.bfloat16) for c in range(CHAINS)]
    outs = None
    for step in range(paths):
        for chain in range(CHAINS):
            block = held[chain]
            if step < paths - 1:
                held[chain] = lax.ppermute(block, ("path", "fsdp"), pairs)
            outs = apply_block(modules, step, chain, block, module_weights, momentum, outs)
    return tuple(outs)


def solution(mesh):
    return jax.shard_map(
        body,
        mesh=mesh,
        in_specs=(
            P("path", "fsdp", None),
            P("path", "fsdp", None),
            P(),
            P(None, "fsdp", None),
            P(None, "fsdp", None),
        ),
        out_specs=(P(None, "fsdp", None), P(None, "fsdp", None)),
        check_vma=False,
    )
```

time: 386 us -> 135 us (0.35)
  waiting for transfers between devices: 339 us -> 35.8 us
  Pallas kernels: 0 us -> 43.7 us
  starting transfers between devices: 0.12 us -> 31.1 us
  other arithmetic: 20.1 us -> 3.14 us
  between operations: 15.7 us -> 2.89 us
  local copies, waits for them, and re-layouts: 5.83 us -> 13 us
    psum x1 -> x0, waiting for transfers between devices: 270 us -> none  [body(): summed = lax.psum(summand, 'path')]
    reduce_scatter x1 -> x0, waiting for transfers between devices: 44 us -> none  [body(): lax.psum_scatter(lax.dot_general(columns, latent_cotangent, (((0,), (0,))...]
    pallas_call x0 -> x16, Pallas kernels: none -> 43.7 us  [apply_block(): pl.pallas_call(apply_kernel, grid_spec=pltpu.PrefetchScalarGridSpec(num_s...]
    ppermute x0 -> x20, waiting for transfers between devices: none -> 35.8 us  [the longest x14 16.6 us: body(): held[chain] = lax.ppermute(block, ('path', 'fsdp'), pairs)]
    ppermute x0 -> x20, starting transfers between devices: none -> 31.1 us  [the longest x14 25.4 us: body(): held[chain] = lax.ppermute(block, ('path', 'fsdp'), pairs)]
    all_gather x1 -> x0, waiting for transfers between devices: 24.4 us -> none  [body(): lax.all_gather(shard_weights, 'fsdp', axis=0, tiled=True)]
    convert_element_type x2 -> x1, other arithmetic: 13.4 us -> 0.13 us  [body(): latent_cotangent = (inverse_rms * (upstream - normed * jnp.mean(upstream...]
    mul x2 -> x0, other arithmetic: 6.49 us -> none  [the longest x1 4.18 us: body(): summand = picked[:, None, None] * delta[None]]
  transfers between devices with their start and end apart: 3 -> 20, of which waited for: 3 -> 16; matrix products, arithmetic and copies ran while one was open for 0% -> 6% of each run, Pallas kernels for 0% -> 31%
where the time goes in v1:
time: 135 us; the launch traced here: 134 us
  Pallas kernels  43.7 us (32%)
  waiting for transfers between devices  35.8 us (27%)
  starting transfers between devices  31.1 us (23%)
  local copies, waits for them, and re-layouts  13 us (10%)
  matrix products  4.44 us (3%)
  other arithmetic  3.14 us (2%)
  between operations  2.89 us (2%)
    pallas_call x16, Pallas kernels, apply_block(): pl.pallas_call(apply_kernel, grid_spec=pltpu.PrefetchScalarGridSpec(num_s...  43.7 us
    ppermute x14, starting transfers between devices, body(): held[chain] = lax.ppermute(block, ('path', 'fsdp'), pairs)  25.4 us
    ppermute x14, waiting for transfers between devices, body(): held[chain] = lax.ppermute(block, ('path', 'fsdp'), pairs)  16.6 us
    ppermute x2, waiting for transfers between devices, path_delta(): total = total + lax.ppermute(there, 'fsdp', to_chip(s)).astype(jnp.float32)  9.28 us
    ppermute x1, waiting for transfers between devices, body(): lax.ppermute(own_weights, 'fsdp', to_chip(s))  8.81 us
    unnamed x38, local copies, waits for them, and re-layouts  5.11 us
    dot_general x2, matrix products, body(): jnp.dot(chip_columns((chip - s) % chips), blocks[s], preferred_element_ty...  3.04 us
  transfers between devices with their start and end apart: 20, of which 16 were waited for; matrix products, arithmetic and copies ran while one was open for 6% of the time, Pallas kernels for 31%

profile of v1, /device:TPU:0, one launch (start us, length us, event | category | flops | bytes accessed | tf_op | source)
XLA Modules:
  0.0 134.0 jit_solution(6497793668451703057)
XLA Ops:
  0.6 3.3 %copy.44 = bf16[1,256,4096]{1,2,0:T(8,128)(2,1)S(1)} copy(bf16[1,256,4096]{2,1,0:T(8,128)(2,1)} %param.6) | data formatting | bytes 4194304 | tf_op args[0]
  4.0 1.1 constant_dynamic-slice_fusion.2
  5.1 2.3 %copy.46 = bf16[256,2,1,1024]{3,0,2,1:T(8,128)(2,1)} copy(bf16[256,2,1,1024]{0,3,2,1:T(8,128)(2,1)} %get-tuple-element.67) | data formatting | bytes 2097152 | tf_op jit(solution)/shard_map/jit(dynamic_index_in_dim)/dynamic_slice | solution.py:106
  7.3 0.5 collective-permute-start
  7.8 0.6 constant_dynamic-slice_fusion
  10.3 1.9 %dynamic-slice_bitcast_fusion.2 = bf16[1024,256]{1,0:T(8,128)(2,1)} fusion(bf16[8,1024,256]{2,1,0:T(8,128)(2,1)} %weights_ref.31, s32[]{:T(128)S(6)} %select_n.91), kind=kLoop, calls=%fused_computation.30 | loop fusion | bytes 1048580 | tf_op jit(solution)/shard_map/jit(dynamic_index_in_dim)/squeeze | solution.py:100
  12.2 2.5 %collective-permute-start.1 = (bf16[1024,256]{1,0:T(8,128)(2,1)}, bf16[1024,256]{1,0:T(8,128)(2,1)}, u32[]{:S(2)}, u32[]{:S(2)}) collective-permute-start(bf16[1024,256]{1,0:T(8,128)(2,1)} %dynamic-slice_bitcast_fusion.2), channel_id=1, source_target_pairs={{0,2},{1,3},{2,0},{3,1},{4,6},{5,7},{6,4},{7,5},{8,10},{9,11},{10,... | collective-permute-start | bytes 1572872 | tf_op jit(solution)/shard_map/ppermute | solution.py:102
  14.7 0.5 copy.45
  15.2 1.0 copy-done
  16.2 2.6 %maximum_select_fusion = bf16[512,2,1024]{2,0,1:T(8,128)(2,1)S(1)} fusion(bf16[256,2,1024]{2,0,1:T(8,128)(2,1)} %copy-done, bf16[256,2,1024]{2,0,1:T(8,128)(2,1)S(1)} %bitcast.29, pred[]{:T(512)S(6)} %eq.28), kind=kLoop, calls=%fused_computation | loop fusion | flops 9437184 | bytes 4194305 | tf_op jit(solution)/shard_map/jit(_where)/select_n | solution.py:109
  18.8 8.8 %collective-permute-done.1 = bf16[1024,256]{1,0:T(8,128)(2,1)} collective-permute-done((bf16[1024,256]{1,0:T(8,128)(2,1)}, bf16[1024,256]{1,0:T(8,128)(2,1)}, u32[]{:S(2)}, u32[]{:S(2)}) %collective-permute-start.1) | collective-permute-done | bytes 524320 | tf_op jit(solution)/shard_map/ppermute | solution.py:102
  27.6 1.5 %fusion = f32[512,256]{0,1:T(8,128)S(1)} fusion(bf16[1024,256]{1,0:T(8,128)(2,1)} %collective-permute-done.1, bf16[512,2,1024]{2,0,1:T(8,128)(2,1)S(1)} %maximum_select_fusion, s32[]{:T(128)S(6)} %select_n.93), kind=kOutput, calls=%fused_computation.3 | convolution fusion | flops 268435456 | bytes 2097156 | tf_op jit(solution)/shard_map/dot_general | solution.py:123
  29.1 1.5 %fusion.4 = f32[512,256]{0,1:T(8,128)S(1)} fusion(f32[512,256]{0,1:T(8,128)S(1)} %fusion, bf16[1024,256]{1,0:T(8,128)(2,1)} %dynamic-slice_bitcast_fusion.2, bf16[512,2,1024]{2,0,1:T(8,128)(2,1)S(1)} %maximum_select_fusion, s32[]{:T(128)S(6)} %select_n.89), kind=kOutput, calls=%fused_computation.7 | convolution fusion | flops 268566528 | bytes 2621444 | tf_op jit(solution)/shard_map/dot_general | solution.py:123
  30.8 0.6 collective-permute-start.3
  31.6 1.0 collective-permute-done.2
  33.1 0.3 convolution_convert_fusion
  33.4 1.8 %collective-permute-start.12 = (bf16[512,256]{1,0:T(8,128)(2,1)S(1)}, bf16[512,256]{1,0:T(8,128)(2,1)S(1)}, u32[]{:S(2)}, u32[]{:S(2)}) collective-permute-start(bf16[512,256]{1,0:T(8,128)(2,1)S(1)} %convolution_convert_fusion), channel_id=1, source_target_pairs={{0,2},{1,3},{2,0},{3,1},{4,6},{5,7},{6,4},{7,5},{8,10},{9,11},{10,... | collective-permute-start | bytes 786440 | tf_op jit(solution)/shard_map/ppermute | solution.py:147
  35.9 6.7 %collective-permute-done.12 = bf16[512,256]{1,0:T(8,128)(2,1)S(1)} collective-permute-done((bf16[512,256]{1,0:T(8,128)(2,1)S(1)}, bf16[512,256]{1,0:T(8,128)(2,1)S(1)}, u32[]{:S(2)}, u32[]{:S(2)}) %collective-permute-start.12) | collective-permute-done | bytes 262176 | tf_op jit(solution)/shard_map/ppermute | solution.py:147
  43.0 1.9 %collective-permute-start.13 = (bf16[512,256]{1,0:T(8,128)(2,1)S(1)}, bf16[512,256]{1,0:T(8,128)(2,1)S(1)}, u32[]{:S(2)}, u32[]{:S(2)}) collective-permute-start(bf16[512,256]{1,0:T(8,128)(2,1)S(1)} %fusion.21.block_ref), channel_id=1, source_target_pairs={{0,8},{1,5},{2,10},{3,7},{4,0},{5,13},{6,2},{7,15},{8,16},{9,1},{1... | collective-permute-start | bytes 786440 | tf_op jit(solution)/shard_map/ppermute | solution.py:169
  44.9 2.6 %collective-permute-done.4 = bf16[512,256]{1,0:T(8,128)(2,1)S(1)} collective-permute-done((bf16[512,256]{1,0:T(8,128)(2,1)S(1)}, bf16[512,256]{1,0:T(8,128)(2,1)S(1)}, u32[]{:S(2)}, u32[]{:S(2)}) %collective-permute-start.4) | collective-permute-done | bytes 262176 | tf_op jit(solution)/shard_map/ppermute | solution.py:147
  47.5 0.3 fusion.33.block_ref
  47.8 1.9 %collective-permute-start.5 = (bf16[512,256]{1,0:T(8,128)(2,1)S(1)}, bf16[512,256]{1,0:T(8,128)(2,1)S(1)}, u32[]{:S(2)}, u32[]{:S(2)}) collective-permute-start(bf16[512,256]{1,0:T(8,128)(2,1)S(1)} %fusion.33.block_ref), channel_id=1, source_target_pairs={{0,8},{1,5},{2,10},{3,7},{4,0},{5,13},{6,2},{7,15},{8,16},{9,1},{1... | collective-permute-start | bytes 786440 | tf_op jit(solution)/shard_map/ppermute | solution.py:169
  49.7 1.6 %collective-permute-start.14 = (bf16[512,256]{1,0:T(8,128)(2,1)S(1)}, bf16[512,256]{1,0:T(8,128)(2,1)S(1)}, u32[]{:S(2)}, u32[]{:S(2)}) collective-permute-start(bf16[512,256]{1,0:T(8,128)(2,1)S(1)} %collective-permute-done.13.block_ref), channel_id=1, source_target_pairs={{0,8},{1,5},{2,10},{3,7},{4,0},{5,13},{6,2},{7,15},{8,16},{9,1},{1... | collective-permute-start | bytes 786440 | tf_op jit(solution)/shard_map/ppermute | solution.py:169
  51.3 3.0 %collective-permute-done.5.block_ref = bf16[512,256]{1,0:T(8,128)(2,1)S(1)} collective-permute-done((bf16[512,256]{1,0:T(8,128)(2,1)S(1)}, bf16[512,256]{1,0:T(8,128)(2,1)S(1)}, u32[]{:S(2)}, u32[]{:S(2)}) %collective-permute-start.5) | collective-permute-done | bytes 262176 | tf_op jit(solution)/shard_map/ppermute | solution.py:169
  54.3 1.8 %collective-permute-start.6 = (bf16[512,256]{1,0:T(8,128)(2,1)S(1)}, bf16[512,256]{1,0:T(8,128)(2,1)S(1)}, u32[]{:S(2)}, u32[]{:S(2)}) collective-permute-start(bf16[512,256]{1,0:T(8,128)(2,1)S(1)} %collective-permute-done.5.block_ref), channel_id=1, source_target_pairs={{0,8},{1,5},{2,10},{3,7},{4,0},{5,13},{6,2},{7,15},{8,16},{9,1},{1... | collective-permute-start | bytes 786440 | tf_op jit(solution)/shard_map/ppermute | solution.py:169
  56.1 1.0 collective-permute-done.14.block_ref
  57.1 1.8 %collective-permute-start.15 = (bf16[512,256]{1,0:T(8,128)(2,1)S(1)}, bf16[512,256]{1,0:T(8,128)(2,1)S(1)}, u32[]{:S(2)}, u32[]{:S(2)}) collective-permute-start(bf16[512,256]{1,0:T(8,128)(2,1)S(1)} %collective-permute-done.14.block_ref), channel_id=1, source_target_pairs={{0,8},{1,5},{2,10},{3,7},{4,0},{5,13},{6,2},{7,15},{8,16},{9,1},{1... | collective-permute-start | bytes 786440 | tf_op jit(solution)/shard_map/ppermute | solution.py:169
  58.9 1.7 %collective-permute-done.6.block_ref = bf16[512,256]{1,0:T(8,128)(2,1)S(1)} collective-permute-done((bf16[512,256]{1,0:T(8,128)(2,1)S(1)}, bf16[512,256]{1,0:T(8,128)(2,1)S(1)}, u32[]{:S(2)}, u32[]{:S(2)}) %collective-permute-start.6) | collective-permute-done | bytes 262176 | tf_op jit(solution)/shard_map/ppermute | solution.py:169
  60.6 1.8 %collective-permute-start.7 = (bf16[512,256]{1,0:T(8,128)(2,1)S(1)}, bf16[512,256]{1,0:T(8,128)(2,1)S(1)}, u32[]{:S(2)}, u32[]{:S(2)}) collective-permute-start(bf16[512,256]{1,0:T(8,128)(2,1)S(1)} %collective-permute-done.6.block_ref), channel_id=1, source_target_pairs={{0,8},{1,5},{2,10},{3,7},{4,0},{5,13},{6,2},{7,15},{8,16},{9,1},{1... | collective-permute-start | bytes 786440 | tf_op jit(solution)/shard_map/ppermute | solution.py:169
  62.5 1.0 collective-permute-done.15.block_ref
  63.5 1.8 %collective-permute-start.16 = (bf16[512,256]{1,0:T(8,128)(2,1)S(1)}, bf16[512,256]{1,0:T(8,128)(2,1)S(1)}, u32[]{:S(2)}, u32[]{:S(2)}) collective-permute-start(bf16[512,256]{1,0:T(8,128)(2,1)S(1)} %collective-permute-done.15.block_ref), channel_id=1, source_target_pairs={{0,8},{1,5},{2,10},{3,7},{4,0},{5,13},{6,2},{7,15},{8,16},{9,1},{1... | collective-permute-start | bytes 786440 | tf_op jit(solution)/shard_map/ppermute | solution.py:169
  65.3 1.7 %collective-permute-done.7.block_ref = bf16[512,256]{1,0:T(8,128)(2,1)S(1)} collective-permute-done((bf16[512,256]{1,0:T(8,128)(2,1)S(1)}, bf16[512,256]{1,0:T(8,128)(2,1)S(1)}, u32[]{:S(2)}, u32[]{:S(2)}) %collective-permute-start.7) | collective-permute-done | bytes 262176 | tf_op jit(solution)/shard_map/ppermute | solution.py:169
  67.0 1.8 %collective-permute-start.8 = (bf16[512,256]{1,0:T(8,128)(2,1)S(1)}, bf16[512,256]{1,0:T(8,128)(2,1)S(1)}, u32[]{:S(2)}, u32[]{:S(2)}) collective-permute-start(bf16[512,256]{1,0:T(8,128)(2,1)S(1)} %collective-permute-done.7.block_ref), channel_id=1, source_target_pairs={{0,8},{1,5},{2,10},{3,7},{4,0},{5,13},{6,2},{7,15},{8,16},{9,1},{1... | collective-permute-start | bytes 786440 | tf_op jit(solution)/shard_map/ppermute | solution.py:169
  68.8 1.0 collective-permute-done.16.block_ref
  69.8 1.8 %collective-permute-start.17 = (bf16[512,256]{1,0:T(8,128)(2,1)S(1)}, bf16[512,256]{1,0:T(8,128)(2,1)S(1)}, u32[]{:S(2)}, u32[]{:S(2)}) collective-permute-start(bf16[512,256]{1,0:T(8,128)(2,1)S(1)} %collective-permute-done.16.block_ref), channel_id=1, source_target_pairs={{0,8},{1,5},{2,10},{3,7},{4,0},{5,13},{6,2},{7,15},{8,16},{9,1},{1... | collective-permute-start | bytes 786440 | tf_op jit(solution)/shard_map/ppermute | solution.py:169
  71.7 1.7 %collective-permute-done.8.block_ref = bf16[512,256]{1,0:T(8,128)(2,1)S(1)} collective-permute-done((bf16[512,256]{1,0:T(8,128)(2,1)S(1)}, bf16[512,256]{1,0:T(8,128)(2,1)S(1)}, u32[]{:S(2)}, u32[]{:S(2)}) %collective-permute-start.8) | collective-permute-done | bytes 262176 | tf_op jit(solution)/shard_map/ppermute | solution.py:169
  73.4 1.8 %collective-permute-start.9 = (bf16[512,256]{1,0:T(8,128)(2,1)S(1)}, bf16[512,256]{1,0:T(8,128)(2,1)S(1)}, u32[]{:S(2)}, u32[]{:S(2)}) collective-permute-start(bf16[512,256]{1,0:T(8,128)(2,1)S(1)} %collective-permute-done.8.block_ref), channel_id=1, source_target_pairs={{0,8},{1,5},{2,10},{3,7},{4,0},{5,13},{6,2},{7,15},{8,16},{9,1},{1... | collective-permute-start | bytes 786440 | tf_op jit(solution)/shard_map/ppermute | solution.py:169
  75.2 1.0 collective-permute-done.17.block_ref
  76.2 1.8 %collective-permute-start.18 = (bf16[512,256]{1,0:T(8,128)(2,1)S(1)}, bf16[512,256]{1,0:T(8,128)(2,1)S(1)}, u32[]{:S(2)}, u32[]{:S(2)}) collective-permute-start(bf16[512,256]{1,0:T(8,128)(2,1)S(1)} %collective-permute-done.17.block_ref), channel_id=1, source_target_pairs={{0,8},{1,5},{2,10},{3,7},{4,0},{5,13},{6,2},{7,15},{8,16},{9,1},{1... | collective-permute-start | bytes 786440 | tf_op jit(solution)/shard_map/ppermute | solution.py:169
  78.0 1.7 %collective-permute-done.9.block_ref = bf16[512,256]{1,0:T(8,128)(2,1)S(1)} collective-permute-done((bf16[512,256]{1,0:T(8,128)(2,1)S(1)}, bf16[512,256]{1,0:T(8,128)(2,1)S(1)}, u32[]{:S(2)}, u32[]{:S(2)}) %collective-permute-start.9) | collective-permute-done | bytes 262176 | tf_op jit(solution)/shard_map/ppermute | solution.py:169
  79.8 1.8 %collective-permute-start.10 = (bf16[512,256]{1,0:T(8,128)(2,1)S(1)}, bf16[512,256]{1,0:T(8,128)(2,1)S(1)}, u32[]{:S(2)}, u32[]{:S(2)}) collective-permute-start(bf16[512,256]{1,0:T(8,128)(2,1)S(1)} %collective-permute-done.9.block_ref), channel_id=1, source_target_pairs={{0,8},{1,5},{2,10},{3,7},{4,0},{5,13},{6,2},{7,15},{8,16},{9,1},{1... | collective-permute-start | bytes 786440 | tf_op jit(solution)/shard_map/ppermute | solution.py:169
  81.6 1.0 collective-permute-done.18.block_ref
  82.6 1.8 %collective-permute-start.19 = (bf16[512,256]{1,0:T(8,128)(2,1)S(1)}, bf16[512,256]{1,0:T(8,128)(2,1)}, u32[]{:S(2)}, u32[]{:S(2)}) collective-permute-start(bf16[512,256]{1,0:T(8,128)(2,1)S(1)} %collective-permute-done.18.block_ref), channel_id=1, source_target_pairs={{0,8},{1,5},{2,10},{3,7},{4,0},{5,13},{6,2},{7,15},{8,16},{9,1},{1... | collective-permute-start | bytes 786440 | tf_op jit(solution)/shard_map/ppermute | solution.py:169
  84.4 1.7 %collective-permute-done.10.block_ref = bf16[512,256]{1,0:T(8,128)(2,1)S(1)} collective-permute-done((bf16[512,256]{1,0:T(8,128)(2,1)S(1)}, bf16[512,256]{1,0:T(8,128)(2,1)S(1)}, u32[]{:S(2)}, u32[]{:S(2)}) %collective-permute-start.10) | collective-permute-done | bytes 262176 | tf_op jit(solution)/shard_map/ppermute | solution.py:169
  86.1 1.8 %collective-permute-start.11 = (bf16[512,256]{1,0:T(8,128)(2,1)S(1)}, bf16[512,256]{1,0:T(8,128)(2,1)S(1)}, u32[]{:S(2)}, u32[]{:S(2)}) collective-permute-start(bf16[512,256]{1,0:T(8,128)(2,1)S(1)} %collective-permute-done.10.block_ref), channel_id=1, source_target_pairs={{0,8},{1,5},{2,10},{3,7},{4,0},{5,13},{6,2},{7,15},{8,16},{9,1},{1... | collective-permute-start | bytes 786440 | tf_op jit(solution)/shard_map/ppermute | solution.py:169
  88.0 0.7 fusion.38
  88.8 0.7 fusion.39
  89.5 2.8 %apply_block.16 = (bf16[8,1024,256]{2,1,0:T(8,128)(2,1)}, f32[8,1024,256]{2,1,0:T(8,128)}) custom-call(s32[1]{0:T(128)} %get-tuple-element.68.index_ref, bf16[512,256]{1,0:T(8,128)(2,1)} %copy-done.15, bf16[8,1024,256]{2,1,0:T(8,128)(2,1)} %weights_ref.31, f32[8,1024,256]{2,1,0:T(8,128)} %moment_ref.31), custom_call_target="tpu_custom_call" | custom-call | flops 786432 | bytes 1835008 | tf_op jit(solution)/shard_map/apply_block/pallas_call | solution.py:67
  92.4 2.8 %apply_block.17 = (bf16[8,1024,256]{2,1,0:T(8,128)(2,1)}, f32[8,1024,256]{2,1,0:T(8,128)}) custom-call(s32[1]{0:T(128)} %get-tuple-element.68.index_ref, bf16[512,256]{1,0:T(8,128)(2,1)} %copy-done.14, bf16[8,1024,256]{2,1,0:T(8,128)(2,1)} %weights_ref.31, f32[8,1024,256]{2,1,0:T(8,128)} %moment_ref.31, ...), custom_call_target="tpu_custom_call", output_to_operand_aliasing={{0}: (4, {}), {1}: (5, {})} | custom-call | flops 786432 | bytes 1835008 | tf_op jit(solution)/shard_map/apply_block/pallas_call | solution.py:67
  95.2 2.7 %apply_block.18 = (bf16[8,1024,256]{2,1,0:T(8,128)(2,1)}, f32[8,1024,256]{2,1,0:T(8,128)}) custom-call(s32[1]{0:T(128)} %get-tuple-element.69.index_ref, bf16[512,256]{1,0:T(8,128)(2,1)} %copy-done.3, bf16[8,1024,256]{2,1,0:T(8,128)(2,1)} %weights_ref.31, f32[8,1024,256]{2,1,0:T(8,128)} %moment_ref.31, ...), custom_call_target="tpu_custom_call", output_to_operand_aliasing={{0}: (4, {}), {1}: (5, {})} | custom-call | flops 786432 | bytes 1835008 | tf_op jit(solution)/shard_map/apply_block/pallas_call | solution.py:67
  97.9 2.7 %apply_block.19 = (bf16[8,1024,256]{2,1,0:T(8,128)(2,1)}, f32[8,1024,256]{2,1,0:T(8,128)}) custom-call(s32[1]{0:T(128)} %get-tuple-element.69.index_ref, bf16[512,256]{1,0:T(8,128)(2,1)} %copy-done.12, bf16[8,1024,256]{2,1,0:T(8,128)(2,1)} %weights_ref.31, f32[8,1024,256]{2,1,0:T(8,128)} %moment_ref.31, ...), custom_call_target="tpu_custom_call", output_to_operand_aliasing={{0}: (4, {}), {1}: (5, {})} | custom-call | flops 786432 | bytes 1835008 | tf_op jit(solution)/shard_map/apply_block/pallas_call | solution.py:67
  100.6 2.7 %apply_block.20 = (bf16[8,1024,256]{2,1,0:T(8,128)(2,1)}, f32[8,1024,256]{2,1,0:T(8,128)}) custom-call(s32[1]{0:T(128)} %get-tuple-element.70.index_ref, bf16[512,256]{1,0:T(8,128)(2,1)} %copy-done.10, bf16[8,1024,256]{2,1,0:T(8,128)(2,1)} %weights_ref.31, f32[8,1024,256]{2,1,0:T(8,128)} %moment_ref.31, ...), custom_call_target="tpu_custom_call", output_to_operand_aliasing={{0}: (4, {}), {1}: (5, {})} | custom-call | flops 786432 | bytes 1835008 | tf_op jit(solution)/shard_map/apply_block/pallas_call | solution.py:67
  103.4 2.7 %apply_block.21 = (bf16[8,1024,256]{2,1,0:T(8,128)(2,1)}, f32[8,1024,256]{2,1,0:T(8,128)}) custom-call(s32[1]{0:T(128)} %get-tuple-element.70.index_ref, bf16[512,256]{1,0:T(8,128)(2,1)} %copy-done.11, bf16[8,1024,256]{2,1,0:T(8,128)(2,1)} %weights_ref.31, f32[8,1024,256]{2,1,0:T(8,128)} %moment_ref.31, ...), custom_call_target="tpu_custom_call", output_to_operand_aliasing={{0}: (4, {}), {1}: (5, {})} | custom-call | flops 786432 | bytes 1835008 | tf_op jit(solution)/shard_map/apply_block/pallas_call | solution.py:67
  106.1 2.7 %apply_block.22 = (bf16[8,1024,256]{2,1,0:T(8,128)(2,1)}, f32[8,1024,256]{2,1,0:T(8,128)}) custom-call(s32[1]{0:T(128)} %get-tuple-element.71.index_ref, bf16[512,256]{1,0:T(8,128)(2,1)} %copy-done.8, bf16[8,1024,256]{2,1,0:T(8,128)(2,1)} %weights_ref.31, f32[8,1024,256]{2,1,0:T(8,128)} %moment_ref.31, ...), custom_call_target="tpu_custom_call", output_to_operand_aliasing={{0}: (4, {}), {1}: (5, {})} | custom-call | flops 786432 | bytes 1835008 | tf_op jit(solution)/shard_map/apply_block/pallas_call | solution.py:67
  108.8 2.7 %apply_block.23 = (bf16[8,1024,256]{2,1,0:T(8,128)(2,1)}, f32[8,1024,256]{2,1,0:T(8,128)}) custom-call(s32[1]{0:T(128)} %get-tuple-element.71.index_ref, bf16[512,256]{1,0:T(8,128)(2,1)} %copy-done.9, bf16[8,1024,256]{2,1,0:T(8,128)(2,1)} %weights_ref.31, f32[8,1024,256]{2,1,0:T(8,128)} %moment_ref.31, ...), custom_call_target="tpu_custom_call", output_to_operand_aliasing={{0}: (4, {}), {1}: (5, {})} | custom-call | flops 786432 | bytes 1835008 | tf_op jit(solution)/shard_map/apply_block/pallas_call | solution.py:67
  111.5 2.7 %apply_block.24 = (bf16[8,1024,256]{2,1,0:T(8,128)(2,1)}, f32[8,1024,256]{2,1,0:T(8,128)}) custom-call(s32[1]{0:T(128)} %get-tuple-element.72.index_ref, bf16[512,256]{1,0:T(8,128)(2,1)} %copy-done.6, bf16[8,1024,256]{2,1,0:T(8,128)(2,1)} %weights_ref.31, f32[8,1024,256]{2,1,0:T(8,128)} %moment_ref.31, ...), custom_call_target="tpu_custom_call", output_to_operand_aliasing={{0}: (4, {}), {1}: (5, {})} | custom-call | flops 786432 | bytes 1835008 | tf_op jit(solution)/shard_map/apply_block/pallas_call | solution.py:67
  114.3 2.7 %apply_block.25 = (bf16[8,1024,256]{2,1,0:T(8,128)(2,1)}, f32[8,1024,256]{2,1,0:T(8,128)}) custom-call(s32[1]{0:T(128)} %get-tuple-element.72.index_ref, bf16[512,256]{1,0:T(8,128)(2,1)} %copy-done.7, bf16[8,1024,256]{2,1,0:T(8,128)(2,1)} %weights_ref.31, f32[8,1024,256]{2,1,0:T(8,128)} %moment_ref.31, ...), custom_call_target="tpu_custom_call", output_to_operand_aliasing={{0}: (4, {}), {1}: (5, {})} | custom-call | flops 786432 | bytes 1835008 | tf_op jit(solution)/shard_map/apply_block/pallas_call | solution.py:67
  117.0 2.7 %apply_block.26 = (bf16[8,1024,256]{2,1,0:T(8,128)(2,1)}, f32[8,1024,256]{2,1,0:T(8,128)}) custom-call(s32[1]{0:T(128)} %get-tuple-element.73.index_ref, bf16[512,256]{1,0:T(8,128)(2,1)} %copy-done.4, bf16[8,1024,256]{2,1,0:T(8,128)(2,1)} %weights_ref.31, f32[8,1024,256]{2,1,0:T(8,128)} %moment_ref.31, ...), custom_call_target="tpu_custom_call", output_to_operand_aliasing={{0}: (4, {}), {1}: (5, {})} | custom-call | flops 786432 | bytes 1835008 | tf_op jit(solution)/shard_map/apply_block/pallas_call | solution.py:67
  119.7 2.7 %apply_block.27 = (bf16[8,1024,256]{2,1,0:T(8,128)(2,1)}, f32[8,1024,256]{2,1,0:T(8,128)}) custom-call(s32[1]{0:T(128)} %get-tuple-element.73.index_ref, bf16[512,256]{1,0:T(8,128)(2,1)} %copy-done.5, bf16[8,1024,256]{2,1,0:T(8,128)(2,1)} %weights_ref.31, f32[8,1024,256]{2,1,0:T(8,128)} %moment_ref.31, ...), custom_call_target="tpu_custom_call", output_to_operand_aliasing={{0}: (4, {}), {1}: (5, {})} | custom-call | flops 786432 | bytes 1835008 | tf_op jit(solution)/shard_map/apply_block/pallas_call | solution.py:67
  122.3 2.8 %apply_block.28 = (bf16[8,1024,256]{2,1,0:T(8,128)(2,1)}, f32[8,1024,256]{2,1,0:T(8,128)}) custom-call(s32[1]{0:T(128)} %get-tuple-element.74.index_ref, bf16[512,256]{1,0:T(8,128)(2,1)} %copy-done.2, bf16[8,1024,256]{2,1,0:T(8,128)(2,1)} %weights_ref.31, f32[8,1024,256]{2,1,0:T(8,128)} %moment_ref.31, ...), custom_call_target="tpu_custom_call", output_to_operand_aliasing={{0}: (4, {}), {1}: (5, {})} | custom-call | flops 786432 | bytes 1835008 | tf_op jit(solution)/shard_map/apply_block/pallas_call | solution.py:67
  125.1 2.8 %apply_block.29 = (bf16[8,1024,256]{2,1,0:T(8,128)(2,1)}, f32[8,1024,256]{2,1,0:T(8,128)}) custom-call(s32[1]{0:T(128)} %get-tuple-element.74.index_ref, bf16[512,256]{1,0:T(8,128)(2,1)} %copy-done.1, bf16[8,1024,256]{2,1,0:T(8,128)(2,1)} %weights_ref.31, f32[8,1024,256]{2,1,0:T(8,128)} %moment_ref.31, ...), custom_call_target="tpu_custom_call", output_to_operand_aliasing={{0}: (4, {}), {1}: (5, {})} | custom-call | flops 786432 | bytes 1835008 | tf_op jit(solution)/shard_map/apply_block/pallas_call | solution.py:67
  127.9 2.7 %apply_block.30 = (bf16[8,1024,256]{2,1,0:T(8,128)(2,1)}, f32[8,1024,256]{2,1,0:T(8,128)}) custom-call(s32[1]{0:T(128)} %get-tuple-element.75.index_ref, bf16[512,256]{1,0:T(8,128)(2,1)} %collective-permute-done.19.block_ref, bf16[8,1024,256]{2,1,0:T(8,128)(2,1)} %weights_ref.31, ...), custom_call_target="tpu_custom_call", output_to_operand_aliasing={{0}: (4, {}), {1}: (5, {})} | custom-call | flops 786432 | bytes 1835008 | tf_op jit(solution)/shard_map/apply_block/pallas_call | solution.py:67
  130.6 0.7 copy-done.13
  131.3 2.7 %apply_block.31 = (bf16[8,1024,256]{2,1,0:T(8,128)(2,1)}, f32[8,1024,256]{2,1,0:T(8,128)}) custom-call(s32[1]{0:T(128)} %get-tuple-element.75.index_ref, bf16[512,256]{1,0:T(8,128)(2,1)} %copy-done.13, bf16[8,1024,256]{2,1,0:T(8,128)(2,1)} %weights_ref.31, f32[8,1024,256]{2,1,0:T(8,128)} %moment_ref.31, ...), custom_call_target="tpu_custom_call", output_to_operand_aliasing={{0}: (4, {}), {1}: (5, {})} | custom-call | flops 786432 | bytes 1835008 | tf_op jit(solution)/shard_map/apply_block/pallas_call | solution.py:67
  (51 shorter events, 2.1 us)
Async XLA Ops:
  3.9 3.9 %copy-start.17 = (s32[8,1]{0,1:T(1,128)S(1)}, s32[8,1]{0,1:T(1,128)}, u32[]{:S(2)}) copy-start(s32[8,1]{0,1:T(1,128)} %param.8) | copy-start | bytes 100
  7.3 7.9 %collective-permute-start = (bf16[256,2,1024]{2,0,1:T(8,128)(2,1)}, bf16[256,2,1024]{2,0,1:T(8,128)(2,1)S(1)}, u32[]{:S(2)}, u32[]{:S(2)}) collective-permute-start(bf16[256,2,1024]{2,0,1:T(8,128)(2,1)} %bitcast.4), channel_id=1, source_target_pairs={{0,1},{1,0},{2,3},{3,2},{4,5},{5,4},{6,7},{7,6},{8,9},{9,8},{10,11... | collective-permute-start | bytes 3145736 | tf_op jit(solution)/shard_map/ppermute | solution.py:107
  12.2 15.4 %collective-permute-start.1 = (bf16[1024,256]{1,0:T(8,128)(2,1)}, bf16[1024,256]{1,0:T(8,128)(2,1)}, u32[]{:S(2)}, u32[]{:S(2)}) collective-permute-start(bf16[1024,256]{1,0:T(8,128)(2,1)} %dynamic-slice_bitcast_fusion.2), channel_id=1, source_target_pairs={{0,2},{1,3},{2,0},{3,1},{4,6},{5,7},{6,4},{7,5},{8,10},{9,11},{10,... | collective-permute-start | bytes 1572872 | tf_op jit(solution)/shard_map/ppermute | solution.py:102
  15.2 1.0 copy-start
  16.2 14.5 %copy-start.16 = (bf16[1,256,256]{2,1,0:T(8,128)(2,1)S(1)}, bf16[1,256,256]{2,1,0:T(8,128)(2,1)}, u32[]{:S(2)}) copy-start(bf16[1,256,256]{2,1,0:T(8,128)(2,1)} %param.7) | copy-start | bytes 393220
  30.6 2.0 %collective-permute-start.2 = (f32[512,256]{0,1:T(8,128)S(1)}, f32[512,256]{0,1:T(8,128)S(1)}, u32[]{:S(2)}, u32[]{:S(2)}) collective-permute-start(f32[512,256]{0,1:T(8,128)S(1)} %fusion.4), channel_id=1, source_target_pairs={{0,1},{1,0},{2,3},{3,2},{4,5},{5,4},{6,7},{7,6},{8,9},{9,8},{10,11... | collective-permute-start | bytes 1572872 | tf_op jit(solution)/shard_map/ppermute | solution.py:128
  30.8 2.0 %collective-permute-start.3 = (bf16[256,256]{0,1:T(8,128)(2,1)S(1)}, bf16[256,256]{0,1:T(8,128)(2,1)S(1)}, u32[]{:S(2)}, u32[]{:S(2)}) collective-permute-start(bf16[256,256]{0,1:T(8,128)(2,1)S(1)} %bitcast.30), channel_id=1, source_target_pairs={{0,1},{1,0},{2,3},{3,2},{4,5},{5,4},{6,7},{7,6},{8,9},{9,8},{10,11... | collective-permute-start | bytes 393224 | tf_op jit(solution)/shard_map/ppermute | solution.py:112
  33.4 9.2 %collective-permute-start.12 = (bf16[512,256]{1,0:T(8,128)(2,1)S(1)}, bf16[512,256]{1,0:T(8,128)(2,1)S(1)}, u32[]{:S(2)}, u32[]{:S(2)}) collective-permute-start(bf16[512,256]{1,0:T(8,128)(2,1)S(1)} %convolution_convert_fusion), channel_id=1, source_target_pairs={{0,2},{1,3},{2,0},{3,1},{4,6},{5,7},{6,4},{7,5},{8,10},{9,11},{10,... | collective-permute-start | bytes 786440 | tf_op jit(solution)/shard_map/ppermute | solution.py:147
  35.6 11.9 %collective-permute-start.4 = (bf16[512,256]{1,0:T(8,128)(2,1)S(1)}, bf16[512,256]{1,0:T(8,128)(2,1)S(1)}, u32[]{:S(2)}, u32[]{:S(2)}) collective-permute-start(bf16[512,256]{1,0:T(8,128)(2,1)S(1)} %convolution_convert_fusion.1), channel_id=1, source_target_pairs={{0,2},{1,3},{2,0},{3,1},{4,6},{5,7},{6,4},{7,5},{8,10},{9,11},{10,... | collective-permute-start | bytes 786440 | tf_op jit(solution)/shard_map/ppermute | solution.py:147
  43.0 25.8 %copy-start.15 = (bf16[512,256]{1,0:T(8,128)(2,1)}, bf16[512,256]{1,0:T(8,128)(2,1)S(1)}, u32[]{:S(2)}) copy-start(bf16[512,256]{1,0:T(8,128)(2,1)S(1)} %fusion.21.block_ref) | copy-start | bytes 786436
  43.0 6.7 %collective-permute-start.13 = (bf16[512,256]{1,0:T(8,128)(2,1)S(1)}, bf16[512,256]{1,0:T(8,128)(2,1)S(1)}, u32[]{:S(2)}, u32[]{:S(2)}) collective-permute-start(bf16[512,256]{1,0:T(8,128)(2,1)S(1)} %fusion.21.block_ref), channel_id=1, source_target_pairs={{0,8},{1,5},{2,10},{3,7},{4,0},{5,13},{6,2},{7,15},{8,16},{9,1},{1... | collective-permute-start | bytes 786440 | tf_op jit(solution)/shard_map/ppermute | solution.py:169
  47.8 3.5 %copy-start.14 = (bf16[512,256]{1,0:T(8,128)(2,1)}, bf16[512,256]{1,0:T(8,128)(2,1)S(1)}, u32[]{:S(2)}) copy-start(bf16[512,256]{1,0:T(8,128)(2,1)S(1)} %fusion.33.block_ref) | copy-start | bytes 786436
  47.8 6.4 %collective-permute-start.5 = (bf16[512,256]{1,0:T(8,128)(2,1)S(1)}, bf16[512,256]{1,0:T(8,128)(2,1)S(1)}, u32[]{:S(2)}, u32[]{:S(2)}) collective-permute-start(bf16[512,256]{1,0:T(8,128)(2,1)S(1)} %fusion.33.block_ref), channel_id=1, source_target_pairs={{0,8},{1,5},{2,10},{3,7},{4,0},{5,13},{6,2},{7,15},{8,16},{9,1},{1... | collective-permute-start | bytes 786440 | tf_op jit(solution)/shard_map/ppermute | solution.py:169
  49.7 42.6 %copy-start.3 = (bf16[512,256]{1,0:T(8,128)(2,1)}, bf16[512,256]{1,0:T(8,128)(2,1)S(1)}, u32[]{:S(2)}) copy-start(bf16[512,256]{1,0:T(8,128)(2,1)S(1)} %collective-permute-done.13.block_ref) | copy-start | bytes 786436
  49.7 7.4 %collective-permute-start.14 = (bf16[512,256]{1,0:T(8,128)(2,1)S(1)}, bf16[512,256]{1,0:T(8,128)(2,1)S(1)}, u32[]{:S(2)}, u32[]{:S(2)}) collective-permute-start(bf16[512,256]{1,0:T(8,128)(2,1)S(1)} %collective-permute-done.13.block_ref), channel_id=1, source_target_pairs={{0,8},{1,5},{2,10},{3,7},{4,0},{5,13},{6,2},{7,15},{8,16},{9,1},{1... | collective-permute-start | bytes 786440 | tf_op jit(solution)/shard_map/ppermute | solution.py:169
  54.3 38.0 %copy-start.12 = (bf16[512,256]{1,0:T(8,128)(2,1)}, bf16[512,256]{1,0:T(8,128)(2,1)S(1)}, u32[]{:S(2)}) copy-start(bf16[512,256]{1,0:T(8,128)(2,1)S(1)} %collective-permute-done.5.block_ref) | copy-start | bytes 786436
  54.3 6.4 %collective-permute-start.6 = (bf16[512,256]{1,0:T(8,128)(2,1)S(1)}, bf16[512,256]{1,0:T(8,128)(2,1)S(1)}, u32[]{:S(2)}, u32[]{:S(2)}) collective-permute-start(bf16[512,256]{1,0:T(8,128)(2,1)S(1)} %collective-permute-done.5.block_ref), channel_id=1, source_target_pairs={{0,8},{1,5},{2,10},{3,7},{4,0},{5,13},{6,2},{7,15},{8,16},{9,1},{1... | collective-permute-start | bytes 786440 | tf_op jit(solution)/shard_map/ppermute | solution.py:169
  57.1 35.2 %copy-start.10 = (bf16[512,256]{1,0:T(8,128)(2,1)}, bf16[512,256]{1,0:T(8,128)(2,1)S(1)}, u32[]{:S(2)}) copy-start(bf16[512,256]{1,0:T(8,128)(2,1)S(1)} %collective-permute-done.14.block_ref) | copy-start | bytes 786436
  57.1 6.4 %collective-permute-start.15 = (bf16[512,256]{1,0:T(8,128)(2,1)S(1)}, bf16[512,256]{1,0:T(8,128)(2,1)S(1)}, u32[]{:S(2)}, u32[]{:S(2)}) collective-permute-start(bf16[512,256]{1,0:T(8,128)(2,1)S(1)} %collective-permute-done.14.block_ref), channel_id=1, source_target_pairs={{0,8},{1,5},{2,10},{3,7},{4,0},{5,13},{6,2},{7,15},{8,16},{9,1},{1... | collective-permute-start | bytes 786440 | tf_op jit(solution)/shard_map/ppermute | solution.py:169
  60.6 31.7 %copy-start.11 = (bf16[512,256]{1,0:T(8,128)(2,1)}, bf16[512,256]{1,0:T(8,128)(2,1)S(1)}, u32[]{:S(2)}) copy-start(bf16[512,256]{1,0:T(8,128)(2,1)S(1)} %collective-permute-done.6.block_ref) | copy-start | bytes 786436
  60.6 6.4 %collective-permute-start.7 = (bf16[512,256]{1,0:T(8,128)(2,1)S(1)}, bf16[512,256]{1,0:T(8,128)(2,1)S(1)}, u32[]{:S(2)}, u32[]{:S(2)}) collective-permute-start(bf16[512,256]{1,0:T(8,128)(2,1)S(1)} %collective-permute-done.6.block_ref), channel_id=1, source_target_pairs={{0,8},{1,5},{2,10},{3,7},{4,0},{5,13},{6,2},{7,15},{8,16},{9,1},{1... | collective-permute-start | bytes 786440 | tf_op jit(solution)/shard_map/ppermute | solution.py:169
  63.5 28.9 %copy-start.8 = (bf16[512,256]{1,0:T(8,128)(2,1)}, bf16[512,256]{1,0:T(8,128)(2,1)S(1)}, u32[]{:S(2)}) copy-start(bf16[512,256]{1,0:T(8,128)(2,1)S(1)} %collective-permute-done.15.block_ref) | copy-start | bytes 786436
  63.5 6.4 %collective-permute-start.16 = (bf16[512,256]{1,0:T(8,128)(2,1)S(1)}, bf16[512,256]{1,0:T(8,128)(2,1)S(1)}, u32[]{:S(2)}, u32[]{:S(2)}) collective-permute-start(bf16[512,256]{1,0:T(8,128)(2,1)S(1)} %collective-permute-done.15.block_ref), channel_id=1, source_target_pairs={{0,8},{1,5},{2,10},{3,7},{4,0},{5,13},{6,2},{7,15},{8,16},{9,1},{1... | collective-permute-start | bytes 786440 | tf_op jit(solution)/shard_map/ppermute | solution.py:169
  67.0 25.3 %copy-start.9 = (bf16[512,256]{1,0:T(8,128)(2,1)}, bf16[512,256]{1,0:T(8,128)(2,1)S(1)}, u32[]{:S(2)}) copy-start(bf16[512,256]{1,0:T(8,128)(2,1)S(1)} %collective-permute-done.7.block_ref) | copy-start | bytes 786436
  67.0 6.4 %collective-permute-start.8 = (bf16[512,256]{1,0:T(8,128)(2,1)S(1)}, bf16[512,256]{1,0:T(8,128)(2,1)S(1)}, u32[]{:S(2)}, u32[]{:S(2)}) collective-permute-start(bf16[512,256]{1,0:T(8,128)(2,1)S(1)} %collective-permute-done.7.block_ref), channel_id=1, source_target_pairs={{0,8},{1,5},{2,10},{3,7},{4,0},{5,13},{6,2},{7,15},{8,16},{9,1},{1... | collective-permute-start | bytes 786440 | tf_op jit(solution)/shard_map/ppermute | solution.py:169
  69.8 22.5 %copy-start.6 = (bf16[512,256]{1,0:T(8,128)(2,1)}, bf16[512,256]{1,0:T(8,128)(2,1)S(1)}, u32[]{:S(2)}) copy-start(bf16[512,256]{1,0:T(8,128)(2,1)S(1)} %collective-permute-done.16.block_ref) | copy-start | bytes 786436
  69.8 6.4 %collective-permute-start.17 = (bf16[512,256]{1,0:T(8,128)(2,1)S(1)}, bf16[512,256]{1,0:T(8,128)(2,1)S(1)}, u32[]{:S(2)}, u32[]{:S(2)}) collective-permute-start(bf16[512,256]{1,0:T(8,128)(2,1)S(1)} %collective-permute-done.16.block_ref), channel_id=1, source_target_pairs={{0,8},{1,5},{2,10},{3,7},{4,0},{5,13},{6,2},{7,15},{8,16},{9,1},{1... | collective-permute-start | bytes 786440 | tf_op jit(solution)/shard_map/ppermute | solution.py:169
  73.4 19.0 %copy-start.7 = (bf16[512,256]{1,0:T(8,128)(2,1)}, bf16[512,256]{1,0:T(8,128)(2,1)S(1)}, u32[]{:S(2)}) copy-start(bf16[512,256]{1,0:T(8,128)(2,1)S(1)} %collective-permute-done.8.block_ref) | copy-start | bytes 786436
  73.4 6.4 %collective-permute-start.9 = (bf16[512,256]{1,0:T(8,128)(2,1)S(1)}, bf16[512,256]{1,0:T(8,128)(2,1)S(1)}, u32[]{:S(2)}, u32[]{:S(2)}) collective-permute-start(bf16[512,256]{1,0:T(8,128)(2,1)S(1)} %collective-permute-done.8.block_ref), channel_id=1, source_target_pairs={{0,8},{1,5},{2,10},{3,7},{4,0},{5,13},{6,2},{7,15},{8,16},{9,1},{1... | collective-permute-start | bytes 786440 | tf_op jit(solution)/shard_map/ppermute | solution.py:169
  76.2 16.2 %copy-start.4 = (bf16[512,256]{1,0:T(8,128)(2,1)}, bf16[512,256]{1,0:T(8,128)(2,1)S(1)}, u32[]{:S(2)}) copy-start(bf16[512,256]{1,0:T(8,128)(2,1)S(1)} %collective-permute-done.17.block_ref) | copy-start | bytes 786436
  76.2 6.4 %collective-permute-start.18 = (bf16[512,256]{1,0:T(8,128)(2,1)S(1)}, bf16[512,256]{1,0:T(8,128)(2,1)S(1)}, u32[]{:S(2)}, u32[]{:S(2)}) collective-permute-start(bf16[512,256]{1,0:T(8,128)(2,1)S(1)} %collective-permute-done.17.block_ref), channel_id=1, source_target_pairs={{0,8},{1,5},{2,10},{3,7},{4,0},{5,13},{6,2},{7,15},{8,16},{9,1},{1... | collective-permute-start | bytes 786440 | tf_op jit(solution)/shard_map/ppermute | solution.py:169
  79.8 12.6 %copy-start.5 = (bf16[512,256]{1,0:T(8,128)(2,1)}, bf16[512,256]{1,0:T(8,128)(2,1)S(1)}, u32[]{:S(2)}) copy-start(bf16[512,256]{1,0:T(8,128)(2,1)S(1)} %collective-permute-done.9.block_ref) | copy-start | bytes 786436
  79.8 6.4 %collective-permute-start.10 = (bf16[512,256]{1,0:T(8,128)(2,1)S(1)}, bf16[512,256]{1,0:T(8,128)(2,1)S(1)}, u32[]{:S(2)}, u32[]{:S(2)}) collective-permute-start(bf16[512,256]{1,0:T(8,128)(2,1)S(1)} %collective-permute-done.9.block_ref), channel_id=1, source_target_pairs={{0,8},{1,5},{2,10},{3,7},{4,0},{5,13},{6,2},{7,15},{8,16},{9,1},{1... | collective-permute-start | bytes 786440 | tf_op jit(solution)/shard_map/ppermute | solution.py:169
  82.6 9.8 %copy-start.2 = (bf16[512,256]{1,0:T(8,128)(2,1)}, bf16[512,256]{1,0:T(8,128)(2,1)S(1)}, u32[]{:S(2)}) copy-start(bf16[512,256]{1,0:T(8,128)(2,1)S(1)} %collective-permute-done.18.block_ref) | copy-start | bytes 786436
  82.6 45.3 %collective-permute-start.19 = (bf16[512,256]{1,0:T(8,128)(2,1)S(1)}, bf16[512,256]{1,0:T(8,128)(2,1)}, u32[]{:S(2)}, u32[]{:S(2)}) collective-permute-start(bf16[512,256]{1,0:T(8,128)(2,1)S(1)} %collective-permute-done.18.block_ref), channel_id=1, source_target_pairs={{0,8},{1,5},{2,10},{3,7},{4,0},{5,13},{6,2},{7,15},{8,16},{9,1},{1... | collective-permute-start | bytes 786440 | tf_op jit(solution)/shard_map/ppermute | solution.py:169
  86.1 6.3 %copy-start.1 = (bf16[512,256]{1,0:T(8,128)(2,1)}, bf16[512,256]{1,0:T(8,128)(2,1)S(1)}, u32[]{:S(2)}) copy-start(bf16[512,256]{1,0:T(8,128)(2,1)S(1)} %collective-permute-done.10.block_ref) | copy-start | bytes 786436
  86.1 44.4 %collective-permute-start.11 = (bf16[512,256]{1,0:T(8,128)(2,1)S(1)}, bf16[512,256]{1,0:T(8,128)(2,1)S(1)}, u32[]{:S(2)}, u32[]{:S(2)}) collective-permute-start(bf16[512,256]{1,0:T(8,128)(2,1)S(1)} %collective-permute-done.10.block_ref), channel_id=1, source_target_pairs={{0,8},{1,5},{2,10},{3,7},{4,0},{5,13},{6,2},{7,15},{8,16},{9,1},{1... | collective-permute-start | bytes 786440 | tf_op jit(solution)/shard_map/ppermute | solution.py:169
  130.6 0.7 copy-start.13

commit v2 on v0

v2 whole, which is shorter than its diff:
```python
import functools
import math

import jax
import jax.numpy as jnp
import numpy as np
from jax import lax
from jax.experimental import pallas as pl
from jax.experimental.pallas import tpu as pltpu
from jax.sharding import PartitionSpec as P

CHAINS = 2
MIB = 1 << 20
VMEM = pl.BlockSpec(memory_space=pltpu.VMEM)
SMEM = pl.BlockSpec(memory_space=pltpu.SMEM)
ANY = pl.BlockSpec(memory_space=pl.ANY)


def outer_update(weights, moment, average):
    new_moment = 0.9 * moment + average
    new_weights = (weights.astype(jnp.float32) - 0.7 * (average + 0.9 * new_moment)).astype(
        jnp.bfloat16
    )
    return (new_weights, new_moment)


def ring_order(paths):
    return [p for p in range(0, paths, 2)] + [p for p in range(paths - 1, 0, -2)]


def ring_plan(paths, shards):
    order = ring_order(paths)
    place = {p: i for i, p in enumerate(order)}
    pairs = []
    source = np.zeros((paths, 2, paths), np.int32)
    for p in range(paths):
        for f in range(shards):
            way = 1 if f % 2 == 0 else -1
            pairs.append((p * shards + f, order[(place[p] + way) % paths] * shards + f))
        for core in range(2):
            way = 1 if core == 0 else -1
            for step in range(paths):
                source[p, core, step] = order[(place[p] - way * step) % paths]
    return pairs, source


def call(kernel, out_shape, in_specs, out_specs, args, scratch=(), limit=8, cost=None):
    return pl.pallas_call(
        kernel,
        in_specs=in_specs,
        out_specs=out_specs,
        out_shape=out_shape,
        scratch_shapes=list(scratch),
        compiler_params=pltpu.CompilerParams(vmem_limit_bytes=limit * MIB),
        cost_estimate=cost,
        name=kernel.func.__name__ if isinstance(kernel, functools.partial) else kernel.__name__,
    )(*args)


def pick_rows(table_ref, where_ref, weights_ref, out_ref, sem):
    copy = pltpu.make_async_copy(weights_ref.at[table_ref[where_ref[0]]], out_ref, sem)
    copy.start()
    copy.wait()


def pick_columns(where_ref, tokens_ref, after_ref, out_ref, sem):
    rows = after_ref.shape[0]
    other = 1 - where_ref[1]
    copies = []
    for block in range(out_ref.shape[1] // rows):
        start = pl.multiple_of((2 * block + other) * rows, 128)
        copies.append(
            pltpu.make_async_copy(
                tokens_ref.at[0, :, pl.ds(start, rows)],
                out_ref.at[:, pl.ds(block * rows, rows)],
                sem.at[block],
            )
        )
    for copy in copies:
        copy.start()
    for copy in copies:
        copy.wait()


def products(where_ref, tokens_ref, taken_ref, weights_ref, block):
    rows = weights_ref.shape[0]
    own = pl.multiple_of((2 * block + where_ref[1]) * rows, 128)
    lent = pl.multiple_of(block * rows, 128)
    weights = weights_ref[...]
    return (
        jnp.dot(tokens_ref[0, :, pl.ds(own, rows)], weights, preferred_element_type=jnp.float32),
        jnp.dot(taken_ref[:, pl.ds(lent, rows)], weights, preferred_element_type=jnp.float32),
    )


def first_products(where_ref, tokens_ref, taken_ref, weights_ref, out_ref, turned_ref):
    rows, tok = weights_ref.shape[0], taken_ref.shape[0]
    a, b = products(where_ref, tokens_ref, taken_ref, weights_ref, where_ref[2])
    out_ref[:tok] = a
    out_ref[tok:] = b
    for block in range(turned_ref.shape[0] // rows):
        own = pl.multiple_of((2 * block + where_ref[1]) * rows, 128)
        spot = pl.ds(block * rows, rows)
        turned_ref[spot, :tok] = tokens_ref[0, :, pl.ds(own, rows)].T
        turned_ref[spot, tok:] = taken_ref[:, spot].T


def next_products(step, where_ref, tokens_ref, taken_ref, weights_ref, sum_ref, out_ref):
    tok = taken_ref.shape[0]
    chips = taken_ref.shape[1] // weights_ref.shape[0]
    block = lax.rem(where_ref[2] + chips - step, chips)
    a, b = products(where_ref, tokens_ref, taken_ref, weights_ref, block)
    out_ref[:tok] = sum_ref[:tok] + a
    out_ref[tok:] = sum_ref[tok:] + b


def cotangent_of(latent, upstream):
    inverse_rms = lax.rsqrt(jnp.mean(latent * latent, axis=-1, keepdims=True) + 1e-06)
    normed = latent * inverse_rms
    return (
        inverse_rms * (upstream - normed * jnp.mean(upstream * normed, axis=-1, keepdims=True))
    ).astype(jnp.bfloat16)


def sent_gradients(where_ref, mine_ref, other_ref, up_ref, other_up_ref, turned_ref, *outs):
    latent_ref, outs = outs[0], outs[1:]
    tok = up_ref.shape[0]
    latent_ref[:tok] = cotangent_of(
        mine_ref[:tok] + other_ref[tok:], up_ref[...].astype(jnp.float32)
    )
    latent_ref[tok:] = cotangent_of(
        mine_ref[tok:] + other_ref[:tok], other_up_ref[...].astype(jnp.float32)
    )
    part = outs[0].shape[0] if outs else 0
    chips = len(outs) // CHAINS + 1
    for i, out_ref in enumerate(outs):
        block = lax.rem(where_ref[2] + 1 + i // CHAINS, chips)
        start = pl.multiple_of(block * part * CHAINS + (i % CHAINS) * part, 16)
        out_ref[...] = jnp.dot(
            turned_ref[pl.ds(start, part), :], latent_ref[...], preferred_element_type=jnp.float32
        ).astype(out_ref.dtype)


def kept_gradients(where_ref, turned_ref, latent_ref, *outs):
    part = outs[0].shape[0]
    for i, out_ref in enumerate(outs):
        start = pl.multiple_of(where_ref[2] * part * CHAINS + i * part, 16)
        out_ref[...] = jnp.dot(
            turned_ref[pl.ds(start, part), :], latent_ref[...], preferred_element_type=jnp.float32
        )


def apply_blocks(steps, table_ref, source_ref, where_ref, weights_ref, moment_ref, *refs):
    count = len(steps)
    blocks, rest = refs[:count], refs[count:]
    out_weights, out_moment, new_weights, new_moment, sems = rest
    paths = table_ref.shape[0]
    tile = 64
    copies = []
    for i, (step, start) in enumerate(steps):
        module = table_ref[source_ref[(where_ref[0] * 2 + where_ref[1]) * paths + step]]
        rows = blocks[i].shape[0]

        def work(t, _, i=i, step=step, start=start, module=module):
            here = pl.ds(pl.multiple_of(t * tile, tile), tile)
            spot = pl.ds(pl.multiple_of(start + t * tile, tile), tile)
            a, b = outer_update(
                weights_ref[module, spot],
                moment_ref[module, spot],
                blocks[i][here].astype(jnp.float32),
            )
            new_weights[step, spot] = a
            new_moment[step, spot] = b
            return 0

        lax.fori_loop(0, rows // tile, work, 0)
        span = pl.ds(start, rows)
        for k, (src, dst) in enumerate(((new_weights, out_weights), (new_moment, out_moment))):
            copy = pltpu.make_async_copy(src.at[step, span], dst.at[module, span], sems.at[i, k])
            copy.start()
            copies.append(copy)
    for copy in copies:
        copy.wait()


def body(tokens, cotangent, module_table, module_weights, momentum):
    paths, shards = lax.axis_size("path"), lax.axis_size("fsdp")
    chips = shards // 2
    path_id, shard_id = lax.axis_index("path"), lax.axis_index("fsdp")
    tok_rows, width = tokens.shape[1:]
    module_count, rows, features = module_weights.shape
    step_size = math.sqrt(width / (tok_rows * shards))
    table = module_table[:, 0]
    where = jnp.stack([path_id, shard_id & 1, shard_id >> 1]).astype(jnp.int32)
    f32, bf16 = jnp.float32, jnp.bfloat16
    shape = jax.ShapeDtypeStruct
    dma = pltpu.SemaphoreType.DMA

    to_core = [(i, i ^ 1) for i in range(shards)]

    def to_chip(step):
        return [(i, (i + 2 * step) % shards) for i in range(shards)]

    own_weights = call(
        pick_rows, shape((rows, features), bf16), [SMEM, SMEM, ANY], VMEM,
        (table, where, module_weights), [dma],
    )
    lent_weights = [lax.ppermute(own_weights, "fsdp", to_chip(s)) for s in range(1, chips)]
    given = call(
        pick_columns, shape((tok_rows, chips * rows), bf16), [SMEM, ANY, ANY], VMEM,
        (where, tokens, own_weights), [dma((chips,))],
    )
    taken = lax.ppermute(given, "fsdp", to_core)
    other_up = lax.ppermute(cotangent[0], "fsdp", to_core)
    partial, turned = call(
        first_products,
        [shape((2 * tok_rows, features), f32), shape((chips * rows, 2 * tok_rows), bf16)],
        [SMEM] + [VMEM] * 3, [VMEM] * 2, (where, tokens, taken, own_weights),
    )
    for s in range(1, chips):
        partial = call(
            functools.partial(next_products, s), shape(partial.shape, f32),
            [SMEM] + [VMEM] * 4, VMEM, (where, tokens, taken, lent_weights[s - 1], partial),
        )
    other = lax.ppermute(partial, "fsdp", to_core)
    part = rows // CHAINS
    latent_cotangent, *sent = call(
        sent_gradients,
        [shape((2 * tok_rows, features), bf16)]
        + [shape((part, features), bf16)] * (CHAINS * (chips - 1)),
        [SMEM] + [VMEM] * 5, [VMEM] * (1 + CHAINS * (chips - 1)),
        (where, partial, other, cotangent[0], other_up, turned),
    )
    kept = call(
        kept_gradients, [shape((part, features), f32)] * CHAINS,
        [SMEM] + [VMEM] * 2, [VMEM] * CHAINS, (where, turned, latent_cotangent),
    )
    held = []
    for c in range(CHAINS):
        total = kept[c]
        for s in range(1, chips):
            arrived = lax.ppermute(sent[(s - 1) * CHAINS + c], "fsdp", to_chip(s))
            total = total + arrived.astype(f32)
        held.append(total * step_size)

    if paths != module_count:
        module = lax.dynamic_index_in_dim(table, path_id, 0, keepdims=False)
        module_ids = jnp.arange(module_count, dtype=jnp.int32)
        picked = (module_ids == module).astype(f32)
        counts = jnp.sum((table[:, None] == module_ids[None, :]).astype(f32), axis=0)
        summed = lax.psum(picked[:, None, None] * jnp.concatenate(held)[None], "path")
        return outer_update(module_weights, momentum, summed / counts[:, None, None])

    pairs, source = ring_plan(paths, shards)
    held = [h.astype(bf16) for h in held]
    blocks, steps = [], []
    for step in range(paths):
        for c in range(CHAINS):
            blocks.append(held[c])
            steps.append((step, c * part))
            if step < paths - 1:
                held[c] = lax.ppermute(held[c], ("path", "fsdp"), pairs)
    return call(
        functools.partial(apply_blocks, steps),
        [shape(module_weights.shape, bf16), shape(momentum.shape, f32)],
        [SMEM] * 3 + [VMEM] * (2 + len(blocks)), [ANY] * 2,
        (table, jnp.asarray(source.reshape(-1)), where, module_weights, momentum, *blocks),
        [
            pltpu.VMEM(module_weights.shape, bf16),
            pltpu.VMEM(momentum.shape, f32),
            dma((len(blocks), 2)),
        ],
        limit=16,
    )


def solution(mesh):
    return jax.shard_map(
        body,
        mesh=mesh,
        in_specs=(
            P("path", "fsdp", None),
            P("path", "fsdp", None),
            P(),
            P(None, "fsdp", None),
            P(None, "fsdp", None),
        ),
        out_specs=(P(None, "fsdp", None), P(None, "fsdp", None)),
        check_vma=False,
    )
```

time: 386 us -> 89.6 us (0.23)
  waiting for transfers between devices: 339 us -> 43 us
  starting transfers between devices: 0.12 us -> 31.2 us
  other arithmetic: 20.1 us -> 0.22 us
  between operations: 15.7 us -> 0.81 us
  Pallas kernels: 0 us -> 11.2 us
  matrix products: 5.09 us -> 0 us
    psum x1 -> x0, waiting for transfers between devices: 270 us -> none  [body(): summed = lax.psum(summand, 'path')]
    reduce_scatter x1 -> x0, waiting for transfers between devices: 44 us -> none  [body(): lax.psum_scatter(lax.dot_general(columns, latent_cotangent, (((0,), (0,))...]
    ppermute x0 -> x20, waiting for transfers between devices: none -> 43 us  [the longest x14 21.1 us: body(): held[c] = lax.ppermute(held[c], ('path', 'fsdp'), pairs)]
    ppermute x0 -> x20, starting transfers between devices: none -> 31.2 us  [the longest x14 25.4 us: body(): held[c] = lax.ppermute(held[c], ('path', 'fsdp'), pairs)]
    all_gather x1 -> x0, waiting for transfers between devices: 24.4 us -> none  [body(): lax.all_gather(shard_weights, 'fsdp', axis=0, tiled=True)]
    convert_element_type x2, other arithmetic: 13.4 us -> 0.15 us  [body(): held = [h.astype(bf16) for h in held]]
    pallas_call x0 -> x7, Pallas kernels: none -> 11.2 us  [call(): pl.pallas_call(kernel, in_specs=in_specs, out_specs=out_specs, out_shape=...]
    mul x2 -> x0, other arithmetic: 6.49 us -> none  [the longest x1 4.18 us: body(): summand = picked[:, None, None] * delta[None]]
  transfers between devices with their start and end apart: 3 -> 20, of which waited for: 3 -> 17; matrix products, arithmetic and copies ran while one was open for 0% -> 0% of each run, Pallas kernels for 0% -> 2%
where the time goes in v2:
time: 89.6 us; the launch traced here: 89.4 us
  waiting for transfers between devices  43 us (48%)
  starting transfers between devices  31.2 us (35%)
  Pallas kernels  11.2 us (12%)
  local copies, waits for them, and re-layouts  3.02 us (3%)
    ppermute x14, starting transfers between devices, body(): held[c] = lax.ppermute(held[c], ('path', 'fsdp'), pairs)  25.4 us
    ppermute x14, waiting for transfers between devices, body(): held[c] = lax.ppermute(held[c], ('path', 'fsdp'), pairs)  21.1 us
    ppermute x1, waiting for transfers between devices, body(): lax.ppermute(own_weights, 'fsdp', to_chip(s))  11.3 us
    pallas_call x7, Pallas kernels, call(): pl.pallas_call(kernel, in_specs=in_specs, out_specs=out_specs, out_shape=...  11.2 us
    ppermute x2, waiting for transfers between devices, body(): arrived = lax.ppermute(sent[(s - 1) * CHAINS + c], 'fsdp', to_chip(s))  9 us
    unnamed x18, local copies, waits for them, and re-layouts  3.02 us
    ppermute x1, starting transfers between devices, body(): lax.ppermute(own_weights, 'fsdp', to_chip(s))  2.56 us
    ppermute x2, starting transfers between devices, body(): arrived = lax.ppermute(sent[(s - 1) * CHAINS + c], 'fsdp', to_chip(s))  2.09 us
  transfers between devices with their start and end apart: 20, of which 17 were waited for; matrix products, arithmetic and copies ran while one was open for 0% of the time, Pallas kernels for 2%

profile of v2, /device:TPU:0, one launch (start us, length us, event | category | flops | bytes accessed | tf_op | source)
XLA Modules:
  0.0 89.4 jit_solution(7787921586552812289)
XLA Ops:
  0.6 0.0 copy-start
  0.6 0.1 pad_add_fusion.where_ref
  0.7 2.3 %copy-done.1 = bf16[8,1024,256]{2,1,0:T(8,128)(2,1)S(1)} copy-done((bf16[8,1024,256]{2,1,0:T(8,128)(2,1)S(1)}, bf16[8,1024,256]{2,1,0:T(8,128)(2,1)}, u32[]{:S(2)}) %copy-start.1) | copy-done | bytes 4194328
  3.0 0.7 copy-done.4
  3.7 0.6 pick_rows.1.after_ref.weights_ref
  4.3 0.0 copy-done
  4.3 0.0 slice-start
  4.3 0.7 pick_columns.1
  5.0 0.0 copy-start.3
  5.0 0.5 collective-permute-start
  5.5 2.6 %collective-permute-start.1 = (bf16[1024,256]{1,0:T(8,128)(2,1)S(1)}, bf16[1024,256]{1,0:T(8,128)(2,1)S(1)}, u32[]{:S(2)}, u32[]{:S(2)}) collective-permute-start(bf16[1024,256]{1,0:T(8,128)(2,1)S(1)} %pick_rows.1.after_ref.weights_ref), channel_id=1, source_target_pairs={{0,2},{1,3},{2,0},{3,1},{4,6},{5,7},{6,4},{7,5},{8,10},{9,11},{10,... | collective-permute-start | bytes 1572872 | tf_op jit(solution)/shard_map/ppermute | solution.py:208
  8.1 0.0 collective-permute-done.taken_ref
  8.1 1.2 %first_products.1 = (f32[512,256]{1,0:T(8,128)S(1)}, bf16[2048,512]{1,0:T(8,128)(2,1)S(1)}) custom-call(s32[3]{0:T(128)S(1)} %pad_add_fusion.where_ref, bf16[1,256,4096]{2,1,0:T(8,128)(2,1)S(1)} %copy-done, bf16[256,2048]{1,0:T(8,128)(2,1)S(1)} %collective-permute-done.taken_ref, bf16[1024,256]{1,0:T(8,128)(2,1)S(1)} %pick_rows.1.after_ref.weights_ref), custom_call_target="tpu_custom_call" | custom-call | tf_op jit(solution)/shard_map/first_products/pallas_call | solution.py:48
  9.3 11.3 %collective-permute-done.1.weights_ref = bf16[1024,256]{1,0:T(8,128)(2,1)S(1)} collective-permute-done((bf16[1024,256]{1,0:T(8,128)(2,1)S(1)}, bf16[1024,256]{1,0:T(8,128)(2,1)S(1)}, u32[]{:S(2)}, u32[]{:S(2)}) %collective-permute-start.1) | collective-permute-done | bytes 524320 | tf_op jit(solution)/shard_map/ppermute | solution.py:208
  20.6 1.0 %next_products.1.mine_ref = f32[512,256]{1,0:T(8,128)S(1)} custom-call(s32[3]{0:T(128)S(1)} %pad_add_fusion.where_ref, bf16[1,256,4096]{2,1,0:T(8,128)(2,1)S(1)} %copy-done, bf16[256,2048]{1,0:T(8,128)(2,1)S(1)} %collective-permute-done.taken_ref, bf16[1024,256]{1,0:T(8,128)(2,1)S(1)} %collective-permute-done.1.weights_ref, ...), custom_call_target="tpu_custom_call" | custom-call | tf_op jit(solution)/shard_map/next_products/pallas_call | solution.py:48
  21.6 0.0 copy-start.2
  21.6 0.0 copy-start.5
  21.6 0.0 copy-start.6
  21.6 0.1 collective-permute-start.2
  21.7 0.0 copy-done.3
  21.7 0.5 collective-permute-start.3
  22.2 1.6 %collective-permute-done.3.other_up_ref = bf16[256,256]{1,0:T(8,128)(2,1)S(1)} collective-permute-done((bf16[256,256]{1,0:T(8,128)(2,1)S(1)}, bf16[256,256]{1,0:T(8,128)(2,1)S(1)}, u32[]{:S(2)}, u32[]{:S(2)}) %collective-permute-start.3) | collective-permute-done | bytes 131104 | tf_op jit(solution)/shard_map/ppermute | solution.py:214
  23.8 0.0 collective-permute-done.2.other_ref
  23.8 1.2 %sent_gradients.1 = (bf16[512,256]{1,0:T(8,128)(2,1)S(1)}, bf16[512,256]{1,0:T(8,128)(2,1)S(1)}, bf16[512,256]{1,0:T(8,128)(2,1)S(1)}) custom-call(s32[3]{0:T(128)S(1)} %pad_add_fusion.where_ref, f32[512,256]{1,0:T(8,128)S(1)} %next_products.1.mine_ref, f32[512,256]{1,0:T(8,128)S(1)} %collective-permute-done.2.other_ref, bf16[256,256]{1,0:T(8,128)(2,1)S(1)} %bitcast.8, ...), custom_call_target="tpu_custom_call" | custom-call | tf_op jit(solution)/shard_map/sent_gradients/pallas_call | solution.py:48
  25.0 1.8 %collective-permute-start.4 = (bf16[512,256]{1,0:T(8,128)(2,1)S(1)}, bf16[512,256]{1,0:T(8,128)(2,1)S(1)}, u32[]{:S(2)}, u32[]{:S(2)}) collective-permute-start(bf16[512,256]{1,0:T(8,128)(2,1)S(1)} %get-tuple-element.13), channel_id=1, source_target_pairs={{0,2},{1,3},{2,0},{3,1},{4,6},{5,7},{6,4},{7,5},{8,10},{9,11},{10,... | collective-permute-start | bytes 786440 | tf_op jit(solution)/shard_map/ppermute | solution.py:242
  26.8 0.3 collective-permute-start.5
  27.1 1.0 %kept_gradients.1 = (f32[512,256]{1,0:T(8,128)S(1)}, f32[512,256]{1,0:T(8,128)S(1)}) custom-call(s32[3]{0:T(128)S(1)} %pad_add_fusion.where_ref, bf16[2048,512]{1,0:T(8,128)(2,1)S(1)} %get-tuple-element.9.turned_ref, bf16[512,256]{1,0:T(8,128)(2,1)S(1)} %get-tuple-element.11.latent_ref), custom_call_target="tpu_custom_call" | custom-call | tf_op jit(solution)/shard_map/kept_gradients/pallas_call | solution.py:48
  28.1 6.1 %collective-permute-done.4 = bf16[512,256]{1,0:T(8,128)(2,1)S(1)} collective-permute-done((bf16[512,256]{1,0:T(8,128)(2,1)S(1)}, bf16[512,256]{1,0:T(8,128)(2,1)S(1)}, u32[]{:S(2)}, u32[]{:S(2)}) %collective-permute-start.4) | collective-permute-done | bytes 262176 | tf_op jit(solution)/shard_map/ppermute | solution.py:242
  34.2 0.1 multiply_convert_fusion.1.refs_0_
  34.3 1.9 %collective-permute-start.6 = (bf16[512,256]{1,0:T(8,128)(2,1)S(1)}, bf16[512,256]{1,0:T(8,128)(2,1)S(1)}, u32[]{:S(2)}, u32[]{:S(2)}) collective-permute-start(bf16[512,256]{1,0:T(8,128)(2,1)S(1)} %multiply_convert_fusion.1.refs_0_), channel_id=1, source_target_pairs={{0,8},{1,5},{2,10},{3,7},{4,0},{5,13},{6,2},{7,15},{8,16},{9,1},{1... | collective-permute-start | bytes 786440 | tf_op jit(solution)/shard_map/ppermute | solution.py:262
  36.2 2.8 %collective-permute-done.5 = bf16[512,256]{1,0:T(8,128)(2,1)S(1)} collective-permute-done((bf16[512,256]{1,0:T(8,128)(2,1)S(1)}, bf16[512,256]{1,0:T(8,128)(2,1)S(1)}, u32[]{:S(2)}, u32[]{:S(2)}) %collective-permute-start.5) | collective-permute-done | bytes 262176 | tf_op jit(solution)/shard_map/ppermute | solution.py:242
  39.1 0.1 multiply_convert_fusion.refs_1_
  39.1 1.9 %collective-permute-start.7 = (bf16[512,256]{1,0:T(8,128)(2,1)S(1)}, bf16[512,256]{1,0:T(8,128)(2,1)S(1)}, u32[]{:S(2)}, u32[]{:S(2)}) collective-permute-start(bf16[512,256]{1,0:T(8,128)(2,1)S(1)} %multiply_convert_fusion.refs_1_), channel_id=1, source_target_pairs={{0,8},{1,5},{2,10},{3,7},{4,0},{5,13},{6,2},{7,15},{8,16},{9,1},{1... | collective-permute-start | bytes 786440 | tf_op jit(solution)/shard_map/ppermute | solution.py:262
  41.0 0.0 collective-permute-done.6.refs_2_
  41.0 1.6 %collective-permute-start.8 = (bf16[512,256]{1,0:T(8,128)(2,1)S(1)}, bf16[512,256]{1,0:T(8,128)(2,1)S(1)}, u32[]{:S(2)}, u32[]{:S(2)}) collective-permute-start(bf16[512,256]{1,0:T(8,128)(2,1)S(1)} %collective-permute-done.6.refs_2_), channel_id=1, source_target_pairs={{0,8},{1,5},{2,10},{3,7},{4,0},{5,13},{6,2},{7,15},{8,16},{9,1},{1... | collective-permute-start | bytes 786440 | tf_op jit(solution)/shard_map/ppermute | solution.py:262
  42.6 3.0 %collective-permute-done.7.refs_3_ = bf16[512,256]{1,0:T(8,128)(2,1)S(1)} collective-permute-done((bf16[512,256]{1,0:T(8,128)(2,1)S(1)}, bf16[512,256]{1,0:T(8,128)(2,1)S(1)}, u32[]{:S(2)}, u32[]{:S(2)}) %collective-permute-start.7) | collective-permute-done | bytes 262176 | tf_op jit(solution)/shard_map/ppermute | solution.py:262
  45.5 1.8 %collective-permute-start.9 = (bf16[512,256]{1,0:T(8,128)(2,1)S(1)}, bf16[512,256]{1,0:T(8,128)(2,1)S(1)}, u32[]{:S(2)}, u32[]{:S(2)}) collective-permute-start(bf16[512,256]{1,0:T(8,128)(2,1)S(1)} %collective-permute-done.7.refs_3_), channel_id=1, source_target_pairs={{0,8},{1,5},{2,10},{3,7},{4,0},{5,13},{6,2},{7,15},{8,16},{9,1},{1... | collective-permute-start | bytes 786440 | tf_op jit(solution)/shard_map/ppermute | solution.py:262
  47.4 1.0 %collective-permute-done.8.refs_4_ = bf16[512,256]{1,0:T(8,128)(2,1)S(1)} collective-permute-done((bf16[512,256]{1,0:T(8,128)(2,1)S(1)}, bf16[512,256]{1,0:T(8,128)(2,1)S(1)}, u32[]{:S(2)}, u32[]{:S(2)}) %collective-permute-start.8) | collective-permute-done | bytes 262176 | tf_op jit(solution)/shard_map/ppermute | solution.py:262
  48.4 1.8 %collective-permute-start.10 = (bf16[512,256]{1,0:T(8,128)(2,1)S(1)}, bf16[512,256]{1,0:T(8,128)(2,1)S(1)}, u32[]{:S(2)}, u32[]{:S(2)}) collective-permute-start(bf16[512,256]{1,0:T(8,128)(2,1)S(1)} %collective-permute-done.8.refs_4_), channel_id=1, source_target_pairs={{0,8},{1,5},{2,10},{3,7},{4,0},{5,13},{6,2},{7,15},{8,16},{9,1},{1... | collective-permute-start | bytes 786440 | tf_op jit(solution)/shard_map/ppermute | solution.py:262
  50.2 1.7 %collective-permute-done.9.refs_5_ = bf16[512,256]{1,0:T(8,128)(2,1)S(1)} collective-permute-done((bf16[512,256]{1,0:T(8,128)(2,1)S(1)}, bf16[512,256]{1,0:T(8,128)(2,1)S(1)}, u32[]{:S(2)}, u32[]{:S(2)}) %collective-permute-start.9) | collective-permute-done | bytes 262176 | tf_op jit(solution)/shard_map/ppermute | solution.py:262
  51.9 1.8 %collective-permute-start.11 = (bf16[512,256]{1,0:T(8,128)(2,1)S(1)}, bf16[512,256]{1,0:T(8,128)(2,1)S(1)}, u32[]{:S(2)}, u32[]{:S(2)}) collective-permute-start(bf16[512,256]{1,0:T(8,128)(2,1)S(1)} %collective-permute-done.9.refs_5_), channel_id=1, source_target_pairs={{0,8},{1,5},{2,10},{3,7},{4,0},{5,13},{6,2},{7,15},{8,16},{9,1},{1... | collective-permute-start | bytes 786440 | tf_op jit(solution)/shard_map/ppermute | solution.py:262
  53.7 1.0 %collective-permute-done.10.refs_6_ = bf16[512,256]{1,0:T(8,128)(2,1)S(1)} collective-permute-done((bf16[512,256]{1,0:T(8,128)(2,1)S(1)}, bf16[512,256]{1,0:T(8,128)(2,1)S(1)}, u32[]{:S(2)}, u32[]{:S(2)}) %collective-permute-start.10) | collective-permute-done | bytes 262176 | tf_op jit(solution)/shard_map/ppermute | solution.py:262
  54.7 1.8 %collective-permute-start.12 = (bf16[512,256]{1,0:T(8,128)(2,1)S(1)}, bf16[512,256]{1,0:T(8,128)(2,1)S(1)}, u32[]{:S(2)}, u32[]{:S(2)}) collective-permute-start(bf16[512,256]{1,0:T(8,128)(2,1)S(1)} %collective-permute-done.10.refs_6_), channel_id=1, source_target_pairs={{0,8},{1,5},{2,10},{3,7},{4,0},{5,13},{6,2},{7,15},{8,16},{9,1},{1... | collective-permute-start | bytes 786440 | tf_op jit(solution)/shard_map/ppermute | solution.py:262
  56.6 1.7 %collective-permute-done.11.refs_7_ = bf16[512,256]{1,0:T(8,128)(2,1)S(1)} collective-permute-done((bf16[512,256]{1,0:T(8,128)(2,1)S(1)}, bf16[512,256]{1,0:T(8,128)(2,1)S(1)}, u32[]{:S(2)}, u32[]{:S(2)}) %collective-permute-start.11) | collective-permute-done | bytes 262176 | tf_op jit(solution)/shard_map/ppermute | solution.py:262
  58.3 1.8 %collective-permute-start.13 = (bf16[512,256]{1,0:T(8,128)(2,1)S(1)}, bf16[512,256]{1,0:T(8,128)(2,1)S(1)}, u32[]{:S(2)}, u32[]{:S(2)}) collective-permute-start(bf16[512,256]{1,0:T(8,128)(2,1)S(1)} %collective-permute-done.11.refs_7_), channel_id=1, source_target_pairs={{0,8},{1,5},{2,10},{3,7},{4,0},{5,13},{6,2},{7,15},{8,16},{9,1},{1... | collective-permute-start | bytes 786440 | tf_op jit(solution)/shard_map/ppermute | solution.py:262
  60.1 1.0 %collective-permute-done.12.refs_8_ = bf16[512,256]{1,0:T(8,128)(2,1)S(1)} collective-permute-done((bf16[512,256]{1,0:T(8,128)(2,1)S(1)}, bf16[512,256]{1,0:T(8,128)(2,1)S(1)}, u32[]{:S(2)}, u32[]{:S(2)}) %collective-permute-start.12) | collective-permute-done | bytes 262176 | tf_op jit(solution)/shard_map/ppermute | solution.py:262
  61.1 1.8 %collective-permute-start.14 = (bf16[512,256]{1,0:T(8,128)(2,1)S(1)}, bf16[512,256]{1,0:T(8,128)(2,1)S(1)}, u32[]{:S(2)}, u32[]{:S(2)}) collective-permute-start(bf16[512,256]{1,0:T(8,128)(2,1)S(1)} %collective-permute-done.12.refs_8_), channel_id=1, source_target_pairs={{0,8},{1,5},{2,10},{3,7},{4,0},{5,13},{6,2},{7,15},{8,16},{9,1},{1... | collective-permute-start | bytes 786440 | tf_op jit(solution)/shard_map/ppermute | solution.py:262
  62.9 1.7 %collective-permute-done.13.refs_9_ = bf16[512,256]{1,0:T(8,128)(2,1)S(1)} collective-permute-done((bf16[512,256]{1,0:T(8,128)(2,1)S(1)}, bf16[512,256]{1,0:T(8,128)(2,1)S(1)}, u32[]{:S(2)}, u32[]{:S(2)}) %collective-permute-start.13) | collective-permute-done | bytes 262176 | tf_op jit(solution)/shard_map/ppermute | solution.py:262
  64.7 1.8 %collective-permute-start.15 = (bf16[512,256]{1,0:T(8,128)(2,1)S(1)}, bf16[512,256]{1,0:T(8,128)(2,1)S(1)}, u32[]{:S(2)}, u32[]{:S(2)}) collective-permute-start(bf16[512,256]{1,0:T(8,128)(2,1)S(1)} %collective-permute-done.13.refs_9_), channel_id=1, source_target_pairs={{0,8},{1,5},{2,10},{3,7},{4,0},{5,13},{6,2},{7,15},{8,16},{9,1},{1... | collective-permute-start | bytes 786440 | tf_op jit(solution)/shard_map/ppermute | solution.py:262
  66.5 1.0 %collective-permute-done.14.refs_10_ = bf16[512,256]{1,0:T(8,128)(2,1)S(1)} collective-permute-done((bf16[512,256]{1,0:T(8,128)(2,1)S(1)}, bf16[512,256]{1,0:T(8,128)(2,1)S(1)}, u32[]{:S(2)}, u32[]{:S(2)}) %collective-permute-start.14) | collective-permute-done | bytes 262176 | tf_op jit(solution)/shard_map/ppermute | solution.py:262
  67.5 1.8 %collective-permute-start.16 = (bf16[512,256]{1,0:T(8,128)(2,1)S(1)}, bf16[512,256]{1,0:T(8,128)(2,1)S(1)}, u32[]{:S(2)}, u32[]{:S(2)}) collective-permute-start(bf16[512,256]{1,0:T(8,128)(2,1)S(1)} %collective-permute-done.14.refs_10_), channel_id=1, source_target_pairs={{0,8},{1,5},{2,10},{3,7},{4,0},{5,13},{6,2},{7,15},{8,16},{9,1},{1... | collective-permute-start | bytes 786440 | tf_op jit(solution)/shard_map/ppermute | solution.py:262
  69.3 1.7 %collective-permute-done.15.refs_11_ = bf16[512,256]{1,0:T(8,128)(2,1)S(1)} collective-permute-done((bf16[512,256]{1,0:T(8,128)(2,1)S(1)}, bf16[512,256]{1,0:T(8,128)(2,1)S(1)}, u32[]{:S(2)}, u32[]{:S(2)}) %collective-permute-start.15) | collective-permute-done | bytes 262176 | tf_op jit(solution)/shard_map/ppermute | solution.py:262
  71.0 1.8 %collective-permute-start.17 = (bf16[512,256]{1,0:T(8,128)(2,1)S(1)}, bf16[512,256]{1,0:T(8,128)(2,1)S(1)}, u32[]{:S(2)}, u32[]{:S(2)}) collective-permute-start(bf16[512,256]{1,0:T(8,128)(2,1)S(1)} %collective-permute-done.15.refs_11_), channel_id=1, source_target_pairs={{0,8},{1,5},{2,10},{3,7},{4,0},{5,13},{6,2},{7,15},{8,16},{9,1},{1... | collective-permute-start | bytes 786440 | tf_op jit(solution)/shard_map/ppermute | solution.py:262
  72.9 1.0 %collective-permute-done.16.refs_12_ = bf16[512,256]{1,0:T(8,128)(2,1)S(1)} collective-permute-done((bf16[512,256]{1,0:T(8,128)(2,1)S(1)}, bf16[512,256]{1,0:T(8,128)(2,1)S(1)}, u32[]{:S(2)}, u32[]{:S(2)}) %collective-permute-start.16) | collective-permute-done | bytes 262176 | tf_op jit(solution)/shard_map/ppermute | solution.py:262
  73.8 1.8 %collective-permute-start.18 = (bf16[512,256]{1,0:T(8,128)(2,1)S(1)}, bf16[512,256]{1,0:T(8,128)(2,1)S(1)}, u32[]{:S(2)}, u32[]{:S(2)}) collective-permute-start(bf16[512,256]{1,0:T(8,128)(2,1)S(1)} %collective-permute-done.16.refs_12_), channel_id=1, source_target_pairs={{0,8},{1,5},{2,10},{3,7},{4,0},{5,13},{6,2},{7,15},{8,16},{9,1},{1... | collective-permute-start | bytes 786440 | tf_op jit(solution)/shard_map/ppermute | solution.py:262
  75.7 1.7 %collective-permute-done.17.refs_13_ = bf16[512,256]{1,0:T(8,128)(2,1)S(1)} collective-permute-done((bf16[512,256]{1,0:T(8,128)(2,1)S(1)}, bf16[512,256]{1,0:T(8,128)(2,1)S(1)}, u32[]{:S(2)}, u32[]{:S(2)}) %collective-permute-start.17) | collective-permute-done | bytes 262176 | tf_op jit(solution)/shard_map/ppermute | solution.py:262
  77.4 1.8 %collective-permute-start.19 = (bf16[512,256]{1,0:T(8,128)(2,1)S(1)}, bf16[512,256]{1,0:T(8,128)(2,1)S(1)}, u32[]{:S(2)}, u32[]{:S(2)}) collective-permute-start(bf16[512,256]{1,0:T(8,128)(2,1)S(1)} %collective-permute-done.17.refs_13_), channel_id=1, source_target_pairs={{0,8},{1,5},{2,10},{3,7},{4,0},{5,13},{6,2},{7,15},{8,16},{9,1},{1... | collective-permute-start | bytes 786440 | tf_op jit(solution)/shard_map/ppermute | solution.py:262
  79.2 1.0 %collective-permute-done.18.refs_14_ = bf16[512,256]{1,0:T(8,128)(2,1)S(1)} collective-permute-done((bf16[512,256]{1,0:T(8,128)(2,1)S(1)}, bf16[512,256]{1,0:T(8,128)(2,1)S(1)}, u32[]{:S(2)}, u32[]{:S(2)}) %collective-permute-start.18) | collective-permute-done | bytes 262176 | tf_op jit(solution)/shard_map/ppermute | solution.py:262
  80.2 3.6 %collective-permute-done.19.refs_15_ = bf16[512,256]{1,0:T(8,128)(2,1)S(1)} collective-permute-done((bf16[512,256]{1,0:T(8,128)(2,1)S(1)}, bf16[512,256]{1,0:T(8,128)(2,1)S(1)}, u32[]{:S(2)}, u32[]{:S(2)}) %collective-permute-start.19) | collective-permute-done | bytes 262176 | tf_op jit(solution)/shard_map/ppermute | solution.py:262
  83.8 0.0 slice-done
  83.8 0.0 slice-done.1
  83.8 0.0 copy-done.2
  83.8 0.0 copy-done.5
  83.8 5.6 %apply_blocks.1 = (bf16[8,1024,256]{2,1,0:T(8,128)(2,1)}, f32[8,1024,256]{2,1,0:T(8,128)}) custom-call(s32[8]{0:T(128)S(1)} %bitcast.10, s32[128]{0:T(128)S(1)} %copy-done.6, s32[3]{0:T(128)S(1)} %pad_add_fusion.where_ref, bf16[8,1024,256]{2,1,0:T(8,128)(2,1)S(1)} %copy-done.2, f32[8,1024,256]{2,1,0:T(8,128)S(1)} %bitcast.6, ...), custom_call_target="tpu_custom_call" | custom-call | tf_op jit(solution)/shard_map/apply_blocks/pallas_call | solution.py:48
  (5 shorter events, 0.0 us)
Async XLA Ops:
  0.6 3.7 %copy-start = (bf16[1,256,4096]{2,1,0:T(8,128)(2,1)S(1)}, bf16[1,256,4096]{2,1,0:T(8,128)(2,1)}, u32[]{:S(2)}) copy-start(bf16[1,256,4096]{2,1,0:T(8,128)(2,1)} %tokens_ref.5) | copy-start | bytes 6291460
  0.7 2.3 %copy-start.1 = (bf16[8,1024,256]{2,1,0:T(8,128)(2,1)S(1)}, bf16[8,1024,256]{2,1,0:T(8,128)(2,1)}, u32[]{:S(2)}) copy-start(bf16[8,1024,256]{2,1,0:T(8,128)(2,1)} %weights_ref.3) | copy-start | bytes 12582916
  3.0 0.7 copy-start.4
  4.3 79.5 %slice-start = ((s8[8388608]{0:T(1024)(128)(4,1)}), s8[4194304]{0:T(1024)(128)(4,1)S(1)}, s32[]{:S(2)}) async-start(s8[8388608]{0:T(1024)(128)(4,1)} %bitcast.5), calls=%async_computation | async-start | bytes 8388608
  5.0 16.7 %copy-start.3 = (bf16[1,256,256]{2,1,0:T(8,128)(2,1)S(1)}, bf16[1,256,256]{2,1,0:T(8,128)(2,1)}, u32[]{:S(2)}) copy-start(bf16[1,256,256]{2,1,0:T(8,128)(2,1)} %param.7) | copy-start | bytes 393220
  5.0 3.1 %collective-permute-start = (bf16[256,2048]{1,0:T(8,128)(2,1)S(1)}, bf16[256,2048]{1,0:T(8,128)(2,1)S(1)}, u32[]{:S(2)}, u32[]{:S(2)}) collective-permute-start(bf16[256,2048]{1,0:T(8,128)(2,1)S(1)} %pick_columns.1), channel_id=1, source_target_pairs={{0,1},{1,0},{2,3},{3,2},{4,5},{5,4},{6,7},{7,6},{8,9},{9,8},{10,11... | collective-permute-start | bytes 3145736 | tf_op jit(solution)/shard_map/ppermute | solution.py:213
  5.5 15.1 %collective-permute-start.1 = (bf16[1024,256]{1,0:T(8,128)(2,1)S(1)}, bf16[1024,256]{1,0:T(8,128)(2,1)S(1)}, u32[]{:S(2)}, u32[]{:S(2)}) collective-permute-start(bf16[1024,256]{1,0:T(8,128)(2,1)S(1)} %pick_rows.1.after_ref.weights_ref), channel_id=1, source_target_pairs={{0,2},{1,3},{2,0},{3,1},{4,6},{5,7},{6,4},{7,5},{8,10},{9,11},{10,... | collective-permute-start | bytes 1572872 | tf_op jit(solution)/shard_map/ppermute | solution.py:208
  20.6 63.2 %slice-start.1 = ((s8[8388608]{0:T(1024)(128)(4,1)}), s8[4194304]{0:T(1024)(128)(4,1)S(1)}, s32[]{:S(2)}) async-start(s8[8388608]{0:T(1024)(128)(4,1)} %bitcast.5), calls=%async_computation.1 | async-start | bytes 8388608
  21.6 62.2 %copy-start.2 = (bf16[8,1024,256]{2,1,0:T(8,128)(2,1)S(1)}, bf16[8,1024,256]{2,1,0:T(8,128)(2,1)}, u32[]{:S(2)}) copy-start(bf16[8,1024,256]{2,1,0:T(8,128)(2,1)} %weights_ref.3) | copy-start | bytes 12582916
  21.6 62.2 %copy-start.5 = (s32[8,1]{0,1:T(1,128)S(1)}, s32[8,1]{0,1:T(1,128)}, u32[]{:S(2)}) copy-start(s32[8,1]{0,1:T(1,128)} %param.8) | copy-start | bytes 100
  21.6 62.2 %copy-start.6 = (s32[128]{0:T(128)S(1)}, s32[128]{0:T(128)}, u32[]{:S(2)}) copy-start(s32[128]{0:T(128)} %constant.15.clone.source_ref) | copy-start | bytes 1540
  21.6 2.2 %collective-permute-start.2 = (f32[512,256]{1,0:T(8,128)S(1)}, f32[512,256]{1,0:T(8,128)S(1)}, u32[]{:S(2)}, u32[]{:S(2)}) collective-permute-start(f32[512,256]{1,0:T(8,128)S(1)} %next_products.1.mine_ref), channel_id=1, source_target_pairs={{0,1},{1,0},{2,3},{3,2},{4,5},{5,4},{6,7},{7,6},{8,9},{9,8},{10,11... | collective-permute-start | bytes 1572872 | tf_op jit(solution)/shard_map/ppermute | solution.py:225
  21.7 2.1 %collective-permute-start.3 = (bf16[256,256]{1,0:T(8,128)(2,1)S(1)}, bf16[256,256]{1,0:T(8,128)(2,1)S(1)}, u32[]{:S(2)}, u32[]{:S(2)}) collective-permute-start(bf16[256,256]{1,0:T(8,128)(2,1)S(1)} %bitcast.7), channel_id=1, source_target_pairs={{0,1},{1,0},{2,3},{3,2},{4,5},{5,4},{6,7},{7,6},{8,9},{9,8},{10,11... | collective-permute-start | bytes 393224 | tf_op jit(solution)/shard_map/ppermute | solution.py:214
  25.0 9.2 %collective-permute-start.4 = (bf16[512,256]{1,0:T(8,128)(2,1)S(1)}, bf16[512,256]{1,0:T(8,128)(2,1)S(1)}, u32[]{:S(2)}, u32[]{:S(2)}) collective-permute-start(bf16[512,256]{1,0:T(8,128)(2,1)S(1)} %get-tuple-element.13), channel_id=1, source_target_pairs={{0,2},{1,3},{2,0},{3,1},{4,6},{5,7},{6,4},{7,5},{8,10},{9,11},{10,... | collective-permute-start | bytes 786440 | tf_op jit(solution)/shard_map/ppermute | solution.py:242
  26.8 12.2 %collective-permute-start.5 = (bf16[512,256]{1,0:T(8,128)(2,1)S(1)}, bf16[512,256]{1,0:T(8,128)(2,1)S(1)}, u32[]{:S(2)}, u32[]{:S(2)}) collective-permute-start(bf16[512,256]{1,0:T(8,128)(2,1)S(1)} %get-tuple-element.15), channel_id=1, source_target_pairs={{0,2},{1,3},{2,0},{3,1},{4,6},{5,7},{6,4},{7,5},{8,10},{9,11},{10,... | collective-permute-start | bytes 786440 | tf_op jit(solution)/shard_map/ppermute | solution.py:242
  34.3 6.7 %collective-permute-start.6 = (bf16[512,256]{1,0:T(8,128)(2,1)S(1)}, bf16[512,256]{1,0:T(8,128)(2,1)S(1)}, u32[]{:S(2)}, u32[]{:S(2)}) collective-permute-start(bf16[512,256]{1,0:T(8,128)(2,1)S(1)} %multiply_convert_fusion.1.refs_0_), channel_id=1, source_target_pairs={{0,8},{1,5},{2,10},{3,7},{4,0},{5,13},{6,2},{7,15},{8,16},{9,1},{1... | collective-permute-start | bytes 786440 | tf_op jit(solution)/shard_map/ppermute | solution.py:262
  39.1 6.4 %collective-permute-start.7 = (bf16[512,256]{1,0:T(8,128)(2,1)S(1)}, bf16[512,256]{1,0:T(8,128)(2,1)S(1)}, u32[]{:S(2)}, u32[]{:S(2)}) collective-permute-start(bf16[512,256]{1,0:T(8,128)(2,1)S(1)} %multiply_convert_fusion.refs_1_), channel_id=1, source_target_pairs={{0,8},{1,5},{2,10},{3,7},{4,0},{5,13},{6,2},{7,15},{8,16},{9,1},{1... | collective-permute-start | bytes 786440 | tf_op jit(solution)/shard_map/ppermute | solution.py:262
  41.0 7.4 %collective-permute-start.8 = (bf16[512,256]{1,0:T(8,128)(2,1)S(1)}, bf16[512,256]{1,0:T(8,128)(2,1)S(1)}, u32[]{:S(2)}, u32[]{:S(2)}) collective-permute-start(bf16[512,256]{1,0:T(8,128)(2,1)S(1)} %collective-permute-done.6.refs_2_), channel_id=1, source_target_pairs={{0,8},{1,5},{2,10},{3,7},{4,0},{5,13},{6,2},{7,15},{8,16},{9,1},{1... | collective-permute-start | bytes 786440 | tf_op jit(solution)/shard_map/ppermute | solution.py:262
  45.5 6.4 %collective-permute-start.9 = (bf16[512,256]{1,0:T(8,128)(2,1)S(1)}, bf16[512,256]{1,0:T(8,128)(2,1)S(1)}, u32[]{:S(2)}, u32[]{:S(2)}) collective-permute-start(bf16[512,256]{1,0:T(8,128)(2,1)S(1)} %collective-permute-done.7.refs_3_), channel_id=1, source_target_pairs={{0,8},{1,5},{2,10},{3,7},{4,0},{5,13},{6,2},{7,15},{8,16},{9,1},{1... | collective-permute-start | bytes 786440 | tf_op jit(solution)/shard_map/ppermute | solution.py:262
  48.4 6.4 %collective-permute-start.10 = (bf16[512,256]{1,0:T(8,128)(2,1)S(1)}, bf16[512,256]{1,0:T(8,128)(2,1)S(1)}, u32[]{:S(2)}, u32[]{:S(2)}) collective-permute-start(bf16[512,256]{1,0:T(8,128)(2,1)S(1)} %collective-permute-done.8.refs_4_), channel_id=1, source_target_pairs={{0,8},{1,5},{2,10},{3,7},{4,0},{5,13},{6,2},{7,15},{8,16},{9,1},{1... | collective-permute-start | bytes 786440 | tf_op jit(solution)/shard_map/ppermute | solution.py:262
  51.9 6.4 %collective-permute-start.11 = (bf16[512,256]{1,0:T(8,128)(2,1)S(1)}, bf16[512,256]{1,0:T(8,128)(2,1)S(1)}, u32[]{:S(2)}, u32[]{:S(2)}) collective-permute-start(bf16[512,256]{1,0:T(8,128)(2,1)S(1)} %collective-permute-done.9.refs_5_), channel_id=1, source_target_pairs={{0,8},{1,5},{2,10},{3,7},{4,0},{5,13},{6,2},{7,15},{8,16},{9,1},{1... | collective-permute-start | bytes 786440 | tf_op jit(solution)/shard_map/ppermute | solution.py:262
  54.7 6.4 %collective-permute-start.12 = (bf16[512,256]{1,0:T(8,128)(2,1)S(1)}, bf16[512,256]{1,0:T(8,128)(2,1)S(1)}, u32[]{:S(2)}, u32[]{:S(2)}) collective-permute-start(bf16[512,256]{1,0:T(8,128)(2,1)S(1)} %collective-permute-done.10.refs_6_), channel_id=1, source_target_pairs={{0,8},{1,5},{2,10},{3,7},{4,0},{5,13},{6,2},{7,15},{8,16},{9,1},{1... | collective-permute-start | bytes 786440 | tf_op jit(solution)/shard_map/ppermute | solution.py:262
  58.3 6.4 %collective-permute-start.13 = (bf16[512,256]{1,0:T(8,128)(2,1)S(1)}, bf16[512,256]{1,0:T(8,128)(2,1)S(1)}, u32[]{:S(2)}, u32[]{:S(2)}) collective-permute-start(bf16[512,256]{1,0:T(8,128)(2,1)S(1)} %collective-permute-done.11.refs_7_), channel_id=1, source_target_pairs={{0,8},{1,5},{2,10},{3,7},{4,0},{5,13},{6,2},{7,15},{8,16},{9,1},{1... | collective-permute-start | bytes 786440 | tf_op jit(solution)/shard_map/ppermute | solution.py:262
  61.1 6.4 %collective-permute-start.14 = (bf16[512,256]{1,0:T(8,128)(2,1)S(1)}, bf16[512,256]{1,0:T(8,128)(2,1)S(1)}, u32[]{:S(2)}, u32[]{:S(2)}) collective-permute-start(bf16[512,256]{1,0:T(8,128)(2,1)S(1)} %collective-permute-done.12.refs_8_), channel_id=1, source_target_pairs={{0,8},{1,5},{2,10},{3,7},{4,0},{5,13},{6,2},{7,15},{8,16},{9,1},{1... | collective-permute-start | bytes 786440 | tf_op jit(solution)/shard_map/ppermute | solution.py:262
  64.7 6.4 %collective-permute-start.15 = (bf16[512,256]{1,0:T(8,128)(2,1)S(1)}, bf16[512,256]{1,0:T(8,128)(2,1)S(1)}, u32[]{:S(2)}, u32[]{:S(2)}) collective-permute-start(bf16[512,256]{1,0:T(8,128)(2,1)S(1)} %collective-permute-done.13.refs_9_), channel_id=1, source_target_pairs={{0,8},{1,5},{2,10},{3,7},{4,0},{5,13},{6,2},{7,15},{8,16},{9,1},{1... | collective-permute-start | bytes 786440 | tf_op jit(solution)/shard_map/ppermute | solution.py:262
  67.5 6.4 %collective-permute-start.16 = (bf16[512,256]{1,0:T(8,128)(2,1)S(1)}, bf16[512,256]{1,0:T(8,128)(2,1)S(1)}, u32[]{:S(2)}, u32[]{:S(2)}) collective-permute-start(bf16[512,256]{1,0:T(8,128)(2,1)S(1)} %collective-permute-done.14.refs_10_), channel_id=1, source_target_pairs={{0,8},{1,5},{2,10},{3,7},{4,0},{5,13},{6,2},{7,15},{8,16},{9,1},{1... | collective-permute-start | bytes 786440 | tf_op jit(solution)/shard_map/ppermute | solution.py:262
  71.0 6.4 %collective-permute-start.17 = (bf16[512,256]{1,0:T(8,128)(2,1)S(1)}, bf16[512,256]{1,0:T(8,128)(2,1)S(1)}, u32[]{:S(2)}, u32[]{:S(2)}) collective-permute-start(bf16[512,256]{1,0:T(8,128)(2,1)S(1)} %collective-permute-done.15.refs_11_), channel_id=1, source_target_pairs={{0,8},{1,5},{2,10},{3,7},{4,0},{5,13},{6,2},{7,15},{8,16},{9,1},{1... | collective-permute-start | bytes 786440 | tf_op jit(solution)/shard_map/ppermute | solution.py:262
  73.8 6.4 %collective-permute-start.18 = (bf16[512,256]{1,0:T(8,128)(2,1)S(1)}, bf16[512,256]{1,0:T(8,128)(2,1)S(1)}, u32[]{:S(2)}, u32[]{:S(2)}) collective-permute-start(bf16[512,256]{1,0:T(8,128)(2,1)S(1)} %collective-permute-done.16.refs_12_), channel_id=1, source_target_pairs={{0,8},{1,5},{2,10},{3,7},{4,0},{5,13},{6,2},{7,15},{8,16},{9,1},{1... | collective-permute-start | bytes 786440 | tf_op jit(solution)/shard_map/ppermute | solution.py:262
  77.4 6.4 %collective-permute-start.19 = (bf16[512,256]{1,0:T(8,128)(2,1)S(1)}, bf16[512,256]{1,0:T(8,128)(2,1)S(1)}, u32[]{:S(2)}, u32[]{:S(2)}) collective-permute-start(bf16[512,256]{1,0:T(8,128)(2,1)S(1)} %collective-permute-done.17.refs_13_), channel_id=1, source_target_pairs={{0,8},{1,5},{2,10},{3,7},{4,0},{5,13},{6,2},{7,15},{8,16},{9,1},{1... | collective-permute-start | bytes 786440 | tf_op jit(solution)/shard_map/ppermute | solution.py:262

commit v3 on v2

v3 whole, which is shorter than its diff:
```python
import functools
import math

import jax
import jax.numpy as jnp
from jax import lax
from jax.experimental import pallas as pl
from jax.experimental.pallas import tpu as pltpu
from jax.sharding import PartitionSpec as P

CHAINS = 2
PIECES = 4
MIB = 1 << 20
VMEM = pl.BlockSpec(memory_space=pltpu.VMEM)
SMEM = pl.BlockSpec(memory_space=pltpu.SMEM)
HBM = pl.BlockSpec(memory_space=pltpu.HBM)


def outer_update(weights, moment, average):
    new_moment = 0.9 * moment + average
    new_weights = (weights.astype(jnp.float32) - 0.7 * (average + 0.9 * new_moment)).astype(
        jnp.bfloat16
    )
    return (new_weights, new_moment)


def ring_order(paths):
    return [p for p in range(0, paths, 2)] + [p for p in range(paths - 1, 0, -2)]


def modules_on_ring(table, path_id):
    paths = table.shape[0]
    ids = jnp.arange(paths, dtype=jnp.int32)
    order = jnp.asarray(ring_order(paths), jnp.int32)
    place = jnp.sum(jnp.where(order == path_id, ids, 0))
    there = (ids + ids[:, None, None]) % paths == place
    on_ring = jnp.sum(jnp.where(there, order, 0), axis=-1, keepdims=True)[:, 0]
    modules = jnp.max(jnp.where(on_ring == ids, table, 0), axis=-1, keepdims=True)
    return jnp.broadcast_to(modules, (paths, 128)).astype(jnp.int32)


def ring_pairs(paths):
    order = ring_order(paths)
    place = {p: i for i, p in enumerate(order)}
    return {way: [(p, order[(place[p] + way) % paths]) for p in range(paths)] for way in (1, -1)}


def cuts(rows):
    unit = next(u for u in (64, 32, 16, 1) if rows % u == 0 and rows >= u * CHAINS)
    share, more = divmod(rows // unit, CHAINS)
    sizes = [unit * (share + (c < more)) for c in range(CHAINS)]
    return [(sum(sizes[:c]), size) for c, size in enumerate(sizes)]


def call(
    kernel, out_shape, in_specs, out_specs, args, scratch=(), limit=8, traffic=0, aliases=None
):
    return pl.pallas_call(
        kernel,
        in_specs=in_specs,
        out_specs=out_specs,
        out_shape=out_shape,
        scratch_shapes=list(scratch),
        compiler_params=pltpu.CompilerParams(vmem_limit_bytes=limit * MIB),
        cost_estimate=pl.CostEstimate(flops=0, bytes_accessed=traffic, transcendentals=0),
        input_output_aliases=aliases or {},
        name=kernel.func.__name__ if isinstance(kernel, functools.partial) else kernel.__name__,
    )(*args)


def core_and_chip():
    shard = lax.axis_index("fsdp")
    return shard & 1, shard >> 1


def pick_rows(table_ref, weights_ref, out_ref, sem):
    module = table_ref[lax.axis_index("path")]
    copy = pltpu.make_async_copy(weights_ref.at[module], out_ref, sem)
    copy.start()
    copy.wait()


def pick_columns(tokens_ref, after_ref, *refs):
    outs, sem = refs[:-1], refs[-1]
    rows = after_ref.shape[0]
    core, _ = core_and_chip()
    copies = []
    for i, out_ref in enumerate(outs):
        part = out_ref.shape[0]
        for block in range(out_ref.shape[1] // rows):
            start = pl.multiple_of((2 * block + 1 - core) * rows, 128)
            copies.append(
                pltpu.make_async_copy(
                    tokens_ref.at[0, pl.ds(i * part, part), pl.ds(start, rows)],
                    out_ref.at[:, pl.ds(block * rows, rows)],
                    sem.at[i, block],
                )
            )
    for copy in copies:
        copy.start()
    for copy in copies:
        copy.wait()


def products(tokens_ref, taken_ref, weights_ref, block):
    rows = weights_ref.shape[0]
    core, _ = core_and_chip()
    own = pl.multiple_of((2 * block + core) * rows, 128)
    lent = pl.multiple_of(block * rows, 128)
    weights = weights_ref[...]
    return (
        jnp.dot(tokens_ref[0, :, pl.ds(own, rows)], weights, preferred_element_type=jnp.float32),
        jnp.dot(taken_ref[:, pl.ds(lent, rows)], weights, preferred_element_type=jnp.float32),
    )


def first_products(tokens_ref, weights_ref, *refs):
    pieces, (out_ref, turned_ref, taken_ref) = refs[:-3], refs[-3:]
    rows, tok = weights_ref.shape[0], taken_ref.shape[0]
    part = pieces[0].shape[0]
    for i, piece in enumerate(pieces):
        taken_ref[i * part : (i + 1) * part] = piece[...]
    core, chip = core_and_chip()
    a, b = products(tokens_ref, taken_ref, weights_ref, chip)
    out_ref[:tok] = a
    out_ref[tok:] = b
    for block in range(turned_ref.shape[0] // rows):
        own = pl.multiple_of((2 * block + core) * rows, 128)
        spot = pl.ds(block * rows, rows)
        turned_ref[spot, :tok] = tokens_ref[0, :, pl.ds(own, rows)].T
        turned_ref[spot, tok:] = taken_ref[:, spot].T


def next_products(step, tokens_ref, taken_ref, weights_ref, sum_ref, out_ref):
    tok = taken_ref.shape[0]
    chips = taken_ref.shape[1] // weights_ref.shape[0]
    block = lax.rem(core_and_chip()[1] + chips - step, chips)
    a, b = products(tokens_ref, taken_ref, weights_ref, block)
    out_ref[:tok] = sum_ref[:tok] + a
    out_ref[tok:] = sum_ref[tok:] + b


def cotangent_of(latent, upstream):
    inverse_rms = lax.rsqrt(jnp.mean(latent * latent, axis=-1, keepdims=True) + 1e-06)
    normed = latent * inverse_rms
    return (
        inverse_rms * (upstream - normed * jnp.mean(upstream * normed, axis=-1, keepdims=True))
    ).astype(jnp.bfloat16)


def sent_gradients(mine_ref, other_ref, up_ref, other_up_ref, turned_ref, *outs):
    latent_ref, outs = outs[0], outs[1:]
    tok = up_ref.shape[0]
    latent_ref[:tok] = cotangent_of(
        mine_ref[:tok] + other_ref[tok:], up_ref[...].astype(jnp.float32)
    )
    latent_ref[tok:] = cotangent_of(
        mine_ref[tok:] + other_ref[:tok], other_up_ref[...].astype(jnp.float32)
    )
    chips = len(outs) // CHAINS + 1
    rows = turned_ref.shape[0] // chips
    for i, out_ref in enumerate(outs):
        block = lax.rem(core_and_chip()[1] + 1 + i // CHAINS, chips)
        offset, size = cuts(rows)[i % CHAINS]
        start = pl.multiple_of(block * rows + offset, 16)
        out_ref[...] = jnp.dot(
            turned_ref[pl.ds(start, size), :], latent_ref[...], preferred_element_type=jnp.float32
        ).astype(out_ref.dtype)


def kept_gradients(turned_ref, latent_ref, *outs):
    rows = sum(out_ref.shape[0] for out_ref in outs)
    for out_ref, (offset, size) in zip(outs, cuts(rows), strict=True):
        start = pl.multiple_of(core_and_chip()[1] * rows + offset, 16)
        out_ref[...] = jnp.dot(
            turned_ref[pl.ds(start, size), :], latent_ref[...], preferred_element_type=jnp.float32
        )


def apply_blocks(steps, modules_ref, weights_ref, moment_ref, *refs):
    blocks, rest = refs[: len(steps)], refs[-5:]
    out_weights, out_moment, new_weights, new_moment, sems = rest
    copies = []
    for i, (behind, start) in enumerate(steps):
        module = jnp.max(modules_ref[behind : behind + 1, :])
        rows = blocks[i].shape[0]
        tile = math.gcd(rows, 64)

        def work(t, _, i=i, start=start, module=module, tile=tile):
            here = pl.ds(pl.multiple_of(t * tile, tile), tile)
            spot = pl.ds(pl.multiple_of(start + t * tile, tile), tile)
            a, b = outer_update(
                weights_ref[module, spot],
                moment_ref[module, spot],
                blocks[i][here].astype(jnp.float32),
            )
            new_weights[i, here] = a
            new_moment[i, here] = b
            return 0

        lax.fori_loop(0, rows // tile, work, 0)
        here, spot = pl.ds(0, rows), pl.ds(start, rows)
        for k, (src, dst) in enumerate(((new_weights, out_weights), (new_moment, out_moment))):
            copy = pltpu.make_async_copy(src.at[i, here], dst.at[module, spot], sems.at[i, k])
            copy.start()
            copies.append(copy)
    for copy in copies:
        copy.wait()


def body(tokens, cotangent, module_table, module_weights, momentum):
    paths, shards = lax.axis_size("path"), lax.axis_size("fsdp")
    chips = shards // 2
    path_id = lax.axis_index("path")
    tok_rows, width = tokens.shape[1:]
    module_count, rows, features = module_weights.shape
    step_size = math.sqrt(width / (tok_rows * shards))
    table = module_table[:, 0]
    f32, bf16 = jnp.float32, jnp.bfloat16
    shape = jax.ShapeDtypeStruct
    dma = pltpu.SemaphoreType.DMA

    to_core = [(i, i ^ 1) for i in range(shards)]

    def to_chip(step):
        return [(i, (i + 2 * step) % shards) for i in range(shards)]

    own_weights = call(
        pick_rows, shape((rows, features), bf16), [SMEM, HBM], VMEM,
        (table, module_weights), [dma], limit=50,
    )
    lent_weights = [lax.ppermute(own_weights, "fsdp", to_chip(s)) for s in range(1, chips)]
    pieces = [shape((tok_rows // PIECES, chips * rows), bf16)] * PIECES
    given = call(
        pick_columns, pieces, [HBM, VMEM], [VMEM] * PIECES,
        (tokens, own_weights), [dma((PIECES, chips))],
    )
    taken = [lax.ppermute(g, "fsdp", to_core) for g in given]
    other_up = lax.ppermute(cotangent[0], "fsdp", to_core)
    partial, turned, taken = call(
        first_products,
        [
            shape((2 * tok_rows, features), f32),
            shape((chips * rows, 2 * tok_rows), bf16),
            shape((tok_rows, chips * rows), bf16),
        ],
        [VMEM] * (2 + PIECES), [VMEM] * 3, (tokens, own_weights, *taken),
    )
    modules = modules_on_ring(table, path_id)
    partial, modules = lax.optimization_barrier((partial, modules))
    for s in range(1, chips):
        partial = call(
            functools.partial(next_products, s), shape(partial.shape, f32),
            [VMEM] * 4, VMEM, (tokens, taken, lent_weights[s - 1], partial),
        )
    other = lax.ppermute(partial, "fsdp", to_core)
    chains = cuts(rows)
    parts = [(size, features) for _, size in chains]
    latent_cotangent, *sent = call(
        sent_gradients,
        [shape((2 * tok_rows, features), bf16)]
        + [shape(p, bf16) for p in parts] * (chips - 1),
        [VMEM] * 5, [VMEM] * (1 + CHAINS * (chips - 1)),
        (partial, other, cotangent[0], other_up, turned),
    )
    kept = call(
        kept_gradients, [shape(p, f32) for p in parts],
        [VMEM] * 2, [VMEM] * CHAINS, (turned, latent_cotangent),
    )
    held = []
    for c in range(CHAINS):
        total = kept[c]
        for s in range(1, chips):
            arrived = lax.ppermute(sent[(s - 1) * CHAINS + c], "fsdp", to_chip(s))
            total = total + arrived.astype(f32)
        held.append(total * step_size)

    if paths != module_count:
        module = lax.dynamic_index_in_dim(table, path_id, 0, keepdims=False)
        module_ids = jnp.arange(module_count, dtype=jnp.int32)
        picked = (module_ids == module).astype(f32)
        counts = jnp.sum((table[:, None] == module_ids[None, :]).astype(f32), axis=0)
        summed = lax.psum(picked[:, None, None] * jnp.concatenate(held)[None], "path")
        return outer_update(module_weights, momentum, summed / counts[:, None, None])

    pairs = ring_pairs(paths)
    outs = []

    def apply(group, outs):
        steps = [(behind, start) for behind, start, _ in group]
        blocks = [block for _, _, block in group]
        most = (len(group), max(block.shape[0] for block in blocks), features)
        return call(
            functools.partial(apply_blocks, steps),
            [shape(module_weights.shape, bf16), shape(momentum.shape, f32)],
            [VMEM] * (3 + len(blocks)) + [HBM] * len(outs), [HBM] * 2,
            (modules, module_weights, momentum, *blocks, *outs),
            [pltpu.VMEM(most, bf16), pltpu.VMEM(most, f32), dma((len(blocks), 2))],
            limit=16,
            traffic=8 * sum(block.size for block in blocks),
            aliases={3 + len(blocks) + i: i for i in range(len(outs))},
        )

    held = [h.astype(bf16) for h in held]
    group = [(0, chains[c][0], h) for c, h in enumerate(held)]
    moving = [[h, h] for h in held]
    waiting = [[(0, start, h)] for (start, _), h in zip(chains, held)]
    for step in range(1, paths // 2 + 1):
        last = 2 * step == paths
        for c, (start, size) in enumerate(chains):
            pair, starts = moving[c], [start, start]
            if last:
                pair = [pair[0][: size // 2], pair[1][size // 2 :]]
                starts = [start, start + size // 2]
            if step > 2 and c == 0:
                pair, outs = lax.optimization_barrier((pair, outs))
            else:
                pair = lax.optimization_barrier(tuple(pair))
            moving[c] = [lax.ppermute(b, "path", pairs[way]) for b, way in zip(pair, (1, -1))]
            if step > 1 and c == 0:
                outs = apply([one for group in waiting for one in group], outs)
                waiting = [[] for _ in chains]
            waiting[c] += [
                ((way * step) % paths, first, b)
                for b, first, way in zip(moving[c], starts, (1, -1))
            ]
    for group in waiting:
        outs = apply(group, outs)
    return tuple(outs)


def solution(mesh):
    return jax.shard_map(
        body,
        mesh=mesh,
        in_specs=(
            P("path", "fsdp", None),
            P("path", "fsdp", None),
            P(),
            P(None, "fsdp", None),
            P(None, "fsdp", None),
        ),
        out_specs=(P(None, "fsdp", None), P(None, "fsdp", None)),
        check_vma=False,
    )
```

time: 89.6 us -> 76.5 us (0.85)
  waiting for transfers between devices: 43 us -> 32.4 us
  starting transfers between devices: 31.2 us -> 23.1 us
  Pallas kernels: 11.2 us -> 17.3 us
  local copies, waits for them, and re-layouts: 3.02 us -> 0.93 us
  other arithmetic: 0.22 us -> 1.75 us
    ppermute x15 -> x20, starting transfers between devices: 25.9 us -> 17.5 us  [the longest x16 16.4 us: body(): lax.ppermute(b, 'path', pairs[way])]
    pallas_call x7 -> x11, Pallas kernels: 11.2 us -> 17.3 us  [call(): pl.pallas_call(kernel, in_specs=in_specs, out_specs=out_specs, out_shape=...]
    ppermute x1, waiting for transfers between devices: 11.3 us -> 5.59 us  [body(): lax.ppermute(own_weights, 'fsdp', to_chip(s))]
    ppermute x15 -> x20, waiting for transfers between devices: 21.1 us -> 15.9 us  [the longest x16 15.5 us: body(): lax.ppermute(b, 'path', pairs[way])]
    unnamed x18 -> x16, local copies, waits for them, and re-layouts: 3.02 us -> 0.83 us
    reduce_sum x0 -> x2, other arithmetic: none -> 1.42 us  [the longest x1 0.73 us: modules_on_ring(): on_ring = jnp.sum(jnp.where(there, order, 0), axis=-1, keepdims=True)[:, 0]]
  transfers between devices with their start and end apart: 20 -> 25, of which waited for: 17 -> 15; matrix products, arithmetic and copies ran while one was open for 0% -> 2% of each run, Pallas kernels for 2% -> 17%
where the time goes in v3:
time: 76.5 us; the launch traced here: 76.3 us
  waiting for transfers between devices  32.4 us (42%)
  starting transfers between devices  23.1 us (30%)
  Pallas kernels  17.3 us (23%)
  other arithmetic  1.75 us (2%)
  local copies, waits for them, and re-layouts  0.93 us (1%)
  between operations  0.88 us (1%)
    pallas_call x11, Pallas kernels, call(): pl.pallas_call(kernel, in_specs=in_specs, out_specs=out_specs, out_shape=...  17.3 us
    ppermute x16, starting transfers between devices, body(): lax.ppermute(b, 'path', pairs[way])  16.4 us
    ppermute x16, waiting for transfers between devices, body(): lax.ppermute(b, 'path', pairs[way])  15.5 us
    ppermute x2, waiting for transfers between devices, body(): arrived = lax.ppermute(sent[(s - 1) * CHAINS + c], 'fsdp', to_chip(s))  9.34 us
    ppermute x1, waiting for transfers between devices, body(): lax.ppermute(own_weights, 'fsdp', to_chip(s))  5.59 us
    ppermute x1, starting transfers between devices, body(): lax.ppermute(own_weights, 'fsdp', to_chip(s))  3 us
    ppermute x2, starting transfers between devices, body(): arrived = lax.ppermute(sent[(s - 1) * CHAINS + c], 'fsdp', to_chip(s))  2.09 us
    ppermute x1, waiting for transfers between devices, body(): other_up = lax.ppermute(cotangent[0], 'fsdp', to_core)  1.58 us
  transfers between devices with their start and end apart: 25, of which 15 were waited for; matrix products, arithmetic and copies ran while one was open for 2% of the time, Pallas kernels for 17%

profile of v3, /device:TPU:0, one launch (start us, length us, event | category | flops | bytes accessed | tf_op | source)
XLA Modules:
  0.0 76.3 jit_solution(18030755829807944054)
XLA Ops:
  0.6 0.8 %copy-done.3 = s32[8,1]{0,1:T(1,128)S(1)} copy-done((s32[8,1]{0,1:T(1,128)S(1)}, s32[8,1]{0,1:T(1,128)}, u32[]{:S(2)}) %copy-start.3) | copy-done | bytes 56
  1.4 1.6 %pick_rows.1.after_ref.weights_ref = bf16[1024,256]{1,0:T(8,128)(2,1)S(1)} custom-call(s32[8]{0:T(128)S(1)} %bitcast.6, bf16[8,1024,256]{2,1,0:T(8,128)(2,1)} %weights_ref.11), custom_call_target="tpu_custom_call" | custom-call | tf_op jit(solution)/shard_map/pick_rows/pallas_call | solution.py:58
  3.1 3.0 %collective-permute-start.4 = (bf16[1024,256]{1,0:T(8,128)(2,1)S(1)}, bf16[1024,256]{1,0:T(8,128)(2,1)S(1)}, u32[]{:S(2)}, u32[]{:S(2)}) collective-permute-start(bf16[1024,256]{1,0:T(8,128)(2,1)S(1)} %pick_rows.1.after_ref.weights_ref), channel_id=1, source_target_pairs={{0,2},{1,3},{2,0},{3,1},{4,6},{5,7},{6,4},{7,5},{8,10},{9,11},{10,... | collective-permute-start | bytes 1572872 | tf_op jit(solution)/shard_map/ppermute | solution.py:232
  6.1 1.2 %pick_columns.1 = (bf16[64,2048]{1,0:T(8,128)(2,1)}, bf16[64,2048]{1,0:T(8,128)(2,1)}, bf16[64,2048]{1,0:T(8,128)(2,1)}, bf16[64,2048]{1,0:T(8,128)(2,1)}) custom-call(bf16[1,256,4096]{2,1,0:T(8,128)(2,1)S(1)} %copy-done.1, bf16[1024,256]{1,0:T(8,128)(2,1)S(1)} %pick_rows.1.after_ref.weights_ref), custom_call_target="tpu_custom_call" | custom-call | tf_op jit(solution)/shard_map/pick_columns/pallas_call | solution.py:58
  7.3 0.1 collective-permute-start
  7.4 0.5 collective-permute-start.1
  7.9 0.1 collective-permute-start.2
  7.9 0.4 collective-permute-start.3
  8.4 0.7 fusion.5
  9.1 0.7 select_reduce_fusion.1
  9.8 0.2 select_reduce_fusion
  10.0 0.0 collective-permute-done.1.refs_1_
  10.0 0.0 collective-permute-done.2.refs_2_
  10.0 0.3 collective-permute-done.3.refs_3_
  10.4 2.0 %first_products.1 = (f32[512,256]{1,0:T(8,128)S(1)}, bf16[2048,512]{1,0:T(8,128)(2,1)S(1)}, bf16[256,2048]{1,0:T(8,128)(2,1)S(1)}) custom-call(bf16[1,256,4096]{2,1,0:T(8,128)(2,1)S(1)} %copy-done.1, bf16[1024,256]{1,0:T(8,128)(2,1)S(1)} %pick_rows.1.after_ref.weights_ref, bf16[64,2048]{1,0:T(8,128)(2,1)S(1)} %collective-permute-done.refs_0_, ...), custom_call_target="tpu_custom_call" | custom-call | tf_op jit(solution)/shard_map/first_products/pallas_call | solution.py:58
  12.3 0.1 broadcast_in_dim.31.modules_ref
  12.4 5.6 %collective-permute-done.4.weights_ref = bf16[1024,256]{1,0:T(8,128)(2,1)S(1)} collective-permute-done((bf16[1024,256]{1,0:T(8,128)(2,1)S(1)}, bf16[1024,256]{1,0:T(8,128)(2,1)S(1)}, u32[]{:S(2)}, u32[]{:S(2)}) %collective-permute-start.4) | collective-permute-done | bytes 524320 | tf_op jit(solution)/shard_map/ppermute | solution.py:232
  18.0 0.4 next_products.1.mine_ref
  18.4 0.0 copy-start
  18.4 0.1 collective-permute-start.5
  18.5 0.5 collective-permute-start.6
  19.0 1.6 %collective-permute-done.6.other_up_ref = bf16[256,256]{1,0:T(8,128)(2,1)S(1)} collective-permute-done((bf16[256,256]{1,0:T(8,128)(2,1)S(1)}, bf16[256,256]{1,0:T(8,128)(2,1)S(1)}, u32[]{:S(2)}, u32[]{:S(2)}) %collective-permute-start.6) | collective-permute-done | bytes 131104 | tf_op jit(solution)/shard_map/ppermute | solution.py:239
  20.6 0.0 collective-permute-done.5.other_ref
  20.6 0.7 sent_gradients.1
  21.3 1.8 %collective-permute-start.16 = (bf16[512,256]{1,0:T(8,128)(2,1)S(1)}, bf16[512,256]{1,0:T(8,128)(2,1)S(1)}, u32[]{:S(2)}, u32[]{:S(2)}) collective-permute-start(bf16[512,256]{1,0:T(8,128)(2,1)S(1)} %get-tuple-element.65), channel_id=1, source_target_pairs={{0,2},{1,3},{2,0},{3,1},{4,6},{5,7},{6,4},{7,5},{8,10},{9,11},{10,... | collective-permute-start | bytes 786440 | tf_op jit(solution)/shard_map/ppermute | solution.py:274
  23.1 0.3 collective-permute-start.7
  23.4 0.4 kept_gradients.1
  23.8 6.7 %collective-permute-done.16 = bf16[512,256]{1,0:T(8,128)(2,1)S(1)} collective-permute-done((bf16[512,256]{1,0:T(8,128)(2,1)S(1)}, bf16[512,256]{1,0:T(8,128)(2,1)S(1)}, u32[]{:S(2)}, u32[]{:S(2)}) %collective-permute-start.16) | collective-permute-done | bytes 262176 | tf_op jit(solution)/shard_map/ppermute | solution.py:274
  30.5 0.1 multiply_convert_fusion.refs_0_
  30.6 1.9 %collective-permute-start.17 = (bf16[512,256]{1,0:T(8,128)(2,1)S(1)}, bf16[512,256]{1,0:T(8,128)(2,1)S(1)}, u32[]{:S(2)}, u32[]{:S(2)}) collective-permute-start(bf16[512,256]{1,0:T(8,128)(2,1)S(1)} %multiply_convert_fusion.refs_0_), channel_id=1, source_target_pairs={{0,8},{4,0},{8,16},{12,4},{16,24},{20,12},{24,28},{28,20},{1,9},{5... | collective-permute-start | bytes 786440 | tf_op jit(solution)/shard_map/ppermute | solution.py:319
  32.4 0.2 collective-permute-start.18
  32.6 2.7 %collective-permute-done.7 = bf16[512,256]{1,0:T(8,128)(2,1)S(1)} collective-permute-done((bf16[512,256]{1,0:T(8,128)(2,1)S(1)}, bf16[512,256]{1,0:T(8,128)(2,1)S(1)}, u32[]{:S(2)}, u32[]{:S(2)}) %collective-permute-start.7) | collective-permute-done | bytes 262176 | tf_op jit(solution)/shard_map/ppermute | solution.py:274
  35.3 0.1 multiply_convert_fusion.1.refs_3_
  35.4 1.9 %collective-permute-start.8 = (bf16[512,256]{1,0:T(8,128)(2,1)S(1)}, bf16[512,256]{1,0:T(8,128)(2,1)S(1)}, u32[]{:S(2)}, u32[]{:S(2)}) collective-permute-start(bf16[512,256]{1,0:T(8,128)(2,1)S(1)} %multiply_convert_fusion.1.refs_3_), channel_id=1, source_target_pairs={{0,8},{4,0},{8,16},{12,4},{16,24},{20,12},{24,28},{28,20},{1,9},{5... | collective-permute-start | bytes 786440 | tf_op jit(solution)/shard_map/ppermute | solution.py:319
  37.3 0.2 collective-permute-start.9
  37.5 0.0 collective-permute-done.17.refs_1_
  37.5 1.4 %collective-permute-done.18.refs_2_ = bf16[512,256]{1,0:T(8,128)(2,1)S(1)} collective-permute-done((bf16[512,256]{1,0:T(8,128)(2,1)S(1)}, bf16[512,256]{1,0:T(8,128)(2,1)S(1)}, u32[]{:S(2)}, u32[]{:S(2)}) %collective-permute-start.18) | collective-permute-done | bytes 262176 | tf_op jit(solution)/shard_map/ppermute | solution.py:319
  38.9 1.6 %collective-permute-start.19 = (bf16[512,256]{1,0:T(8,128)(2,1)S(1)}, bf16[512,256]{1,0:T(8,128)(2,1)S(1)}, u32[]{:S(2)}, u32[]{:S(2)}) collective-permute-start(bf16[512,256]{1,0:T(8,128)(2,1)S(1)} %collective-permute-done.17.refs_1_), channel_id=1, source_target_pairs={{0,8},{4,0},{8,16},{12,4},{16,24},{20,12},{24,28},{28,20},{1,9},{5... | collective-permute-start | bytes 786440 | tf_op jit(solution)/shard_map/ppermute | solution.py:319
  40.5 0.4 collective-permute-start.20
  40.9 3.8 %collective-permute-done.8.refs_4_ = bf16[512,256]{1,0:T(8,128)(2,1)S(1)} collective-permute-done((bf16[512,256]{1,0:T(8,128)(2,1)S(1)}, bf16[512,256]{1,0:T(8,128)(2,1)S(1)}, u32[]{:S(2)}, u32[]{:S(2)}) %collective-permute-start.8) | collective-permute-done | bytes 262176 | tf_op jit(solution)/shard_map/ppermute | solution.py:319
  44.7 1.8 %collective-permute-done.9.refs_5_ = bf16[512,256]{1,0:T(8,128)(2,1)S(1)} collective-permute-done((bf16[512,256]{1,0:T(8,128)(2,1)S(1)}, bf16[512,256]{1,0:T(8,128)(2,1)S(1)}, u32[]{:S(2)}, u32[]{:S(2)}) %collective-permute-start.9) | collective-permute-done | bytes 262176 | tf_op jit(solution)/shard_map/ppermute | solution.py:319
  46.5 1.6 %collective-permute-start.10 = (bf16[512,256]{1,0:T(8,128)(2,1)S(1)}, bf16[512,256]{1,0:T(8,128)(2,1)S(1)}, u32[]{:S(2)}, u32[]{:S(2)}) collective-permute-start(bf16[512,256]{1,0:T(8,128)(2,1)S(1)} %collective-permute-done.8.refs_4_), channel_id=1, source_target_pairs={{0,8},{4,0},{8,16},{12,4},{16,24},{20,12},{24,28},{28,20},{1,9},{5... | collective-permute-start | bytes 786440 | tf_op jit(solution)/shard_map/ppermute | solution.py:319
  48.1 0.4 collective-permute-start.11
  48.5 3.3 %apply_blocks.5 = (bf16[8,1024,256]{2,1,0:T(8,128)(2,1)}, f32[8,1024,256]{2,1,0:T(8,128)}) custom-call(s32[8,128]{1,0:T(8,128)S(1)} %broadcast_in_dim.31.modules_ref, bf16[8,1024,256]{2,1,0:T(8,128)(2,1)S(1)} %copy-done, f32[8,1024,256]{2,1,0:T(8,128)S(1)} %bitcast.3, bf16[512,256]{1,0:T(8,128)(2,1)S(1)} %multiply_convert_fusion.refs_0_, ...), custom_call_target="tpu_custom_call" | custom-call | bytes 6291456 | tf_op jit(solution)/shard_map/apply_blocks/pallas_call | solution.py:58
  51.8 0.0 collective-permute-done.19.refs_0_
  51.8 0.3 collective-permute-done.20.refs_1_
  52.1 1.6 %collective-permute-start.21 = (bf16[512,256]{1,0:T(8,128)(2,1)S(1)}, bf16[512,256]{1,0:T(8,128)(2,1)S(1)}, u32[]{:S(2)}, u32[]{:S(2)}) collective-permute-start(bf16[512,256]{1,0:T(8,128)(2,1)S(1)} %collective-permute-done.19.refs_0_), channel_id=1, source_target_pairs={{0,8},{4,0},{8,16},{12,4},{16,24},{20,12},{24,28},{28,20},{1,9},{5... | collective-permute-start | bytes 786440 | tf_op jit(solution)/shard_map/ppermute | solution.py:319
  53.7 0.4 collective-permute-start.22
  54.1 1.8 %collective-permute-done.10.refs_2_ = bf16[512,256]{1,0:T(8,128)(2,1)S(1)} collective-permute-done((bf16[512,256]{1,0:T(8,128)(2,1)S(1)}, bf16[512,256]{1,0:T(8,128)(2,1)S(1)}, u32[]{:S(2)}, u32[]{:S(2)}) %collective-permute-start.10) | collective-permute-done | bytes 262176 | tf_op jit(solution)/shard_map/ppermute | solution.py:319
  55.9 1.8 %collective-permute-done.11.refs_3_ = bf16[512,256]{1,0:T(8,128)(2,1)S(1)} collective-permute-done((bf16[512,256]{1,0:T(8,128)(2,1)S(1)}, bf16[512,256]{1,0:T(8,128)(2,1)S(1)}, u32[]{:S(2)}, u32[]{:S(2)}) %collective-permute-start.11) | collective-permute-done | bytes 262176 | tf_op jit(solution)/shard_map/ppermute | solution.py:319
  57.7 1.6 %collective-permute-start.12 = (bf16[512,256]{1,0:T(8,128)(2,1)S(1)}, bf16[512,256]{1,0:T(8,128)(2,1)S(1)}, u32[]{:S(2)}, u32[]{:S(2)}) collective-permute-start(bf16[512,256]{1,0:T(8,128)(2,1)S(1)} %collective-permute-done.10.refs_2_), channel_id=1, source_target_pairs={{0,8},{4,0},{8,16},{12,4},{16,24},{20,12},{24,28},{28,20},{1,9},{5... | collective-permute-start | bytes 786440 | tf_op jit(solution)/shard_map/ppermute | solution.py:319
  59.3 0.4 collective-permute-start.13
  59.8 2.5 %apply_blocks.6 = (bf16[8,1024,256]{2,1,0:T(8,128)(2,1)}, f32[8,1024,256]{2,1,0:T(8,128)}) custom-call(s32[8,128]{1,0:T(8,128)S(1)} %broadcast_in_dim.31.modules_ref, bf16[8,1024,256]{2,1,0:T(8,128)(2,1)S(1)} %copy-done, f32[8,1024,256]{2,1,0:T(8,128)S(1)} %bitcast.3, ...), custom_call_target="tpu_custom_call", output_to_operand_aliasing={{0}: (7, {}), {1}: (8, {})} | custom-call | bytes 4194304 | tf_op jit(solution)/shard_map/apply_blocks/pallas_call | solution.py:58
  62.3 1.1 %collective-permute-done.22.refs_1_ = bf16[512,256]{1,0:T(8,128)(2,1)S(1)} collective-permute-done((bf16[512,256]{1,0:T(8,128)(2,1)S(1)}, bf16[512,256]{1,0:T(8,128)(2,1)S(1)}, u32[]{:S(2)}, u32[]{:S(2)}) %collective-permute-start.22) | collective-permute-done | bytes 262176 | tf_op jit(solution)/shard_map/ppermute | solution.py:319
  63.4 1.6 %collective-permute-start.23 = (bf16[256,256]{1,0:T(8,128)(2,1)S(1)}, bf16[256,256]{1,0:T(8,128)(2,1)S(1)}, u32[]{:S(2)}, u32[]{:S(2)}) collective-permute-start(bf16[256,256]{1,0:T(8,128)(2,1)S(1)} %slice.18), channel_id=1, source_target_pairs={{0,8},{4,0},{8,16},{12,4},{16,24},{20,12},{24,28},{28,20},{1,9},{5... | collective-permute-start | bytes 393224 | tf_op jit(solution)/shard_map/ppermute | solution.py:319
  65.0 0.4 collective-permute-start.24
  65.4 1.4 %collective-permute-done.12.refs_2_ = bf16[512,256]{1,0:T(8,128)(2,1)S(1)} collective-permute-done((bf16[512,256]{1,0:T(8,128)(2,1)S(1)}, bf16[512,256]{1,0:T(8,128)(2,1)S(1)}, u32[]{:S(2)}, u32[]{:S(2)}) %collective-permute-start.12) | collective-permute-done | bytes 262176 | tf_op jit(solution)/shard_map/ppermute | solution.py:319
  66.9 1.5 %collective-permute-done.13.refs_3_ = bf16[512,256]{1,0:T(8,128)(2,1)S(1)} collective-permute-done((bf16[512,256]{1,0:T(8,128)(2,1)S(1)}, bf16[512,256]{1,0:T(8,128)(2,1)S(1)}, u32[]{:S(2)}, u32[]{:S(2)}) %collective-permute-start.13) | collective-permute-done | bytes 262176 | tf_op jit(solution)/shard_map/ppermute | solution.py:319
  68.4 1.6 %collective-permute-start.14 = (bf16[256,256]{1,0:T(8,128)(2,1)S(1)}, bf16[256,256]{1,0:T(8,128)(2,1)S(1)}, u32[]{:S(2)}, u32[]{:S(2)}) collective-permute-start(bf16[256,256]{1,0:T(8,128)(2,1)S(1)} %slice.16), channel_id=1, source_target_pairs={{0,8},{4,0},{8,16},{12,4},{16,24},{20,12},{24,28},{28,20},{1,9},{5... | collective-permute-start | bytes 393224 | tf_op jit(solution)/shard_map/ppermute | solution.py:319
  70.0 0.4 collective-permute-start.15
  70.5 2.5 %apply_blocks.7 = (bf16[8,1024,256]{2,1,0:T(8,128)(2,1)}, f32[8,1024,256]{2,1,0:T(8,128)}) custom-call(s32[8,128]{1,0:T(8,128)S(1)} %broadcast_in_dim.31.modules_ref, bf16[8,1024,256]{2,1,0:T(8,128)(2,1)S(1)} %copy-done, f32[8,1024,256]{2,1,0:T(8,128)S(1)} %bitcast.3, ...), custom_call_target="tpu_custom_call", output_to_operand_aliasing={{0}: (7, {}), {1}: (8, {})} | custom-call | bytes 4194304 | tf_op jit(solution)/shard_map/apply_blocks/pallas_call | solution.py:58
  73.0 1.4 %apply_blocks.8 = (bf16[8,1024,256]{2,1,0:T(8,128)(2,1)}, f32[8,1024,256]{2,1,0:T(8,128)}) custom-call(s32[8,128]{1,0:T(8,128)S(1)} %broadcast_in_dim.31.modules_ref, bf16[8,1024,256]{2,1,0:T(8,128)(2,1)S(1)} %copy-done, f32[8,1024,256]{2,1,0:T(8,128)S(1)} %bitcast.3, ...), custom_call_target="tpu_custom_call", output_to_operand_aliasing={{0}: (5, {}), {1}: (6, {})} | custom-call | bytes 1048576 | tf_op jit(solution)/shard_map/apply_blocks/pallas_call | solution.py:58
  74.4 0.6 collective-permute-done.15.refs_1_
  75.0 1.4 %apply_blocks.9 = (bf16[8,1024,256]{2,1,0:T(8,128)(2,1)}, f32[8,1024,256]{2,1,0:T(8,128)}) custom-call(s32[8,128]{1,0:T(8,128)S(1)} %broadcast_in_dim.31.modules_ref, bf16[8,1024,256]{2,1,0:T(8,128)(2,1)S(1)} %copy-done, f32[8,1024,256]{2,1,0:T(8,128)S(1)} %bitcast.3, ...), custom_call_target="tpu_custom_call", output_to_operand_aliasing={{0}: (5, {}), {1}: (6, {})} | custom-call | bytes 1048576 | tf_op jit(solution)/shard_map/apply_blocks/pallas_call | solution.py:58
  (24 shorter events, 0.1 us)
Async XLA Ops:
  0.6 5.4 %copy-start.1 = (bf16[1,256,4096]{2,1,0:T(8,128)(2,1)S(1)}, bf16[1,256,4096]{2,1,0:T(8,128)(2,1)}, u32[]{:S(2)}) copy-start(bf16[1,256,4096]{2,1,0:T(8,128)(2,1)} %tokens_ref.5) | copy-start | bytes 6291460
  0.6 0.8 %copy-start.3 = (s32[8,1]{0,1:T(1,128)S(1)}, s32[8,1]{0,1:T(1,128)}, u32[]{:S(2)}) copy-start(s32[8,1]{0,1:T(1,128)} %param.8) | copy-start | bytes 100
  1.4 6.9 %copy-start.5 = (s32[8]{0:T(128)S(1)}, s32[8]{0:T(128)}, u32[]{:S(2)}) copy-start(s32[8]{0:T(128)} %constant.28.clone) | copy-start | bytes 100
  1.4 8.4 %copy-start.4 = (s32[8,1]{0,1:T(1,128)S(1)}, s32[8,1]{0,1:T(1,128)}, u32[]{:S(2)}) copy-start(s32[8,1]{0,1:T(1,128)} %param.8) | copy-start | bytes 100
  3.1 14.9 %collective-permute-start.4 = (bf16[1024,256]{1,0:T(8,128)(2,1)S(1)}, bf16[1024,256]{1,0:T(8,128)(2,1)S(1)}, u32[]{:S(2)}, u32[]{:S(2)}) collective-permute-start(bf16[1024,256]{1,0:T(8,128)(2,1)S(1)} %pick_rows.1.after_ref.weights_ref), channel_id=1, source_target_pairs={{0,2},{1,3},{2,0},{3,1},{4,6},{5,7},{6,4},{7,5},{8,10},{9,11},{10,... | collective-permute-start | bytes 1572872 | tf_op jit(solution)/shard_map/ppermute | solution.py:232
  7.3 2.7 %collective-permute-start = (bf16[64,2048]{1,0:T(8,128)(2,1)}, bf16[64,2048]{1,0:T(8,128)(2,1)S(1)}, u32[]{:S(2)}, u32[]{:S(2)}) collective-permute-start(bf16[64,2048]{1,0:T(8,128)(2,1)} %get-tuple-element.44), channel_id=1, source_target_pairs={{0,1},{1,0},{2,3},{3,2},{4,5},{5,4},{6,7},{7,6},{8,9},{9,8},{10,11... | collective-permute-start | bytes 786440 | tf_op jit(solution)/shard_map/ppermute | solution.py:238
  7.4 2.6 %collective-permute-start.1 = (bf16[64,2048]{1,0:T(8,128)(2,1)}, bf16[64,2048]{1,0:T(8,128)(2,1)}, u32[]{:S(2)}, u32[]{:S(2)}) collective-permute-start(bf16[64,2048]{1,0:T(8,128)(2,1)} %get-tuple-element.45), channel_id=1, source_target_pairs={{0,1},{1,0},{2,3},{3,2},{4,5},{5,4},{6,7},{7,6},{8,9},{9,8},{10,11... | collective-permute-start | bytes 786440 | tf_op jit(solution)/shard_map/ppermute | solution.py:238
  7.9 2.2 %collective-permute-start.2 = (bf16[64,2048]{1,0:T(8,128)(2,1)}, bf16[64,2048]{1,0:T(8,128)(2,1)}, u32[]{:S(2)}, u32[]{:S(2)}) collective-permute-start(bf16[64,2048]{1,0:T(8,128)(2,1)} %get-tuple-element.46), channel_id=1, source_target_pairs={{0,1},{1,0},{2,3},{3,2},{4,5},{5,4},{6,7},{7,6},{8,9},{9,8},{10,11... | collective-permute-start | bytes 786440 | tf_op jit(solution)/shard_map/ppermute | solution.py:238
  7.9 2.4 %collective-permute-start.3 = (bf16[64,2048]{1,0:T(8,128)(2,1)}, bf16[64,2048]{1,0:T(8,128)(2,1)}, u32[]{:S(2)}, u32[]{:S(2)}) collective-permute-start(bf16[64,2048]{1,0:T(8,128)(2,1)} %get-tuple-element.47), channel_id=1, source_target_pairs={{0,1},{1,0},{2,3},{3,2},{4,5},{5,4},{6,7},{7,6},{8,9},{9,8},{10,11... | collective-permute-start | bytes 786440 | tf_op jit(solution)/shard_map/ppermute | solution.py:238
  10.0 8.5 %copy-start.2 = (bf16[1,256,256]{2,1,0:T(8,128)(2,1)S(1)}, bf16[1,256,256]{2,1,0:T(8,128)(2,1)}, u32[]{:S(2)}) copy-start(bf16[1,256,256]{2,1,0:T(8,128)(2,1)} %param.7) | copy-start | bytes 393220
  10.4 38.2 %slice-start = ((s8[8388608]{0:T(1024)(128)(4,1)}), s8[4194304]{0:T(1024)(128)(4,1)S(1)}, s32[]{:S(2)}) async-start(s8[8388608]{0:T(1024)(128)(4,1)} %bitcast.2), calls=%async_computation | async-start | bytes 8388608
  18.0 30.5 %slice-start.1 = ((s8[8388608]{0:T(1024)(128)(4,1)}), s8[4194304]{0:T(1024)(128)(4,1)S(1)}, s32[]{:S(2)}) async-start(s8[8388608]{0:T(1024)(128)(4,1)} %bitcast.2), calls=%async_computation.1 | async-start | bytes 8388608
  18.4 30.1 %copy-start = (bf16[8,1024,256]{2,1,0:T(8,128)(2,1)S(1)}, bf16[8,1024,256]{2,1,0:T(8,128)(2,1)}, u32[]{:S(2)}) copy-start(bf16[8,1024,256]{2,1,0:T(8,128)(2,1)} %weights_ref.11) | copy-start | bytes 12582916
  18.4 2.2 %collective-permute-start.5 = (f32[512,256]{1,0:T(8,128)S(1)}, f32[512,256]{1,0:T(8,128)S(1)}, u32[]{:S(2)}, u32[]{:S(2)}) collective-permute-start(f32[512,256]{1,0:T(8,128)S(1)} %next_products.1.mine_ref), channel_id=1, source_target_pairs={{0,1},{1,0},{2,3},{3,2},{4,5},{5,4},{6,7},{7,6},{8,9},{9,8},{10,11... | collective-permute-start | bytes 1572872 | tf_op jit(solution)/shard_map/ppermute | solution.py:256
  18.5 2.1 %collective-permute-start.6 = (bf16[256,256]{1,0:T(8,128)(2,1)S(1)}, bf16[256,256]{1,0:T(8,128)(2,1)S(1)}, u32[]{:S(2)}, u32[]{:S(2)}) collective-permute-start(bf16[256,256]{1,0:T(8,128)(2,1)S(1)} %bitcast.4), channel_id=1, source_target_pairs={{0,1},{1,0},{2,3},{3,2},{4,5},{5,4},{6,7},{7,6},{8,9},{9,8},{10,11... | collective-permute-start | bytes 393224 | tf_op jit(solution)/shard_map/ppermute | solution.py:239
  21.3 9.2 %collective-permute-start.16 = (bf16[512,256]{1,0:T(8,128)(2,1)S(1)}, bf16[512,256]{1,0:T(8,128)(2,1)S(1)}, u32[]{:S(2)}, u32[]{:S(2)}) collective-permute-start(bf16[512,256]{1,0:T(8,128)(2,1)S(1)} %get-tuple-element.65), channel_id=1, source_target_pairs={{0,2},{1,3},{2,0},{3,1},{4,6},{5,7},{6,4},{7,5},{8,10},{9,11},{10,... | collective-permute-start | bytes 786440 | tf_op jit(solution)/shard_map/ppermute | solution.py:274
  23.1 12.2 %collective-permute-start.7 = (bf16[512,256]{1,0:T(8,128)(2,1)S(1)}, bf16[512,256]{1,0:T(8,128)(2,1)S(1)}, u32[]{:S(2)}, u32[]{:S(2)}) collective-permute-start(bf16[512,256]{1,0:T(8,128)(2,1)S(1)} %get-tuple-element.55), channel_id=1, source_target_pairs={{0,2},{1,3},{2,0},{3,1},{4,6},{5,7},{6,4},{7,5},{8,10},{9,11},{10,... | collective-permute-start | bytes 786440 | tf_op jit(solution)/shard_map/ppermute | solution.py:274
  30.6 6.9 %collective-permute-start.17 = (bf16[512,256]{1,0:T(8,128)(2,1)S(1)}, bf16[512,256]{1,0:T(8,128)(2,1)S(1)}, u32[]{:S(2)}, u32[]{:S(2)}) collective-permute-start(bf16[512,256]{1,0:T(8,128)(2,1)S(1)} %multiply_convert_fusion.refs_0_), channel_id=1, source_target_pairs={{0,8},{4,0},{8,16},{12,4},{16,24},{20,12},{24,28},{28,20},{1,9},{5... | collective-permute-start | bytes 786440 | tf_op jit(solution)/shard_map/ppermute | solution.py:319
  32.4 6.4 %collective-permute-start.18 = (bf16[512,256]{1,0:T(8,128)(2,1)S(1)}, bf16[512,256]{1,0:T(8,128)(2,1)S(1)}, u32[]{:S(2)}, u32[]{:S(2)}) collective-permute-start(bf16[512,256]{1,0:T(8,128)(2,1)S(1)} %multiply_convert_fusion.refs_0_), channel_id=1, source_target_pairs={{0,4},{4,12},{8,0},{12,20},{16,8},{20,28},{24,16},{28,24},{1,5},{5... | collective-permute-start | bytes 786440 | tf_op jit(solution)/shard_map/ppermute | solution.py:319
  35.4 9.3 %collective-permute-start.8 = (bf16[512,256]{1,0:T(8,128)(2,1)S(1)}, bf16[512,256]{1,0:T(8,128)(2,1)S(1)}, u32[]{:S(2)}, u32[]{:S(2)}) collective-permute-start(bf16[512,256]{1,0:T(8,128)(2,1)S(1)} %multiply_convert_fusion.1.refs_3_), channel_id=1, source_target_pairs={{0,8},{4,0},{8,16},{12,4},{16,24},{20,12},{24,28},{28,20},{1,9},{5... | collective-permute-start | bytes 786440 | tf_op jit(solution)/shard_map/ppermute | solution.py:319
  37.3 9.2 %collective-permute-start.9 = (bf16[512,256]{1,0:T(8,128)(2,1)S(1)}, bf16[512,256]{1,0:T(8,128)(2,1)S(1)}, u32[]{:S(2)}, u32[]{:S(2)}) collective-permute-start(bf16[512,256]{1,0:T(8,128)(2,1)S(1)} %multiply_convert_fusion.1.refs_3_), channel_id=1, source_target_pairs={{0,4},{4,12},{8,0},{12,20},{16,8},{20,28},{24,16},{28,24},{1,5},{5... | collective-permute-start | bytes 786440 | tf_op jit(solution)/shard_map/ppermute | solution.py:319
  38.9 12.9 %collective-permute-start.19 = (bf16[512,256]{1,0:T(8,128)(2,1)S(1)}, bf16[512,256]{1,0:T(8,128)(2,1)S(1)}, u32[]{:S(2)}, u32[]{:S(2)}) collective-permute-start(bf16[512,256]{1,0:T(8,128)(2,1)S(1)} %collective-permute-done.17.refs_1_), channel_id=1, source_target_pairs={{0,8},{4,0},{8,16},{12,4},{16,24},{20,12},{24,28},{28,20},{1,9},{5... | collective-permute-start | bytes 786440 | tf_op jit(solution)/shard_map/ppermute | solution.py:319
  40.5 11.7 %collective-permute-start.20 = (bf16[512,256]{1,0:T(8,128)(2,1)S(1)}, bf16[512,256]{1,0:T(8,128)(2,1)S(1)}, u32[]{:S(2)}, u32[]{:S(2)}) collective-permute-start(bf16[512,256]{1,0:T(8,128)(2,1)S(1)} %collective-permute-done.18.refs_2_), channel_id=1, source_target_pairs={{0,4},{4,12},{8,0},{12,20},{16,8},{20,28},{24,16},{28,24},{1,5},{5... | collective-permute-start | bytes 786440 | tf_op jit(solution)/shard_map/ppermute | solution.py:319
  46.5 9.4 %collective-permute-start.10 = (bf16[512,256]{1,0:T(8,128)(2,1)S(1)}, bf16[512,256]{1,0:T(8,128)(2,1)S(1)}, u32[]{:S(2)}, u32[]{:S(2)}) collective-permute-start(bf16[512,256]{1,0:T(8,128)(2,1)S(1)} %collective-permute-done.8.refs_4_), channel_id=1, source_target_pairs={{0,8},{4,0},{8,16},{12,4},{16,24},{20,12},{24,28},{28,20},{1,9},{5... | collective-permute-start | bytes 786440 | tf_op jit(solution)/shard_map/ppermute | solution.py:319
  48.1 9.7 %collective-permute-start.11 = (bf16[512,256]{1,0:T(8,128)(2,1)S(1)}, bf16[512,256]{1,0:T(8,128)(2,1)S(1)}, u32[]{:S(2)}, u32[]{:S(2)}) collective-permute-start(bf16[512,256]{1,0:T(8,128)(2,1)S(1)} %collective-permute-done.9.refs_5_), channel_id=1, source_target_pairs={{0,4},{4,12},{8,0},{12,20},{16,8},{20,28},{24,16},{28,24},{1,5},{5... | collective-permute-start | bytes 786440 | tf_op jit(solution)/shard_map/ppermute | solution.py:319
  52.1 10.1 %collective-permute-start.21 = (bf16[512,256]{1,0:T(8,128)(2,1)S(1)}, bf16[512,256]{1,0:T(8,128)(2,1)S(1)}, u32[]{:S(2)}, u32[]{:S(2)}) collective-permute-start(bf16[512,256]{1,0:T(8,128)(2,1)S(1)} %collective-permute-done.19.refs_0_), channel_id=1, source_target_pairs={{0,8},{4,0},{8,16},{12,4},{16,24},{20,12},{24,28},{28,20},{1,9},{5... | collective-permute-start | bytes 786440 | tf_op jit(solution)/shard_map/ppermute | solution.py:319
  53.7 9.7 %collective-permute-start.22 = (bf16[512,256]{1,0:T(8,128)(2,1)S(1)}, bf16[512,256]{1,0:T(8,128)(2,1)S(1)}, u32[]{:S(2)}, u32[]{:S(2)}) collective-permute-start(bf16[512,256]{1,0:T(8,128)(2,1)S(1)} %collective-permute-done.20.refs_1_), channel_id=1, source_target_pairs={{0,4},{4,12},{8,0},{12,20},{16,8},{20,28},{24,16},{28,24},{1,5},{5... | collective-permute-start | bytes 786440 | tf_op jit(solution)/shard_map/ppermute | solution.py:319
  57.7 9.1 %collective-permute-start.12 = (bf16[512,256]{1,0:T(8,128)(2,1)S(1)}, bf16[512,256]{1,0:T(8,128)(2,1)S(1)}, u32[]{:S(2)}, u32[]{:S(2)}) collective-permute-start(bf16[512,256]{1,0:T(8,128)(2,1)S(1)} %collective-permute-done.10.refs_2_), channel_id=1, source_target_pairs={{0,8},{4,0},{8,16},{12,4},{16,24},{20,12},{24,28},{28,20},{1,9},{5... | collective-permute-start | bytes 786440 | tf_op jit(solution)/shard_map/ppermute | solution.py:319
  59.3 9.1 %collective-permute-start.13 = (bf16[512,256]{1,0:T(8,128)(2,1)S(1)}, bf16[512,256]{1,0:T(8,128)(2,1)S(1)}, u32[]{:S(2)}, u32[]{:S(2)}) collective-permute-start(bf16[512,256]{1,0:T(8,128)(2,1)S(1)} %collective-permute-done.11.refs_3_), channel_id=1, source_target_pairs={{0,4},{4,12},{8,0},{12,20},{16,8},{20,28},{24,16},{28,24},{1,5},{5... | collective-permute-start | bytes 786440 | tf_op jit(solution)/shard_map/ppermute | solution.py:319
  63.4 9.6 %collective-permute-start.23 = (bf16[256,256]{1,0:T(8,128)(2,1)S(1)}, bf16[256,256]{1,0:T(8,128)(2,1)S(1)}, u32[]{:S(2)}, u32[]{:S(2)}) collective-permute-start(bf16[256,256]{1,0:T(8,128)(2,1)S(1)} %slice.18), channel_id=1, source_target_pairs={{0,8},{4,0},{8,16},{12,4},{16,24},{20,12},{24,28},{28,20},{1,9},{5... | collective-permute-start | bytes 393224 | tf_op jit(solution)/shard_map/ppermute | solution.py:319
  65.0 8.0 %collective-permute-start.24 = (bf16[256,256]{1,0:T(8,128)(2,1)S(1)}, bf16[256,256]{1,0:T(8,128)(2,1)S(1)}, u32[]{:S(2)}, u32[]{:S(2)}) collective-permute-start(bf16[256,256]{1,0:T(8,128)(2,1)S(1)} %slice.19), channel_id=1, source_target_pairs={{0,4},{4,12},{8,0},{12,20},{16,8},{20,28},{24,16},{28,24},{1,5},{5... | collective-permute-start | bytes 393224 | tf_op jit(solution)/shard_map/ppermute | solution.py:319
  68.4 6.0 %collective-permute-start.14 = (bf16[256,256]{1,0:T(8,128)(2,1)S(1)}, bf16[256,256]{1,0:T(8,128)(2,1)S(1)}, u32[]{:S(2)}, u32[]{:S(2)}) collective-permute-start(bf16[256,256]{1,0:T(8,128)(2,1)S(1)} %slice.16), channel_id=1, source_target_pairs={{0,8},{4,0},{8,16},{12,4},{16,24},{20,12},{24,28},{28,20},{1,9},{5... | collective-permute-start | bytes 393224 | tf_op jit(solution)/shard_map/ppermute | solution.py:319
  70.0 5.0 %collective-permute-start.15 = (bf16[256,256]{1,0:T(8,128)(2,1)S(1)}, bf16[256,256]{1,0:T(8,128)(2,1)S(1)}, u32[]{:S(2)}, u32[]{:S(2)}) collective-permute-start(bf16[256,256]{1,0:T(8,128)(2,1)S(1)} %slice.17), channel_id=1, source_target_pairs={{0,4},{4,12},{8,0},{12,20},{16,8},{20,28},{24,16},{28,24},{1,5},{5... | collective-permute-start | bytes 393224 | tf_op jit(solution)/shard_map/ppermute | solution.py:319

commit v4 on v3

--- a/solution.py
+++ b/solution.py
@@ -50,6 +50,10 @@
     share, more = divmod(rows // unit, CHAINS)
     sizes = [unit * (share + (c < more)) for c in range(CHAINS)]
     return [(sum(sizes[:c]), size) for c, size in enumerate(sizes)]
+
+
+def far_share(size):
+    return size // 2
 
 
 def call(
@@ -74,7 +78,9 @@
 
 
 def pick_rows(table_ref, weights_ref, out_ref, sem):
-    module = table_ref[lax.axis_index("path")]
+    table = table_ref[...]
+    here = lax.broadcasted_iota(jnp.int32, table.shape, 1) == lax.axis_index("path")
+    module = jnp.max(jnp.where(here, table, 0))
     copy = pltpu.make_async_copy(weights_ref.at[module], out_ref, sem)
     copy.start()
     copy.wait()
@@ -148,33 +154,35 @@
     ).astype(jnp.bfloat16)
 
 
-def sent_gradients(mine_ref, other_ref, up_ref, other_up_ref, turned_ref, *outs):
-    latent_ref, outs = outs[0], outs[1:]
+def part_gradient(ahead, part, turned_ref, latent_ref):
+    shards = lax.axis_size("fsdp")
+    rows = turned_ref.shape[0] // (shards // 2)
+    block = lax.rem(core_and_chip()[1] + ahead, shards // 2)
+    offset, size = cuts(rows)[part]
+    start = pl.multiple_of(block * rows + offset, 16)
+    return jnp.dot(
+        turned_ref[pl.ds(start, size), :], latent_ref[...], preferred_element_type=jnp.float32
+    )
+
+
+def first_gradients(
+    wanted, mine_ref, other_ref, up_ref, other_up_ref, turned_ref, latent_ref, *outs
+):
     tok = up_ref.shape[0]
     latent_ref[:tok] = cotangent_of(
-        mine_ref[:tok] + other_ref[tok:], up_ref[...].astype(jnp.float32)
+        mine_ref[:tok] + other_ref[tok:].astype(jnp.float32), up_ref[...].astype(jnp.float32)
     )
     latent_ref[tok:] = cotangent_of(
-        mine_ref[tok:] + other_ref[:tok], other_up_ref[...].astype(jnp.float32)
-    )
-    chips = len(outs) // CHAINS + 1
-    rows = turned_ref.shape[0] // chips
-    for i, out_ref in enumerate(outs):
-        block = lax.rem(core_and_chip()[1] + 1 + i // CHAINS, chips)
-        offset, size = cuts(rows)[i % CHAINS]
-        start = pl.multiple_of(block * rows + offset, 16)
-        out_ref[...] = jnp.dot(
-            turned_ref[pl.ds(start, size), :], latent_ref[...], preferred_element_type=jnp.float32
-        ).astype(out_ref.dtype)
-
-
-def kept_gradients(turned_ref, latent_ref, *outs):
-    rows = sum(out_ref.shape[0] for out_ref in outs)
-    for out_ref, (offset, size) in zip(outs, cuts(rows), strict=True):
-        start = pl.multiple_of(core_and_chip()[1] * rows + offset, 16)
-        out_ref[...] = jnp.dot(
-            turned_ref[pl.ds(start, size), :], latent_ref[...], preferred_element_type=jnp.float32
-        )
+        mine_ref[tok:] + other_ref[:tok].astype(jnp.float32),
+        other_up_ref[...].astype(jnp.float32),
+    )
+    for (ahead, part), out_ref in zip(wanted, outs, strict=True):
+        out_ref[...] = part_gradient(ahead, part, turned_ref, latent_ref).astype(out_ref.dtype)
+
+
+def more_gradients(wanted, turned_ref, latent_ref, *outs):
+    for (ahead, part), out_ref in zip(wanted, outs, strict=True):
+        out_ref[...] = part_gradient(ahead, part, turned_ref, latent_ref).astype(out_ref.dtype)
 
 
 def apply_blocks(steps, modules_ref, weights_ref, moment_ref, *refs):
@@ -226,8 +234,8 @@
         return [(i, (i + 2 * step) % shards) for i in range(shards)]
 
     own_weights = call(
-        pick_rows, shape((rows, features), bf16), [SMEM, HBM], VMEM,
-        (table, module_weights), [dma], limit=50,
+        pick_rows, shape((rows, features), bf16), [VMEM, HBM], VMEM,
+        (table[None], module_weights), [dma], limit=50,
     )
     lent_weights = [lax.ppermute(own_weights, "fsdp", to_chip(s)) for s in range(1, chips)]
     pieces = [shape((tok_rows // PIECES, chips * rows), bf16)] * PIECES
@@ -235,8 +243,8 @@
         pick_columns, pieces, [HBM, VMEM], [VMEM] * PIECES,
         (tokens, own_weights), [dma((PIECES, chips))],
     )
+    other_up = lax.ppermute(cotangent[0], "fsdp", to_core)
     taken = [lax.ppermute(g, "fsdp", to_core) for g in given]
-    other_up = lax.ppermute(cotangent[0], "fsdp", to_core)
     partial, turned, taken = call(
         first_products,
         [
@@ -247,32 +255,37 @@
         [VMEM] * (2 + PIECES), [VMEM] * 3, (tokens, own_weights, *taken),
     )
     modules = modules_on_ring(table, path_id)
-    partial, modules = lax.optimization_barrier((partial, modules))
+    partial, modules, other_up = lax.optimization_barrier((partial, modules, other_up))
     for s in range(1, chips):
         partial = call(
             functools.partial(next_products, s), shape(partial.shape, f32),
             [VMEM] * 4, VMEM, (tokens, taken, lent_weights[s - 1], partial),
         )
-    other = lax.ppermute(partial, "fsdp", to_core)
+    other = lax.ppermute(partial.astype(bf16), "fsdp", to_core)
     chains = cuts(rows)
-    parts = [(size, features) for _, size in chains]
-    latent_cotangent, *sent = call(
-        sent_gradients,
-        [shape((2 * tok_rows, features), bf16)]
-        + [shape(p, bf16) for p in parts] * (chips - 1),
-        [VMEM] * 5, [VMEM] * (1 + CHAINS * (chips - 1)),
+
+    def outputs(wanted):
+        return [shape((chains[c][1], features), bf16 if ahead else f32) for ahead, c in wanted]
+
+    first = [(ahead, 0) for ahead in range(1, chips)]
+    more = [(ahead, c) for c in range(1, CHAINS) for ahead in range(1, chips)]
+    more += [(0, c) for c in range(CHAINS)]
+    latent_cotangent, *early = call(
+        functools.partial(first_gradients, first),
+        [shape((2 * tok_rows, features), bf16)] + outputs(first),
+        [VMEM] * 5, [VMEM] * (1 + len(first)),
         (partial, other, cotangent[0], other_up, turned),
     )
-    kept = call(
-        kept_gradients, [shape(p, f32) for p in parts],
-        [VMEM] * 2, [VMEM] * CHAINS, (turned, latent_cotangent),
-    )
+    late = call(
+        functools.partial(more_gradients, more), outputs(more),
+        [VMEM] * 2, [VMEM] * len(more), (turned, latent_cotangent),
+    )
+    gradients = dict(zip(first + more, [*early, *late], strict=True))
     held = []
     for c in range(CHAINS):
-        total = kept[c]
+        total = gradients[0, c]
         for s in range(1, chips):
-            arrived = lax.ppermute(sent[(s - 1) * CHAINS + c], "fsdp", to_chip(s))
-            total = total + arrived.astype(f32)
+            total = total + lax.ppermute(gradients[s, c], "fsdp", to_chip(s)).astype(f32)
         held.append(total * step_size)
 
     if paths != module_count:
@@ -310,22 +323,25 @@
         for c, (start, size) in enumerate(chains):
             pair, starts = moving[c], [start, start]
             if last:
-                pair = [pair[0][: size // 2], pair[1][size // 2 :]]
-                starts = [start, start + size // 2]
+                first = far_share(size)
+                pair = [pair[0][:first], pair[1][first:]]
+                starts = [start, start + first]
             if step > 2 and c == 0:
                 pair, outs = lax.optimization_barrier((pair, outs))
             else:
                 pair = lax.optimization_barrier(tuple(pair))
             moving[c] = [lax.ppermute(b, "path", pairs[way]) for b, way in zip(pair, (1, -1))]
-            if step > 1 and c == 0:
+            if step > 1 and c == 0 and not last:
                 outs = apply([one for group in waiting for one in group], outs)
                 waiting = [[] for _ in chains]
             waiting[c] += [
                 ((way * step) % paths, first, b)
                 for b, first, way in zip(moving[c], starts, (1, -1))
             ]
-    for group in waiting:
-        outs = apply(group, outs)
+    final = waiting[-1][2:]
+    waiting[-1] = waiting[-1][:2]
+    outs = apply([one for group in waiting for one in group], outs)
+    outs = apply(final, outs)
     return tuple(outs)
 
 

time: 76.5 us -> 75.5 us (0.987)
  Pallas kernels: 17.3 us -> 16.2 us
    ppermute x1, waiting for transfers between devices: 1.58 us -> 0.01 us  [body(): other_up = lax.ppermute(cotangent[0], 'fsdp', to_core)]
    ppermute x3, waiting for transfers between devices: 9.35 us -> 10.7 us  [the longest x2 9.14 us: body(): lax.ppermute(gradients[s, c], 'fsdp', to_chip(s)).astype(f32)]
    pallas_call x11 -> x10, Pallas kernels: 17.3 us -> 16.2 us  [call(): pl.pallas_call(kernel, in_specs=in_specs, out_specs=out_specs, out_shape=...]
    ppermute x16, waiting for transfers between devices: 15.5 us -> 16.3 us  [body(): lax.ppermute(b, 'path', pairs[way])]
  transfers between devices with their start and end apart: 25 -> 25, of which waited for: 15 -> 16; matrix products, arithmetic and copies ran while one was open for 2% -> 3% of each run, Pallas kernels for 17% -> 17%
where the time goes in v4:
time: 75.5 us; the launch traced here: 75.4 us
  waiting for transfers between devices  32.6 us (43%)
  starting transfers between devices  22.9 us (30%)
  Pallas kernels  16.2 us (21%)
  other arithmetic  1.87 us (2%)
  local copies, waits for them, and re-layouts  0.94 us (1%)
  between operations  0.86 us (1%)
    ppermute x16, starting transfers between devices, body(): lax.ppermute(b, 'path', pairs[way])  16.4 us
    ppermute x16, waiting for transfers between devices, body(): lax.ppermute(b, 'path', pairs[way])  16.3 us
    pallas_call x10, Pallas kernels, call(): pl.pallas_call(kernel, in_specs=in_specs, out_specs=out_specs, out_shape=...  16.2 us
    ppermute x2, waiting for transfers between devices, body(): lax.ppermute(gradients[s, c], 'fsdp', to_chip(s)).astype(f32)  9.14 us
    ppermute x1, waiting for transfers between devices, body(): lax.ppermute(own_weights, 'fsdp', to_chip(s))  5.56 us
    ppermute x1, starting transfers between devices, body(): lax.ppermute(own_weights, 'fsdp', to_chip(s))  3 us
    ppermute x2, starting transfers between devices, body(): lax.ppermute(gradients[s, c], 'fsdp', to_chip(s)).astype(f32)  2.16 us
    ppermute x1, waiting for transfers between devices, body(): other = lax.ppermute(partial.astype(bf16), 'fsdp', to_core)  1.52 us
  transfers between devices with their start and end apart: 25, of which 16 were waited for; matrix products, arithmetic and copies ran while one was open for 3% of the time, Pallas kernels for 17%

profile of v4, /device:TPU:0, one launch (start us, length us, event | category | flops | bytes accessed | tf_op | source)
XLA Modules:
  0.0 75.4 jit_solution(9911843913370993314)
XLA Ops:
  0.7 0.8 %copy-done.3 = s32[8,1]{0,1:T(1,128)S(1)} copy-done((s32[8,1]{0,1:T(1,128)S(1)}, s32[8,1]{0,1:T(1,128)}, u32[]{:S(2)}) %copy-start.3) | copy-done | bytes 56
  1.5 1.2 %pick_rows.1.after_ref.weights_ref = bf16[1024,256]{1,0:T(8,128)(2,1)S(1)} custom-call(s32[1,8]{1,0:T(1,128)S(1)} %bitcast.7, bf16[8,1024,256]{2,1,0:T(8,128)(2,1)} %weights_ref.9), custom_call_target="tpu_custom_call" | custom-call | tf_op jit(solution)/shard_map/pick_rows/pallas_call | solution.py:62
  2.7 3.0 %collective-permute-start.5 = (bf16[1024,256]{1,0:T(8,128)(2,1)S(1)}, bf16[1024,256]{1,0:T(8,128)(2,1)S(1)}, u32[]{:S(2)}, u32[]{:S(2)}) collective-permute-start(bf16[1024,256]{1,0:T(8,128)(2,1)S(1)} %pick_rows.1.after_ref.weights_ref), channel_id=1, source_target_pairs={{0,2},{1,3},{2,0},{3,1},{4,6},{5,7},{6,4},{7,5},{8,10},{9,11},{10,... | collective-permute-start | bytes 1572872 | tf_op jit(solution)/shard_map/ppermute | solution.py:240
  5.7 1.2 %pick_columns.1 = (bf16[64,2048]{1,0:T(8,128)(2,1)}, bf16[64,2048]{1,0:T(8,128)(2,1)}, bf16[64,2048]{1,0:T(8,128)(2,1)}, bf16[64,2048]{1,0:T(8,128)(2,1)}) custom-call(bf16[1,256,4096]{2,1,0:T(8,128)(2,1)S(1)} %copy-done.1, bf16[1024,256]{1,0:T(8,128)(2,1)S(1)} %pick_rows.1.after_ref.weights_ref), custom_call_target="tpu_custom_call" | custom-call | tf_op jit(solution)/shard_map/pick_columns/pallas_call | solution.py:62
  6.9 0.1 collective-permute-start
  7.0 0.5 collective-permute-start.1
  7.5 0.1 collective-permute-start.2
  7.6 0.4 collective-permute-start.3
  8.0 0.7 fusion.5
  8.7 0.0 collective-permute-done.refs_0_
  8.8 0.1 collective-permute-start.4
  8.9 0.8 %select_reduce_fusion.1 = s32[8]{0:T(128)S(1)} fusion(s32[8]{0:T(128)S(1)} %copy-done.5, s32[]{:T(128)} %fusion.5), kind=kLoop, calls=%fused_computation.9 | loop fusion | flops 952 | bytes 68 | tf_op jit(solution)/shard_map/reduce_sum | solution.py:37
  9.7 0.2 select_reduce_fusion
  9.9 0.0 collective-permute-done.2.refs_2_
  9.9 0.1 collective-permute-done.3.refs_3_
  10.0 2.0 %first_products.1 = (f32[512,256]{1,0:T(8,128)S(1)}, bf16[2048,512]{1,0:T(8,128)(2,1)S(1)}, bf16[256,2048]{1,0:T(8,128)(2,1)S(1)}) custom-call(bf16[1,256,4096]{2,1,0:T(8,128)(2,1)S(1)} %copy-done.1, bf16[1024,256]{1,0:T(8,128)(2,1)S(1)} %pick_rows.1.after_ref.weights_ref, bf16[64,2048]{1,0:T(8,128)(2,1)S(1)} %collective-permute-done.refs_0_, ...), custom_call_target="tpu_custom_call" | custom-call | tf_op jit(solution)/shard_map/first_products/pallas_call | solution.py:62
  12.0 0.0 collective-permute-done.4.other_up_ref
  12.0 0.1 broadcast_in_dim.31.modules_ref
  12.1 5.6 %collective-permute-done.5.weights_ref = bf16[1024,256]{1,0:T(8,128)(2,1)S(1)} collective-permute-done((bf16[1024,256]{1,0:T(8,128)(2,1)S(1)}, bf16[1024,256]{1,0:T(8,128)(2,1)S(1)}, u32[]{:S(2)}, u32[]{:S(2)}) %collective-permute-start.5) | collective-permute-done | bytes 524320 | tf_op jit(solution)/shard_map/ppermute | solution.py:240
  17.6 0.4 next_products.1.mine_ref
  18.1 0.0 slice-start.1
  18.1 0.0 copy-start
  18.1 0.1 collective-permute-start.6
  18.2 1.5 %collective-permute-done.6.other_ref = bf16[512,256]{1,0:T(8,128)(2,1)S(1)} collective-permute-done((bf16[512,256]{1,0:T(8,128)(2,1)S(1)}, bf16[512,256]{1,0:T(8,128)(2,1)S(1)}, u32[]{:S(2)}, u32[]{:S(2)}) %collective-permute-start.6) | collective-permute-done | bytes 262176 | tf_op jit(solution)/shard_map/ppermute | solution.py:264
  19.8 0.5 first_gradients.1
  20.3 1.8 %collective-permute-start.16 = (bf16[512,256]{1,0:T(8,128)(2,1)S(1)}, bf16[512,256]{1,0:T(8,128)(2,1)S(1)}, u32[]{:S(2)}, u32[]{:S(2)}) collective-permute-start(bf16[512,256]{1,0:T(8,128)(2,1)S(1)} %get-tuple-element.65), channel_id=1, source_target_pairs={{0,2},{1,3},{2,0},{3,1},{4,6},{5,7},{6,4},{7,5},{8,10},{9,11},{10,... | collective-permute-start | bytes 786440 | tf_op jit(solution)/shard_map/ppermute | solution.py:288
  22.1 0.6 more_gradients.1
  22.7 0.4 collective-permute-start.7
  23.0 6.5 %collective-permute-done.16 = bf16[512,256]{1,0:T(8,128)(2,1)S(1)} collective-permute-done((bf16[512,256]{1,0:T(8,128)(2,1)S(1)}, bf16[512,256]{1,0:T(8,128)(2,1)S(1)}, u32[]{:S(2)}, u32[]{:S(2)}) %collective-permute-start.16) | collective-permute-done | bytes 262176 | tf_op jit(solution)/shard_map/ppermute | solution.py:288
  29.5 0.1 multiply_convert_fusion.refs_0_
  29.6 1.9 %collective-permute-start.17 = (bf16[512,256]{1,0:T(8,128)(2,1)S(1)}, bf16[512,256]{1,0:T(8,128)(2,1)S(1)}, u32[]{:S(2)}, u32[]{:S(2)}) collective-permute-start(bf16[512,256]{1,0:T(8,128)(2,1)S(1)} %multiply_convert_fusion.refs_0_), channel_id=1, source_target_pairs={{0,8},{4,0},{8,16},{12,4},{16,24},{20,12},{24,28},{28,20},{1,9},{5... | collective-permute-start | bytes 786440 | tf_op jit(solution)/shard_map/ppermute | solution.py:333
  31.5 0.2 collective-permute-start.18
  31.7 2.7 %collective-permute-done.7 = bf16[512,256]{1,0:T(8,128)(2,1)S(1)} collective-permute-done((bf16[512,256]{1,0:T(8,128)(2,1)S(1)}, bf16[512,256]{1,0:T(8,128)(2,1)S(1)}, u32[]{:S(2)}, u32[]{:S(2)}) %collective-permute-start.7) | collective-permute-done | bytes 262176 | tf_op jit(solution)/shard_map/ppermute | solution.py:288
  34.3 0.1 multiply_convert_fusion.1.refs_3_
  34.4 1.9 %collective-permute-start.8 = (bf16[512,256]{1,0:T(8,128)(2,1)S(1)}, bf16[512,256]{1,0:T(8,128)(2,1)S(1)}, u32[]{:S(2)}, u32[]{:S(2)}) collective-permute-start(bf16[512,256]{1,0:T(8,128)(2,1)S(1)} %multiply_convert_fusion.1.refs_3_), channel_id=1, source_target_pairs={{0,8},{4,0},{8,16},{12,4},{16,24},{20,12},{24,28},{28,20},{1,9},{5... | collective-permute-start | bytes 786440 | tf_op jit(solution)/shard_map/ppermute | solution.py:333
  36.3 0.2 collective-permute-start.9
  36.5 0.0 collective-permute-done.17.refs_1_
  36.5 1.4 %collective-permute-done.18.refs_2_ = bf16[512,256]{1,0:T(8,128)(2,1)S(1)} collective-permute-done((bf16[512,256]{1,0:T(8,128)(2,1)S(1)}, bf16[512,256]{1,0:T(8,128)(2,1)S(1)}, u32[]{:S(2)}, u32[]{:S(2)}) %collective-permute-start.18) | collective-permute-done | bytes 262176 | tf_op jit(solution)/shard_map/ppermute | solution.py:333
  37.9 1.6 %collective-permute-start.19 = (bf16[512,256]{1,0:T(8,128)(2,1)S(1)}, bf16[512,256]{1,0:T(8,128)(2,1)S(1)}, u32[]{:S(2)}, u32[]{:S(2)}) collective-permute-start(bf16[512,256]{1,0:T(8,128)(2,1)S(1)} %collective-permute-done.17.refs_1_), channel_id=1, source_target_pairs={{0,8},{4,0},{8,16},{12,4},{16,24},{20,12},{24,28},{28,20},{1,9},{5... | collective-permute-start | bytes 786440 | tf_op jit(solution)/shard_map/ppermute | solution.py:333
  39.5 0.4 collective-permute-start.20
  39.9 3.8 %collective-permute-done.8.refs_4_ = bf16[512,256]{1,0:T(8,128)(2,1)S(1)} collective-permute-done((bf16[512,256]{1,0:T(8,128)(2,1)S(1)}, bf16[512,256]{1,0:T(8,128)(2,1)S(1)}, u32[]{:S(2)}, u32[]{:S(2)}) %collective-permute-start.8) | collective-permute-done | bytes 262176 | tf_op jit(solution)/shard_map/ppermute | solution.py:333
  43.7 1.8 %collective-permute-done.9.refs_5_ = bf16[512,256]{1,0:T(8,128)(2,1)S(1)} collective-permute-done((bf16[512,256]{1,0:T(8,128)(2,1)S(1)}, bf16[512,256]{1,0:T(8,128)(2,1)S(1)}, u32[]{:S(2)}, u32[]{:S(2)}) %collective-permute-start.9) | collective-permute-done | bytes 262176 | tf_op jit(solution)/shard_map/ppermute | solution.py:333
  45.5 1.6 %collective-permute-start.10 = (bf16[512,256]{1,0:T(8,128)(2,1)S(1)}, bf16[512,256]{1,0:T(8,128)(2,1)S(1)}, u32[]{:S(2)}, u32[]{:S(2)}) collective-permute-start(bf16[512,256]{1,0:T(8,128)(2,1)S(1)} %collective-permute-done.8.refs_4_), channel_id=1, source_target_pairs={{0,8},{4,0},{8,16},{12,4},{16,24},{20,12},{24,28},{28,20},{1,9},{5... | collective-permute-start | bytes 786440 | tf_op jit(solution)/shard_map/ppermute | solution.py:333
  47.1 0.4 collective-permute-start.11
  47.6 3.3 %apply_blocks.4 = (bf16[8,1024,256]{2,1,0:T(8,128)(2,1)}, f32[8,1024,256]{2,1,0:T(8,128)}) custom-call(s32[8,128]{1,0:T(8,128)S(1)} %broadcast_in_dim.31.modules_ref, bf16[8,1024,256]{2,1,0:T(8,128)(2,1)S(1)} %copy-done, f32[8,1024,256]{2,1,0:T(8,128)S(1)} %bitcast.4, bf16[512,256]{1,0:T(8,128)(2,1)S(1)} %multiply_convert_fusion.refs_0_, ...), custom_call_target="tpu_custom_call" | custom-call | bytes 6291456 | tf_op jit(solution)/shard_map/apply_blocks/pallas_call | solution.py:62
  50.9 0.3 collective-permute-done.20.refs_1_
  51.1 1.6 %collective-permute-start.21 = (bf16[512,256]{1,0:T(8,128)(2,1)S(1)}, bf16[512,256]{1,0:T(8,128)(2,1)S(1)}, u32[]{:S(2)}, u32[]{:S(2)}) collective-permute-start(bf16[512,256]{1,0:T(8,128)(2,1)S(1)} %collective-permute-done.19.refs_0_), channel_id=1, source_target_pairs={{0,8},{4,0},{8,16},{12,4},{16,24},{20,12},{24,28},{28,20},{1,9},{5... | collective-permute-start | bytes 786440 | tf_op jit(solution)/shard_map/ppermute | solution.py:333
  52.7 0.4 collective-permute-start.22
  53.2 1.8 %collective-permute-done.10.refs_2_ = bf16[512,256]{1,0:T(8,128)(2,1)S(1)} collective-permute-done((bf16[512,256]{1,0:T(8,128)(2,1)S(1)}, bf16[512,256]{1,0:T(8,128)(2,1)S(1)}, u32[]{:S(2)}, u32[]{:S(2)}) %collective-permute-start.10) | collective-permute-done | bytes 262176 | tf_op jit(solution)/shard_map/ppermute | solution.py:333
  54.9 1.8 %collective-permute-done.11.refs_3_ = bf16[512,256]{1,0:T(8,128)(2,1)S(1)} collective-permute-done((bf16[512,256]{1,0:T(8,128)(2,1)S(1)}, bf16[512,256]{1,0:T(8,128)(2,1)S(1)}, u32[]{:S(2)}, u32[]{:S(2)}) %collective-permute-start.11) | collective-permute-done | bytes 262176 | tf_op jit(solution)/shard_map/ppermute | solution.py:333
  56.8 1.6 %collective-permute-start.12 = (bf16[512,256]{1,0:T(8,128)(2,1)S(1)}, bf16[512,256]{1,0:T(8,128)(2,1)S(1)}, u32[]{:S(2)}, u32[]{:S(2)}) collective-permute-start(bf16[512,256]{1,0:T(8,128)(2,1)S(1)} %collective-permute-done.10.refs_2_), channel_id=1, source_target_pairs={{0,8},{4,0},{8,16},{12,4},{16,24},{20,12},{24,28},{28,20},{1,9},{5... | collective-permute-start | bytes 786440 | tf_op jit(solution)/shard_map/ppermute | solution.py:333
  58.3 0.4 collective-permute-start.13
  58.8 2.5 %apply_blocks.5 = (bf16[8,1024,256]{2,1,0:T(8,128)(2,1)}, f32[8,1024,256]{2,1,0:T(8,128)}) custom-call(s32[8,128]{1,0:T(8,128)S(1)} %broadcast_in_dim.31.modules_ref, bf16[8,1024,256]{2,1,0:T(8,128)(2,1)S(1)} %copy-done, f32[8,1024,256]{2,1,0:T(8,128)S(1)} %bitcast.4, ...), custom_call_target="tpu_custom_call", output_to_operand_aliasing={{0}: (7, {}), {1}: (8, {})} | custom-call | bytes 4194304 | tf_op jit(solution)/shard_map/apply_blocks/pallas_call | solution.py:62
  61.3 1.1 %collective-permute-done.22.refs_1_ = bf16[512,256]{1,0:T(8,128)(2,1)S(1)} collective-permute-done((bf16[512,256]{1,0:T(8,128)(2,1)S(1)}, bf16[512,256]{1,0:T(8,128)(2,1)S(1)}, u32[]{:S(2)}, u32[]{:S(2)}) %collective-permute-start.22) | collective-permute-done | bytes 262176 | tf_op jit(solution)/shard_map/ppermute | solution.py:333
  62.4 1.6 %collective-permute-start.23 = (bf16[256,256]{1,0:T(8,128)(2,1)S(1)}, bf16[256,256]{1,0:T(8,128)(2,1)S(1)}, u32[]{:S(2)}, u32[]{:S(2)}) collective-permute-start(bf16[256,256]{1,0:T(8,128)(2,1)S(1)} %slice.18), channel_id=1, source_target_pairs={{0,8},{4,0},{8,16},{12,4},{16,24},{20,12},{24,28},{28,20},{1,9},{5... | collective-permute-start | bytes 393224 | tf_op jit(solution)/shard_map/ppermute | solution.py:333
  64.0 0.4 collective-permute-start.24
  64.5 1.4 %collective-permute-done.12.refs_4_ = bf16[512,256]{1,0:T(8,128)(2,1)S(1)} collective-permute-done((bf16[512,256]{1,0:T(8,128)(2,1)S(1)}, bf16[512,256]{1,0:T(8,128)(2,1)S(1)}, u32[]{:S(2)}, u32[]{:S(2)}) %collective-permute-start.12) | collective-permute-done | bytes 262176 | tf_op jit(solution)/shard_map/ppermute | solution.py:333
  65.9 1.5 %collective-permute-done.13.refs_5_ = bf16[512,256]{1,0:T(8,128)(2,1)S(1)} collective-permute-done((bf16[512,256]{1,0:T(8,128)(2,1)S(1)}, bf16[512,256]{1,0:T(8,128)(2,1)S(1)}, u32[]{:S(2)}, u32[]{:S(2)}) %collective-permute-start.13) | collective-permute-done | bytes 262176 | tf_op jit(solution)/shard_map/ppermute | solution.py:333
  67.4 1.6 %collective-permute-start.14 = (bf16[256,256]{1,0:T(8,128)(2,1)S(1)}, bf16[256,256]{1,0:T(8,128)(2,1)S(1)}, u32[]{:S(2)}, u32[]{:S(2)}) collective-permute-start(bf16[256,256]{1,0:T(8,128)(2,1)S(1)} %slice.16), channel_id=1, source_target_pairs={{0,8},{4,0},{8,16},{12,4},{16,24},{20,12},{24,28},{28,20},{1,9},{5... | collective-permute-start | bytes 393224 | tf_op jit(solution)/shard_map/ppermute | solution.py:333
  69.0 0.4 collective-permute-start.15
  69.5 0.5 collective-permute-done.24.refs_3_
  70.0 3.1 %apply_blocks.6 = (bf16[8,1024,256]{2,1,0:T(8,128)(2,1)}, f32[8,1024,256]{2,1,0:T(8,128)}) custom-call(s32[8,128]{1,0:T(8,128)S(1)} %broadcast_in_dim.31.modules_ref, bf16[8,1024,256]{2,1,0:T(8,128)(2,1)S(1)} %copy-done, f32[8,1024,256]{2,1,0:T(8,128)S(1)} %bitcast.4, ...), custom_call_target="tpu_custom_call", output_to_operand_aliasing={{0}: (9, {}), {1}: (10, {})} | custom-call | bytes 5242880 | tf_op jit(solution)/shard_map/apply_blocks/pallas_call | solution.py:62
  73.1 0.9 %collective-permute-done.15.refs_1_ = bf16[256,256]{1,0:T(8,128)(2,1)S(1)} collective-permute-done((bf16[256,256]{1,0:T(8,128)(2,1)S(1)}, bf16[256,256]{1,0:T(8,128)(2,1)S(1)}, u32[]{:S(2)}, u32[]{:S(2)}) %collective-permute-start.15) | collective-permute-done | bytes 131104 | tf_op jit(solution)/shard_map/ppermute | solution.py:333
  74.0 1.4 %apply_blocks.7 = (bf16[8,1024,256]{2,1,0:T(8,128)(2,1)}, f32[8,1024,256]{2,1,0:T(8,128)}) custom-call(s32[8,128]{1,0:T(8,128)S(1)} %broadcast_in_dim.31.modules_ref, bf16[8,1024,256]{2,1,0:T(8,128)(2,1)S(1)} %copy-done, f32[8,1024,256]{2,1,0:T(8,128)S(1)} %bitcast.4, ...), custom_call_target="tpu_custom_call", output_to_operand_aliasing={{0}: (5, {}), {1}: (6, {})} | custom-call | bytes 1048576 | tf_op jit(solution)/shard_map/apply_blocks/pallas_call | solution.py:62
  (24 shorter events, 0.1 us)
Async XLA Ops:
  0.6 5.1 %copy-start.1 = (bf16[1,256,4096]{2,1,0:T(8,128)(2,1)S(1)}, bf16[1,256,4096]{2,1,0:T(8,128)(2,1)}, u32[]{:S(2)}) copy-start(bf16[1,256,4096]{2,1,0:T(8,128)(2,1)} %tokens_ref.5) | copy-start | bytes 6291460
  0.6 8.1 %copy-start.2 = (bf16[1,256,256]{2,1,0:T(8,128)(2,1)S(1)}, bf16[1,256,256]{2,1,0:T(8,128)(2,1)}, u32[]{:S(2)}) copy-start(bf16[1,256,256]{2,1,0:T(8,128)(2,1)} %param.7) | copy-start | bytes 393220
  0.6 0.8 %copy-start.3 = (s32[8,1]{0,1:T(1,128)S(1)}, s32[8,1]{0,1:T(1,128)}, u32[]{:S(2)}) copy-start(s32[8,1]{0,1:T(1,128)} %param.8) | copy-start | bytes 100
  1.5 6.6 %copy-start.5 = (s32[8]{0:T(128)S(1)}, s32[8]{0:T(128)}, u32[]{:S(2)}) copy-start(s32[8]{0:T(128)} %constant.28.clone) | copy-start | bytes 100
  1.5 8.2 %copy-start.4 = (s32[8,1]{0,1:T(1,128)S(1)}, s32[8,1]{0,1:T(1,128)}, u32[]{:S(2)}) copy-start(s32[8,1]{0,1:T(1,128)} %param.8) | copy-start | bytes 100
  2.7 14.9 %collective-permute-start.5 = (bf16[1024,256]{1,0:T(8,128)(2,1)S(1)}, bf16[1024,256]{1,0:T(8,128)(2,1)S(1)}, u32[]{:S(2)}, u32[]{:S(2)}) collective-permute-start(bf16[1024,256]{1,0:T(8,128)(2,1)S(1)} %pick_rows.1.after_ref.weights_ref), channel_id=1, source_target_pairs={{0,2},{1,3},{2,0},{3,1},{4,6},{5,7},{6,4},{7,5},{8,10},{9,11},{10,... | collective-permute-start | bytes 1572872 | tf_op jit(solution)/shard_map/ppermute | solution.py:240
  6.9 1.8 %collective-permute-start = (bf16[64,2048]{1,0:T(8,128)(2,1)}, bf16[64,2048]{1,0:T(8,128)(2,1)S(1)}, u32[]{:S(2)}, u32[]{:S(2)}) collective-permute-start(bf16[64,2048]{1,0:T(8,128)(2,1)} %get-tuple-element.43), channel_id=1, source_target_pairs={{0,1},{1,0},{2,3},{3,2},{4,5},{5,4},{6,7},{7,6},{8,9},{9,8},{10,11... | collective-permute-start | bytes 786440 | tf_op jit(solution)/shard_map/ppermute | solution.py:247
  7.0 2.9 %collective-permute-start.1 = (bf16[64,2048]{1,0:T(8,128)(2,1)}, bf16[64,2048]{1,0:T(8,128)(2,1)}, u32[]{:S(2)}, u32[]{:S(2)}) collective-permute-start(bf16[64,2048]{1,0:T(8,128)(2,1)} %get-tuple-element.44), channel_id=1, source_target_pairs={{0,1},{1,0},{2,3},{3,2},{4,5},{5,4},{6,7},{7,6},{8,9},{9,8},{10,11... | collective-permute-start | bytes 786440 | tf_op jit(solution)/shard_map/ppermute | solution.py:247
  7.5 2.4 %collective-permute-start.2 = (bf16[64,2048]{1,0:T(8,128)(2,1)}, bf16[64,2048]{1,0:T(8,128)(2,1)}, u32[]{:S(2)}, u32[]{:S(2)}) collective-permute-start(bf16[64,2048]{1,0:T(8,128)(2,1)} %get-tuple-element.45), channel_id=1, source_target_pairs={{0,1},{1,0},{2,3},{3,2},{4,5},{5,4},{6,7},{7,6},{8,9},{9,8},{10,11... | collective-permute-start | bytes 786440 | tf_op jit(solution)/shard_map/ppermute | solution.py:247
  7.6 2.4 %collective-permute-start.3 = (bf16[64,2048]{1,0:T(8,128)(2,1)}, bf16[64,2048]{1,0:T(8,128)(2,1)}, u32[]{:S(2)}, u32[]{:S(2)}) collective-permute-start(bf16[64,2048]{1,0:T(8,128)(2,1)} %get-tuple-element.46), channel_id=1, source_target_pairs={{0,1},{1,0},{2,3},{3,2},{4,5},{5,4},{6,7},{7,6},{8,9},{9,8},{10,11... | collective-permute-start | bytes 786440 | tf_op jit(solution)/shard_map/ppermute | solution.py:247
  8.8 3.2 %collective-permute-start.4 = (bf16[256,256]{1,0:T(8,128)(2,1)S(1)}, bf16[256,256]{1,0:T(8,128)(2,1)S(1)}, u32[]{:S(2)}, u32[]{:S(2)}) collective-permute-start(bf16[256,256]{1,0:T(8,128)(2,1)S(1)} %bitcast.5), channel_id=1, source_target_pairs={{0,1},{1,0},{2,3},{3,2},{4,5},{5,4},{6,7},{7,6},{8,9},{9,8},{10,11... | collective-permute-start | bytes 393224 | tf_op jit(solution)/shard_map/ppermute | solution.py:246
  10.0 37.5 %slice-start = ((s8[8388608]{0:T(1024)(128)(4,1)}), s8[4194304]{0:T(1024)(128)(4,1)S(1)}, s32[]{:S(2)}) async-start(s8[8388608]{0:T(1024)(128)(4,1)} %bitcast.3), calls=%async_computation | async-start | bytes 8388608
  18.1 29.5 %slice-start.1 = ((s8[8388608]{0:T(1024)(128)(4,1)}), s8[4194304]{0:T(1024)(128)(4,1)S(1)}, s32[]{:S(2)}) async-start(s8[8388608]{0:T(1024)(128)(4,1)} %bitcast.3), calls=%async_computation.1 | async-start | bytes 8388608
  18.1 29.5 %copy-start = (bf16[8,1024,256]{2,1,0:T(8,128)(2,1)S(1)}, bf16[8,1024,256]{2,1,0:T(8,128)(2,1)}, u32[]{:S(2)}) copy-start(bf16[8,1024,256]{2,1,0:T(8,128)(2,1)} %weights_ref.9) | copy-start | bytes 12582916
  18.1 1.6 %collective-permute-start.6 = (bf16[512,256]{1,0:T(8,128)(2,1)S(1)}, bf16[512,256]{1,0:T(8,128)(2,1)S(1)}, u32[]{:S(2)}, u32[]{:S(2)}) collective-permute-start(bf16[512,256]{1,0:T(8,128)(2,1)S(1)} %convert_element_type.15), channel_id=1, source_target_pairs={{0,1},{1,0},{2,3},{3,2},{4,5},{5,4},{6,7},{7,6},{8,9},{9,8},{10,11... | collective-permute-start | bytes 786440 | tf_op jit(solution)/shard_map/ppermute | solution.py:264
  20.3 9.2 %collective-permute-start.16 = (bf16[512,256]{1,0:T(8,128)(2,1)S(1)}, bf16[512,256]{1,0:T(8,128)(2,1)S(1)}, u32[]{:S(2)}, u32[]{:S(2)}) collective-permute-start(bf16[512,256]{1,0:T(8,128)(2,1)S(1)} %get-tuple-element.65), channel_id=1, source_target_pairs={{0,2},{1,3},{2,0},{3,1},{4,6},{5,7},{6,4},{7,5},{8,10},{9,11},{10,... | collective-permute-start | bytes 786440 | tf_op jit(solution)/shard_map/ppermute | solution.py:288
  22.7 11.7 %collective-permute-start.7 = (bf16[512,256]{1,0:T(8,128)(2,1)S(1)}, bf16[512,256]{1,0:T(8,128)(2,1)S(1)}, u32[]{:S(2)}, u32[]{:S(2)}) collective-permute-start(bf16[512,256]{1,0:T(8,128)(2,1)S(1)} %get-tuple-element.55), channel_id=1, source_target_pairs={{0,2},{1,3},{2,0},{3,1},{4,6},{5,7},{6,4},{7,5},{8,10},{9,11},{10,... | collective-permute-start | bytes 786440 | tf_op jit(solution)/shard_map/ppermute | solution.py:288
  29.6 6.9 %collective-permute-start.17 = (bf16[512,256]{1,0:T(8,128)(2,1)S(1)}, bf16[512,256]{1,0:T(8,128)(2,1)S(1)}, u32[]{:S(2)}, u32[]{:S(2)}) collective-permute-start(bf16[512,256]{1,0:T(8,128)(2,1)S(1)} %multiply_convert_fusion.refs_0_), channel_id=1, source_target_pairs={{0,8},{4,0},{8,16},{12,4},{16,24},{20,12},{24,28},{28,20},{1,9},{5... | collective-permute-start | bytes 786440 | tf_op jit(solution)/shard_map/ppermute | solution.py:333
  31.5 6.4 %collective-permute-start.18 = (bf16[512,256]{1,0:T(8,128)(2,1)S(1)}, bf16[512,256]{1,0:T(8,128)(2,1)S(1)}, u32[]{:S(2)}, u32[]{:S(2)}) collective-permute-start(bf16[512,256]{1,0:T(8,128)(2,1)S(1)} %multiply_convert_fusion.refs_0_), channel_id=1, source_target_pairs={{0,4},{4,12},{8,0},{12,20},{16,8},{20,28},{24,16},{28,24},{1,5},{5... | collective-permute-start | bytes 786440 | tf_op jit(solution)/shard_map/ppermute | solution.py:333
  34.4 9.3 %collective-permute-start.8 = (bf16[512,256]{1,0:T(8,128)(2,1)S(1)}, bf16[512,256]{1,0:T(8,128)(2,1)S(1)}, u32[]{:S(2)}, u32[]{:S(2)}) collective-permute-start(bf16[512,256]{1,0:T(8,128)(2,1)S(1)} %multiply_convert_fusion.1.refs_3_), channel_id=1, source_target_pairs={{0,8},{4,0},{8,16},{12,4},{16,24},{20,12},{24,28},{28,20},{1,9},{5... | collective-permute-start | bytes 786440 | tf_op jit(solution)/shard_map/ppermute | solution.py:333
  36.3 9.2 %collective-permute-start.9 = (bf16[512,256]{1,0:T(8,128)(2,1)S(1)}, bf16[512,256]{1,0:T(8,128)(2,1)S(1)}, u32[]{:S(2)}, u32[]{:S(2)}) collective-permute-start(bf16[512,256]{1,0:T(8,128)(2,1)S(1)} %multiply_convert_fusion.1.refs_3_), channel_id=1, source_target_pairs={{0,4},{4,12},{8,0},{12,20},{16,8},{20,28},{24,16},{28,24},{1,5},{5... | collective-permute-start | bytes 786440 | tf_op jit(solution)/shard_map/ppermute | solution.py:333
  37.9 13.0 %collective-permute-start.19 = (bf16[512,256]{1,0:T(8,128)(2,1)S(1)}, bf16[512,256]{1,0:T(8,128)(2,1)S(1)}, u32[]{:S(2)}, u32[]{:S(2)}) collective-permute-start(bf16[512,256]{1,0:T(8,128)(2,1)S(1)} %collective-permute-done.17.refs_1_), channel_id=1, source_target_pairs={{0,8},{4,0},{8,16},{12,4},{16,24},{20,12},{24,28},{28,20},{1,9},{5... | collective-permute-start | bytes 786440 | tf_op jit(solution)/shard_map/ppermute | solution.py:333
  39.5 11.7 %collective-permute-start.20 = (bf16[512,256]{1,0:T(8,128)(2,1)S(1)}, bf16[512,256]{1,0:T(8,128)(2,1)S(1)}, u32[]{:S(2)}, u32[]{:S(2)}) collective-permute-start(bf16[512,256]{1,0:T(8,128)(2,1)S(1)} %collective-permute-done.18.refs_2_), channel_id=1, source_target_pairs={{0,4},{4,12},{8,0},{12,20},{16,8},{20,28},{24,16},{28,24},{1,5},{5... | collective-permute-start | bytes 786440 | tf_op jit(solution)/shard_map/ppermute | solution.py:333
  45.5 9.4 %collective-permute-start.10 = (bf16[512,256]{1,0:T(8,128)(2,1)S(1)}, bf16[512,256]{1,0:T(8,128)(2,1)S(1)}, u32[]{:S(2)}, u32[]{:S(2)}) collective-permute-start(bf16[512,256]{1,0:T(8,128)(2,1)S(1)} %collective-permute-done.8.refs_4_), channel_id=1, source_target_pairs={{0,8},{4,0},{8,16},{12,4},{16,24},{20,12},{24,28},{28,20},{1,9},{5... | collective-permute-start | bytes 786440 | tf_op jit(solution)/shard_map/ppermute | solution.py:333
  47.1 9.7 %collective-permute-start.11 = (bf16[512,256]{1,0:T(8,128)(2,1)S(1)}, bf16[512,256]{1,0:T(8,128)(2,1)S(1)}, u32[]{:S(2)}, u32[]{:S(2)}) collective-permute-start(bf16[512,256]{1,0:T(8,128)(2,1)S(1)} %collective-permute-done.9.refs_5_), channel_id=1, source_target_pairs={{0,4},{4,12},{8,0},{12,20},{16,8},{20,28},{24,16},{28,24},{1,5},{5... | collective-permute-start | bytes 786440 | tf_op jit(solution)/shard_map/ppermute | solution.py:333
  51.1 10.1 %collective-permute-start.21 = (bf16[512,256]{1,0:T(8,128)(2,1)S(1)}, bf16[512,256]{1,0:T(8,128)(2,1)S(1)}, u32[]{:S(2)}, u32[]{:S(2)}) collective-permute-start(bf16[512,256]{1,0:T(8,128)(2,1)S(1)} %collective-permute-done.19.refs_0_), channel_id=1, source_target_pairs={{0,8},{4,0},{8,16},{12,4},{16,24},{20,12},{24,28},{28,20},{1,9},{5... | collective-permute-start | bytes 786440 | tf_op jit(solution)/shard_map/ppermute | solution.py:333
  52.7 9.7 %collective-permute-start.22 = (bf16[512,256]{1,0:T(8,128)(2,1)S(1)}, bf16[512,256]{1,0:T(8,128)(2,1)S(1)}, u32[]{:S(2)}, u32[]{:S(2)}) collective-permute-start(bf16[512,256]{1,0:T(8,128)(2,1)S(1)} %collective-permute-done.20.refs_1_), channel_id=1, source_target_pairs={{0,4},{4,12},{8,0},{12,20},{16,8},{20,28},{24,16},{28,24},{1,5},{5... | collective-permute-start | bytes 786440 | tf_op jit(solution)/shard_map/ppermute | solution.py:333
  56.8 9.1 %collective-permute-start.12 = (bf16[512,256]{1,0:T(8,128)(2,1)S(1)}, bf16[512,256]{1,0:T(8,128)(2,1)S(1)}, u32[]{:S(2)}, u32[]{:S(2)}) collective-permute-start(bf16[512,256]{1,0:T(8,128)(2,1)S(1)} %collective-permute-done.10.refs_2_), channel_id=1, source_target_pairs={{0,8},{4,0},{8,16},{12,4},{16,24},{20,12},{24,28},{28,20},{1,9},{5... | collective-permute-start | bytes 786440 | tf_op jit(solution)/shard_map/ppermute | solution.py:333
  58.3 9.1 %collective-permute-start.13 = (bf16[512,256]{1,0:T(8,128)(2,1)S(1)}, bf16[512,256]{1,0:T(8,128)(2,1)S(1)}, u32[]{:S(2)}, u32[]{:S(2)}) collective-permute-start(bf16[512,256]{1,0:T(8,128)(2,1)S(1)} %collective-permute-done.11.refs_3_), channel_id=1, source_target_pairs={{0,4},{4,12},{8,0},{12,20},{16,8},{20,28},{24,16},{28,24},{1,5},{5... | collective-permute-start | bytes 786440 | tf_op jit(solution)/shard_map/ppermute | solution.py:333
  62.4 7.1 %collective-permute-start.23 = (bf16[256,256]{1,0:T(8,128)(2,1)S(1)}, bf16[256,256]{1,0:T(8,128)(2,1)S(1)}, u32[]{:S(2)}, u32[]{:S(2)}) collective-permute-start(bf16[256,256]{1,0:T(8,128)(2,1)S(1)} %slice.18), channel_id=1, source_target_pairs={{0,8},{4,0},{8,16},{12,4},{16,24},{20,12},{24,28},{28,20},{1,9},{5... | collective-permute-start | bytes 393224 | tf_op jit(solution)/shard_map/ppermute | solution.py:333
  64.0 6.0 %collective-permute-start.24 = (bf16[256,256]{1,0:T(8,128)(2,1)S(1)}, bf16[256,256]{1,0:T(8,128)(2,1)S(1)}, u32[]{:S(2)}, u32[]{:S(2)}) collective-permute-start(bf16[256,256]{1,0:T(8,128)(2,1)S(1)} %slice.19), channel_id=1, source_target_pairs={{0,4},{4,12},{8,0},{12,20},{16,8},{20,28},{24,16},{28,24},{1,5},{5... | collective-permute-start | bytes 393224 | tf_op jit(solution)/shard_map/ppermute | solution.py:333
  67.4 5.7 %collective-permute-start.14 = (bf16[256,256]{1,0:T(8,128)(2,1)S(1)}, bf16[256,256]{1,0:T(8,128)(2,1)S(1)}, u32[]{:S(2)}, u32[]{:S(2)}) collective-permute-start(bf16[256,256]{1,0:T(8,128)(2,1)S(1)} %slice.16), channel_id=1, source_target_pairs={{0,8},{4,0},{8,16},{12,4},{16,24},{20,12},{24,28},{28,20},{1,9},{5... | collective-permute-start | bytes 393224 | tf_op jit(solution)/shard_map/ppermute | solution.py:333
  69.0 5.0 %collective-permute-start.15 = (bf16[256,256]{1,0:T(8,128)(2,1)S(1)}, bf16[256,256]{1,0:T(8,128)(2,1)S(1)}, u32[]{:S(2)}, u32[]{:S(2)}) collective-permute-start(bf16[256,256]{1,0:T(8,128)(2,1)S(1)} %slice.17), channel_id=1, source_target_pairs={{0,4},{4,12},{8,0},{12,20},{16,8},{20,28},{24,16},{28,24},{1,5},{5... | collective-permute-start | bytes 393224 | tf_op jit(solution)/shard_map/ppermute | solution.py:333

commit v5 on v4

--- a/solution.py
+++ b/solution.py
@@ -328,7 +328,7 @@
                 starts = [start, start + first]
             if step > 2 and c == 0:
                 pair, outs = lax.optimization_barrier((pair, outs))
-            else:
+            elif not last:
                 pair = lax.optimization_barrier(tuple(pair))
             moving[c] = [lax.ppermute(b, "path", pairs[way]) for b, way in zip(pair, (1, -1))]
             if step > 1 and c == 0 and not last:
@@ -338,10 +338,10 @@
                 ((way * step) % paths, first, b)
                 for b, first, way in zip(moving[c], starts, (1, -1))
             ]
-    final = waiting[-1][2:]
-    waiting[-1] = waiting[-1][:2]
-    outs = apply([one for group in waiting for one in group], outs)
-    outs = apply(final, outs)
+    far = [group[-2:] for group in waiting]
+    outs = apply([one for group in waiting for one in group[:-2]], outs)
+    for group in far:
+        outs = apply(group, outs)
     return tuple(outs)
 
 

time: 75.5 us -> 74.6 us (0.988)
  waiting for transfers between devices: 32.6 us -> 31 us
    ppermute x16, waiting for transfers between devices: 16.3 us -> 14.5 us  [body(): lax.ppermute(b, 'path', pairs[way])]
    pallas_call x10 -> x11, Pallas kernels: 16.2 us -> 16.9 us  [call(): pl.pallas_call(kernel, in_specs=in_specs, out_specs=out_specs, out_shape=...]
  transfers between devices with their start and end apart: 25 -> 25, of which waited for: 16 -> 14; matrix products, arithmetic and copies ran while one was open for 3% -> 3% of each run, Pallas kernels for 17% -> 18%
where the time goes in v5:
time: 74.6 us; the launch traced here: 74.5 us
  waiting for transfers between devices  31 us (42%)
  starting transfers between devices  22.9 us (31%)
  Pallas kernels  16.9 us (23%)
  other arithmetic  1.78 us (2%)
  local copies, waits for them, and re-layouts  0.94 us (1%)
  between operations  0.89 us (1%)
    pallas_call x11, Pallas kernels, call(): pl.pallas_call(kernel, in_specs=in_specs, out_specs=out_specs, out_shape=...  16.9 us
    ppermute x16, starting transfers between devices, body(): lax.ppermute(b, 'path', pairs[way])  16.5 us
    ppermute x16, waiting for transfers between devices, body(): lax.ppermute(b, 'path', pairs[way])  14.5 us
    ppermute x2, waiting for transfers between devices, body(): lax.ppermute(gradients[s, c], 'fsdp', to_chip(s)).astype(f32)  9.14 us
    ppermute x1, waiting for transfers between devices, body(): lax.ppermute(own_weights, 'fsdp', to_chip(s))  5.56 us
    ppermute x1, starting transfers between devices, body(): lax.ppermute(own_weights, 'fsdp', to_chip(s))  3 us
    ppermute x2, starting transfers between devices, body(): lax.ppermute(gradients[s, c], 'fsdp', to_chip(s)).astype(f32)  2.16 us
    ppermute x1, waiting for transfers between devices, body(): other = lax.ppermute(partial.astype(bf16), 'fsdp', to_core)  1.52 us
  transfers between devices with their start and end apart: 25, of which 14 were waited for; matrix products, arithmetic and copies ran while one was open for 3% of the time, Pallas kernels for 18%

profile of v5, /device:TPU:0, one launch (start us, length us, event | category | flops | bytes accessed | tf_op | source)
XLA Modules:
  0.0 74.5 jit_solution(4839010412968279152)
XLA Ops:
  0.7 0.8 %copy-done.3 = s32[8,1]{0,1:T(1,128)S(1)} copy-done((s32[8,1]{0,1:T(1,128)S(1)}, s32[8,1]{0,1:T(1,128)}, u32[]{:S(2)}) %copy-start.3) | copy-done | bytes 56
  1.5 1.2 %pick_rows.1.after_ref.weights_ref = bf16[1024,256]{1,0:T(8,128)(2,1)S(1)} custom-call(s32[1,8]{1,0:T(1,128)S(1)} %bitcast.7, bf16[8,1024,256]{2,1,0:T(8,128)(2,1)} %weights_ref.11), custom_call_target="tpu_custom_call" | custom-call | tf_op jit(solution)/shard_map/pick_rows/pallas_call | solution.py:62
  2.7 3.0 %collective-permute-start.5 = (bf16[1024,256]{1,0:T(8,128)(2,1)S(1)}, bf16[1024,256]{1,0:T(8,128)(2,1)S(1)}, u32[]{:S(2)}, u32[]{:S(2)}) collective-permute-start(bf16[1024,256]{1,0:T(8,128)(2,1)S(1)} %pick_rows.1.after_ref.weights_ref), channel_id=1, source_target_pairs={{0,2},{1,3},{2,0},{3,1},{4,6},{5,7},{6,4},{7,5},{8,10},{9,11},{10,... | collective-permute-start | bytes 1572872 | tf_op jit(solution)/shard_map/ppermute | solution.py:240
  5.7 1.2 %pick_columns.1 = (bf16[64,2048]{1,0:T(8,128)(2,1)}, bf16[64,2048]{1,0:T(8,128)(2,1)}, bf16[64,2048]{1,0:T(8,128)(2,1)}, bf16[64,2048]{1,0:T(8,128)(2,1)}) custom-call(bf16[1,256,4096]{2,1,0:T(8,128)(2,1)S(1)} %copy-done.1, bf16[1024,256]{1,0:T(8,128)(2,1)S(1)} %pick_rows.1.after_ref.weights_ref), custom_call_target="tpu_custom_call" | custom-call | tf_op jit(solution)/shard_map/pick_columns/pallas_call | solution.py:62
  6.9 0.1 collective-permute-start
  7.0 0.5 collective-permute-start.1
  7.5 0.1 collective-permute-start.2
  7.6 0.4 collective-permute-start.3
  8.0 0.7 fusion.5
  8.7 0.0 collective-permute-done.refs_0_
  8.8 0.1 collective-permute-start.4
  8.9 0.7 select_reduce_fusion.1
  9.6 0.2 select_reduce_fusion
  9.8 0.0 collective-permute-done.2.refs_2_
  9.8 0.2 collective-permute-done.3.refs_3_
  10.0 2.0 %first_products.1 = (f32[512,256]{1,0:T(8,128)S(1)}, bf16[2048,512]{1,0:T(8,128)(2,1)S(1)}, bf16[256,2048]{1,0:T(8,128)(2,1)S(1)}) custom-call(bf16[1,256,4096]{2,1,0:T(8,128)(2,1)S(1)} %copy-done.1, bf16[1024,256]{1,0:T(8,128)(2,1)S(1)} %pick_rows.1.after_ref.weights_ref, bf16[64,2048]{1,0:T(8,128)(2,1)S(1)} %collective-permute-done.refs_0_, ...), custom_call_target="tpu_custom_call" | custom-call | tf_op jit(solution)/shard_map/first_products/pallas_call | solution.py:62
  12.0 0.1 broadcast_in_dim.31.modules_ref
  12.1 5.6 %collective-permute-done.5.weights_ref = bf16[1024,256]{1,0:T(8,128)(2,1)S(1)} collective-permute-done((bf16[1024,256]{1,0:T(8,128)(2,1)S(1)}, bf16[1024,256]{1,0:T(8,128)(2,1)S(1)}, u32[]{:S(2)}, u32[]{:S(2)}) %collective-permute-start.5) | collective-permute-done | bytes 524320 | tf_op jit(solution)/shard_map/ppermute | solution.py:240
  17.6 0.4 next_products.1.mine_ref
  18.1 0.0 slice-start.1
  18.1 0.0 copy-start
  18.1 0.1 collective-permute-start.6
  18.2 1.5 %collective-permute-done.6.other_ref = bf16[512,256]{1,0:T(8,128)(2,1)S(1)} collective-permute-done((bf16[512,256]{1,0:T(8,128)(2,1)S(1)}, bf16[512,256]{1,0:T(8,128)(2,1)S(1)}, u32[]{:S(2)}, u32[]{:S(2)}) %collective-permute-start.6) | collective-permute-done | bytes 262176 | tf_op jit(solution)/shard_map/ppermute | solution.py:264
  19.8 0.5 first_gradients.1
  20.3 1.8 %collective-permute-start.16 = (bf16[512,256]{1,0:T(8,128)(2,1)S(1)}, bf16[512,256]{1,0:T(8,128)(2,1)S(1)}, u32[]{:S(2)}, u32[]{:S(2)}) collective-permute-start(bf16[512,256]{1,0:T(8,128)(2,1)S(1)} %get-tuple-element.63), channel_id=1, source_target_pairs={{0,2},{1,3},{2,0},{3,1},{4,6},{5,7},{6,4},{7,5},{8,10},{9,11},{10,... | collective-permute-start | bytes 786440 | tf_op jit(solution)/shard_map/ppermute | solution.py:288
  22.1 0.6 more_gradients.1
  22.7 0.3 collective-permute-start.7
  23.0 6.5 %collective-permute-done.16 = bf16[512,256]{1,0:T(8,128)(2,1)S(1)} collective-permute-done((bf16[512,256]{1,0:T(8,128)(2,1)S(1)}, bf16[512,256]{1,0:T(8,128)(2,1)S(1)}, u32[]{:S(2)}, u32[]{:S(2)}) %collective-permute-start.16) | collective-permute-done | bytes 262176 | tf_op jit(solution)/shard_map/ppermute | solution.py:288
  29.5 0.1 multiply_convert_fusion.refs_0_
  29.6 1.9 %collective-permute-start.17 = (bf16[512,256]{1,0:T(8,128)(2,1)S(1)}, bf16[512,256]{1,0:T(8,128)(2,1)S(1)}, u32[]{:S(2)}, u32[]{:S(2)}) collective-permute-start(bf16[512,256]{1,0:T(8,128)(2,1)S(1)} %multiply_convert_fusion.refs_0_), channel_id=1, source_target_pairs={{0,8},{4,0},{8,16},{12,4},{16,24},{20,12},{24,28},{28,20},{1,9},{5... | collective-permute-start | bytes 786440 | tf_op jit(solution)/shard_map/ppermute | solution.py:333
  31.5 0.2 collective-permute-start.18
  31.7 2.7 %collective-permute-done.7 = bf16[512,256]{1,0:T(8,128)(2,1)S(1)} collective-permute-done((bf16[512,256]{1,0:T(8,128)(2,1)S(1)}, bf16[512,256]{1,0:T(8,128)(2,1)S(1)}, u32[]{:S(2)}, u32[]{:S(2)}) %collective-permute-start.7) | collective-permute-done | bytes 262176 | tf_op jit(solution)/shard_map/ppermute | solution.py:288
  34.3 0.1 multiply_convert_fusion.1.refs_3_
  34.4 1.9 %collective-permute-start.8 = (bf16[512,256]{1,0:T(8,128)(2,1)S(1)}, bf16[512,256]{1,0:T(8,128)(2,1)S(1)}, u32[]{:S(2)}, u32[]{:S(2)}) collective-permute-start(bf16[512,256]{1,0:T(8,128)(2,1)S(1)} %multiply_convert_fusion.1.refs_3_), channel_id=1, source_target_pairs={{0,8},{4,0},{8,16},{12,4},{16,24},{20,12},{24,28},{28,20},{1,9},{5... | collective-permute-start | bytes 786440 | tf_op jit(solution)/shard_map/ppermute | solution.py:333
  36.3 0.2 collective-permute-start.9
  36.5 0.0 collective-permute-done.17.refs_1_
  36.5 1.4 %collective-permute-done.18.refs_2_ = bf16[512,256]{1,0:T(8,128)(2,1)S(1)} collective-permute-done((bf16[512,256]{1,0:T(8,128)(2,1)S(1)}, bf16[512,256]{1,0:T(8,128)(2,1)S(1)}, u32[]{:S(2)}, u32[]{:S(2)}) %collective-permute-start.18) | collective-permute-done | bytes 262176 | tf_op jit(solution)/shard_map/ppermute | solution.py:333
  37.9 1.6 %collective-permute-start.19 = (bf16[512,256]{1,0:T(8,128)(2,1)S(1)}, bf16[512,256]{1,0:T(8,128)(2,1)S(1)}, u32[]{:S(2)}, u32[]{:S(2)}) collective-permute-start(bf16[512,256]{1,0:T(8,128)(2,1)S(1)} %collective-permute-done.17.refs_1_), channel_id=1, source_target_pairs={{0,8},{4,0},{8,16},{12,4},{16,24},{20,12},{24,28},{28,20},{1,9},{5... | collective-permute-start | bytes 786440 | tf_op jit(solution)/shard_map/ppermute | solution.py:333
  39.5 0.4 collective-permute-start.20
  39.9 3.8 %collective-permute-done.8.refs_4_ = bf16[512,256]{1,0:T(8,128)(2,1)S(1)} collective-permute-done((bf16[512,256]{1,0:T(8,128)(2,1)S(1)}, bf16[512,256]{1,0:T(8,128)(2,1)S(1)}, u32[]{:S(2)}, u32[]{:S(2)}) %collective-permute-start.8) | collective-permute-done | bytes 262176 | tf_op jit(solution)/shard_map/ppermute | solution.py:333
  43.7 1.8 %collective-permute-done.9.refs_5_ = bf16[512,256]{1,0:T(8,128)(2,1)S(1)} collective-permute-done((bf16[512,256]{1,0:T(8,128)(2,1)S(1)}, bf16[512,256]{1,0:T(8,128)(2,1)S(1)}, u32[]{:S(2)}, u32[]{:S(2)}) %collective-permute-start.9) | collective-permute-done | bytes 262176 | tf_op jit(solution)/shard_map/ppermute | solution.py:333
  45.5 1.6 %collective-permute-start.10 = (bf16[512,256]{1,0:T(8,128)(2,1)S(1)}, bf16[512,256]{1,0:T(8,128)(2,1)S(1)}, u32[]{:S(2)}, u32[]{:S(2)}) collective-permute-start(bf16[512,256]{1,0:T(8,128)(2,1)S(1)} %collective-permute-done.8.refs_4_), channel_id=1, source_target_pairs={{0,8},{4,0},{8,16},{12,4},{16,24},{20,12},{24,28},{28,20},{1,9},{5... | collective-permute-start | bytes 786440 | tf_op jit(solution)/shard_map/ppermute | solution.py:333
  47.1 0.4 collective-permute-start.11
  47.6 3.3 %apply_blocks.5 = (bf16[8,1024,256]{2,1,0:T(8,128)(2,1)}, f32[8,1024,256]{2,1,0:T(8,128)}) custom-call(s32[8,128]{1,0:T(8,128)S(1)} %broadcast_in_dim.31.modules_ref, bf16[8,1024,256]{2,1,0:T(8,128)(2,1)S(1)} %copy-done, f32[8,1024,256]{2,1,0:T(8,128)S(1)} %bitcast.4, bf16[512,256]{1,0:T(8,128)(2,1)S(1)} %multiply_convert_fusion.refs_0_, ...), custom_call_target="tpu_custom_call" | custom-call | bytes 6291456 | tf_op jit(solution)/shard_map/apply_blocks/pallas_call | solution.py:62
  50.9 0.0 collective-permute-done.19.refs_0_
  50.9 0.3 collective-permute-done.20.refs_1_
  51.1 1.6 %collective-permute-start.21 = (bf16[512,256]{1,0:T(8,128)(2,1)S(1)}, bf16[512,256]{1,0:T(8,128)(2,1)S(1)}, u32[]{:S(2)}, u32[]{:S(2)}) collective-permute-start(bf16[512,256]{1,0:T(8,128)(2,1)S(1)} %collective-permute-done.19.refs_0_), channel_id=1, source_target_pairs={{0,8},{4,0},{8,16},{12,4},{16,24},{20,12},{24,28},{28,20},{1,9},{5... | collective-permute-start | bytes 786440 | tf_op jit(solution)/shard_map/ppermute | solution.py:333
  52.7 0.4 collective-permute-start.22
  53.2 1.8 %collective-permute-done.10.refs_2_ = bf16[512,256]{1,0:T(8,128)(2,1)S(1)} collective-permute-done((bf16[512,256]{1,0:T(8,128)(2,1)S(1)}, bf16[512,256]{1,0:T(8,128)(2,1)S(1)}, u32[]{:S(2)}, u32[]{:S(2)}) %collective-permute-start.10) | collective-permute-done | bytes 262176 | tf_op jit(solution)/shard_map/ppermute | solution.py:333
  54.9 1.8 %collective-permute-done.11.refs_3_ = bf16[512,256]{1,0:T(8,128)(2,1)S(1)} collective-permute-done((bf16[512,256]{1,0:T(8,128)(2,1)S(1)}, bf16[512,256]{1,0:T(8,128)(2,1)S(1)}, u32[]{:S(2)}, u32[]{:S(2)}) %collective-permute-start.11) | collective-permute-done | bytes 262176 | tf_op jit(solution)/shard_map/ppermute | solution.py:333
  56.8 1.6 %collective-permute-start.12 = (bf16[512,256]{1,0:T(8,128)(2,1)S(1)}, bf16[512,256]{1,0:T(8,128)(2,1)S(1)}, u32[]{:S(2)}, u32[]{:S(2)}) collective-permute-start(bf16[512,256]{1,0:T(8,128)(2,1)S(1)} %collective-permute-done.10.refs_2_), channel_id=1, source_target_pairs={{0,8},{4,0},{8,16},{12,4},{16,24},{20,12},{24,28},{28,20},{1,9},{5... | collective-permute-start | bytes 786440 | tf_op jit(solution)/shard_map/ppermute | solution.py:333
  58.3 0.4 collective-permute-start.14
  58.8 2.5 %apply_blocks.6 = (bf16[8,1024,256]{2,1,0:T(8,128)(2,1)}, f32[8,1024,256]{2,1,0:T(8,128)}) custom-call(s32[8,128]{1,0:T(8,128)S(1)} %broadcast_in_dim.31.modules_ref, bf16[8,1024,256]{2,1,0:T(8,128)(2,1)S(1)} %copy-done, f32[8,1024,256]{2,1,0:T(8,128)S(1)} %bitcast.4, ...), custom_call_target="tpu_custom_call", output_to_operand_aliasing={{0}: (7, {}), {1}: (8, {})} | custom-call | bytes 4194304 | tf_op jit(solution)/shard_map/apply_blocks/pallas_call | solution.py:62
  61.3 1.1 %collective-permute-done.22.refs_1_ = bf16[512,256]{1,0:T(8,128)(2,1)S(1)} collective-permute-done((bf16[512,256]{1,0:T(8,128)(2,1)S(1)}, bf16[512,256]{1,0:T(8,128)(2,1)S(1)}, u32[]{:S(2)}, u32[]{:S(2)}) %collective-permute-start.22) | collective-permute-done | bytes 262176 | tf_op jit(solution)/shard_map/ppermute | solution.py:333
  62.4 1.6 %collective-permute-start.23 = (bf16[256,256]{1,0:T(8,128)(2,1)S(1)}, bf16[256,256]{1,0:T(8,128)(2,1)S(1)}, u32[]{:S(2)}, u32[]{:S(2)}) collective-permute-start(bf16[256,256]{1,0:T(8,128)(2,1)S(1)} %slice.18), channel_id=1, source_target_pairs={{0,8},{4,0},{8,16},{12,4},{16,24},{20,12},{24,28},{28,20},{1,9},{5... | collective-permute-start | bytes 393224 | tf_op jit(solution)/shard_map/ppermute | solution.py:333
  64.0 0.4 collective-permute-start.24
  64.5 1.7 %collective-permute-done.12.refs_2_ = bf16[512,256]{1,0:T(8,128)(2,1)S(1)} collective-permute-done((bf16[512,256]{1,0:T(8,128)(2,1)S(1)}, bf16[512,256]{1,0:T(8,128)(2,1)S(1)}, u32[]{:S(2)}, u32[]{:S(2)}) %collective-permute-start.12) | collective-permute-done | bytes 262176 | tf_op jit(solution)/shard_map/ppermute | solution.py:333
  66.2 1.9 %collective-permute-start.13 = (bf16[256,256]{1,0:T(8,128)(2,1)S(1)}, bf16[256,256]{1,0:T(8,128)(2,1)S(1)}, u32[]{:S(2)}, u32[]{:S(2)}) collective-permute-start(bf16[256,256]{1,0:T(8,128)(2,1)S(1)} %slice.16), channel_id=1, source_target_pairs={{0,8},{4,0},{8,16},{12,4},{16,24},{20,12},{24,28},{28,20},{1,9},{5... | collective-permute-start | bytes 393224 | tf_op jit(solution)/shard_map/ppermute | solution.py:333
  68.1 0.3 collective-permute-start.15
  68.3 2.5 %apply_blocks.7 = (bf16[8,1024,256]{2,1,0:T(8,128)(2,1)}, f32[8,1024,256]{2,1,0:T(8,128)}) custom-call(s32[8,128]{1,0:T(8,128)S(1)} %broadcast_in_dim.31.modules_ref, bf16[8,1024,256]{2,1,0:T(8,128)(2,1)S(1)} %copy-done, f32[8,1024,256]{2,1,0:T(8,128)S(1)} %bitcast.4, ...), custom_call_target="tpu_custom_call", output_to_operand_aliasing={{0}: (7, {}), {1}: (8, {})} | custom-call | bytes 4194304 | tf_op jit(solution)/shard_map/apply_blocks/pallas_call | solution.py:62
  70.8 0.0 collective-permute-done.23.refs_0_
  70.8 1.4 %apply_blocks.8 = (bf16[8,1024,256]{2,1,0:T(8,128)(2,1)}, f32[8,1024,256]{2,1,0:T(8,128)}) custom-call(s32[8,128]{1,0:T(8,128)S(1)} %broadcast_in_dim.31.modules_ref, bf16[8,1024,256]{2,1,0:T(8,128)(2,1)S(1)} %copy-done, f32[8,1024,256]{2,1,0:T(8,128)S(1)} %bitcast.4, ...), custom_call_target="tpu_custom_call", output_to_operand_aliasing={{0}: (5, {}), {1}: (6, {})} | custom-call | bytes 1048576 | tf_op jit(solution)/shard_map/apply_blocks/pallas_call | solution.py:62
  72.2 0.9 %collective-permute-done.15.refs_1_ = bf16[256,256]{1,0:T(8,128)(2,1)S(1)} collective-permute-done((bf16[256,256]{1,0:T(8,128)(2,1)S(1)}, bf16[256,256]{1,0:T(8,128)(2,1)S(1)}, u32[]{:S(2)}, u32[]{:S(2)}) %collective-permute-start.15) | collective-permute-done | bytes 131104 | tf_op jit(solution)/shard_map/ppermute | solution.py:333
  73.1 1.4 %apply_blocks.9 = (bf16[8,1024,256]{2,1,0:T(8,128)(2,1)}, f32[8,1024,256]{2,1,0:T(8,128)}) custom-call(s32[8,128]{1,0:T(8,128)S(1)} %broadcast_in_dim.31.modules_ref, bf16[8,1024,256]{2,1,0:T(8,128)(2,1)S(1)} %copy-done, f32[8,1024,256]{2,1,0:T(8,128)S(1)} %bitcast.4, ...), custom_call_target="tpu_custom_call", output_to_operand_aliasing={{0}: (5, {}), {1}: (6, {})} | custom-call | bytes 1048576 | tf_op jit(solution)/shard_map/apply_blocks/pallas_call | solution.py:62
  (25 shorter events, 0.1 us)
Async XLA Ops:
  0.6 5.1 %copy-start.1 = (bf16[1,256,4096]{2,1,0:T(8,128)(2,1)S(1)}, bf16[1,256,4096]{2,1,0:T(8,128)(2,1)}, u32[]{:S(2)}) copy-start(bf16[1,256,4096]{2,1,0:T(8,128)(2,1)} %tokens_ref.5) | copy-start | bytes 6291460
  0.6 8.1 %copy-start.2 = (bf16[1,256,256]{2,1,0:T(8,128)(2,1)S(1)}, bf16[1,256,256]{2,1,0:T(8,128)(2,1)}, u32[]{:S(2)}) copy-start(bf16[1,256,256]{2,1,0:T(8,128)(2,1)} %param.7) | copy-start | bytes 393220
  0.6 0.8 %copy-start.3 = (s32[8,1]{0,1:T(1,128)S(1)}, s32[8,1]{0,1:T(1,128)}, u32[]{:S(2)}) copy-start(s32[8,1]{0,1:T(1,128)} %param.8) | copy-start | bytes 100
  1.5 6.6 %copy-start.5 = (s32[8]{0:T(128)S(1)}, s32[8]{0:T(128)}, u32[]{:S(2)}) copy-start(s32[8]{0:T(128)} %constant.28.clone) | copy-start | bytes 100
  1.5 8.2 %copy-start.4 = (s32[8,1]{0,1:T(1,128)S(1)}, s32[8,1]{0,1:T(1,128)}, u32[]{:S(2)}) copy-start(s32[8,1]{0,1:T(1,128)} %param.8) | copy-start | bytes 100
  2.7 14.9 %collective-permute-start.5 = (bf16[1024,256]{1,0:T(8,128)(2,1)S(1)}, bf16[1024,256]{1,0:T(8,128)(2,1)S(1)}, u32[]{:S(2)}, u32[]{:S(2)}) collective-permute-start(bf16[1024,256]{1,0:T(8,128)(2,1)S(1)} %pick_rows.1.after_ref.weights_ref), channel_id=1, source_target_pairs={{0,2},{1,3},{2,0},{3,1},{4,6},{5,7},{6,4},{7,5},{8,10},{9,11},{10,... | collective-permute-start | bytes 1572872 | tf_op jit(solution)/shard_map/ppermute | solution.py:240
  6.9 1.8 %collective-permute-start = (bf16[64,2048]{1,0:T(8,128)(2,1)}, bf16[64,2048]{1,0:T(8,128)(2,1)S(1)}, u32[]{:S(2)}, u32[]{:S(2)}) collective-permute-start(bf16[64,2048]{1,0:T(8,128)(2,1)} %get-tuple-element.43), channel_id=1, source_target_pairs={{0,1},{1,0},{2,3},{3,2},{4,5},{5,4},{6,7},{7,6},{8,9},{9,8},{10,11... | collective-permute-start | bytes 786440 | tf_op jit(solution)/shard_map/ppermute | solution.py:247
  7.0 2.8 %collective-permute-start.1 = (bf16[64,2048]{1,0:T(8,128)(2,1)}, bf16[64,2048]{1,0:T(8,128)(2,1)}, u32[]{:S(2)}, u32[]{:S(2)}) collective-permute-start(bf16[64,2048]{1,0:T(8,128)(2,1)} %get-tuple-element.44), channel_id=1, source_target_pairs={{0,1},{1,0},{2,3},{3,2},{4,5},{5,4},{6,7},{7,6},{8,9},{9,8},{10,11... | collective-permute-start | bytes 786440 | tf_op jit(solution)/shard_map/ppermute | solution.py:247
  7.5 2.3 %collective-permute-start.2 = (bf16[64,2048]{1,0:T(8,128)(2,1)}, bf16[64,2048]{1,0:T(8,128)(2,1)}, u32[]{:S(2)}, u32[]{:S(2)}) collective-permute-start(bf16[64,2048]{1,0:T(8,128)(2,1)} %get-tuple-element.45), channel_id=1, source_target_pairs={{0,1},{1,0},{2,3},{3,2},{4,5},{5,4},{6,7},{7,6},{8,9},{9,8},{10,11... | collective-permute-start | bytes 786440 | tf_op jit(solution)/shard_map/ppermute | solution.py:247
  7.6 2.4 %collective-permute-start.3 = (bf16[64,2048]{1,0:T(8,128)(2,1)}, bf16[64,2048]{1,0:T(8,128)(2,1)}, u32[]{:S(2)}, u32[]{:S(2)}) collective-permute-start(bf16[64,2048]{1,0:T(8,128)(2,1)} %get-tuple-element.46), channel_id=1, source_target_pairs={{0,1},{1,0},{2,3},{3,2},{4,5},{5,4},{6,7},{7,6},{8,9},{9,8},{10,11... | collective-permute-start | bytes 786440 | tf_op jit(solution)/shard_map/ppermute | solution.py:247
  8.8 3.2 %collective-permute-start.4 = (bf16[256,256]{1,0:T(8,128)(2,1)S(1)}, bf16[256,256]{1,0:T(8,128)(2,1)S(1)}, u32[]{:S(2)}, u32[]{:S(2)}) collective-permute-start(bf16[256,256]{1,0:T(8,128)(2,1)S(1)} %bitcast.5), channel_id=1, source_target_pairs={{0,1},{1,0},{2,3},{3,2},{4,5},{5,4},{6,7},{7,6},{8,9},{9,8},{10,11... | collective-permute-start | bytes 393224 | tf_op jit(solution)/shard_map/ppermute | solution.py:246
  10.0 37.5 %slice-start = ((s8[8388608]{0:T(1024)(128)(4,1)}), s8[4194304]{0:T(1024)(128)(4,1)S(1)}, s32[]{:S(2)}) async-start(s8[8388608]{0:T(1024)(128)(4,1)} %bitcast.3), calls=%async_computation | async-start | bytes 8388608
  18.1 29.5 %slice-start.1 = ((s8[8388608]{0:T(1024)(128)(4,1)}), s8[4194304]{0:T(1024)(128)(4,1)S(1)}, s32[]{:S(2)}) async-start(s8[8388608]{0:T(1024)(128)(4,1)} %bitcast.3), calls=%async_computation.1 | async-start | bytes 8388608
  18.1 29.5 %copy-start = (bf16[8,1024,256]{2,1,0:T(8,128)(2,1)S(1)}, bf16[8,1024,256]{2,1,0:T(8,128)(2,1)}, u32[]{:S(2)}) copy-start(bf16[8,1024,256]{2,1,0:T(8,128)(2,1)} %weights_ref.11) | copy-start | bytes 12582916
  18.1 1.6 %collective-permute-start.6 = (bf16[512,256]{1,0:T(8,128)(2,1)S(1)}, bf16[512,256]{1,0:T(8,128)(2,1)S(1)}, u32[]{:S(2)}, u32[]{:S(2)}) collective-permute-start(bf16[512,256]{1,0:T(8,128)(2,1)S(1)} %convert_element_type.15), channel_id=1, source_target_pairs={{0,1},{1,0},{2,3},{3,2},{4,5},{5,4},{6,7},{7,6},{8,9},{9,8},{10,11... | collective-permute-start | bytes 786440 | tf_op jit(solution)/shard_map/ppermute | solution.py:264
  20.3 9.2 %collective-permute-start.16 = (bf16[512,256]{1,0:T(8,128)(2,1)S(1)}, bf16[512,256]{1,0:T(8,128)(2,1)S(1)}, u32[]{:S(2)}, u32[]{:S(2)}) collective-permute-start(bf16[512,256]{1,0:T(8,128)(2,1)S(1)} %get-tuple-element.63), channel_id=1, source_target_pairs={{0,2},{1,3},{2,0},{3,1},{4,6},{5,7},{6,4},{7,5},{8,10},{9,11},{10,... | collective-permute-start | bytes 786440 | tf_op jit(solution)/shard_map/ppermute | solution.py:288
  22.7 11.7 %collective-permute-start.7 = (bf16[512,256]{1,0:T(8,128)(2,1)S(1)}, bf16[512,256]{1,0:T(8,128)(2,1)S(1)}, u32[]{:S(2)}, u32[]{:S(2)}) collective-permute-start(bf16[512,256]{1,0:T(8,128)(2,1)S(1)} %get-tuple-element.55), channel_id=1, source_target_pairs={{0,2},{1,3},{2,0},{3,1},{4,6},{5,7},{6,4},{7,5},{8,10},{9,11},{10,... | collective-permute-start | bytes 786440 | tf_op jit(solution)/shard_map/ppermute | solution.py:288
  29.6 6.9 %collective-permute-start.17 = (bf16[512,256]{1,0:T(8,128)(2,1)S(1)}, bf16[512,256]{1,0:T(8,128)(2,1)S(1)}, u32[]{:S(2)}, u32[]{:S(2)}) collective-permute-start(bf16[512,256]{1,0:T(8,128)(2,1)S(1)} %multiply_convert_fusion.refs_0_), channel_id=1, source_target_pairs={{0,8},{4,0},{8,16},{12,4},{16,24},{20,12},{24,28},{28,20},{1,9},{5... | collective-permute-start | bytes 786440 | tf_op jit(solution)/shard_map/ppermute | solution.py:333
  31.5 6.4 %collective-permute-start.18 = (bf16[512,256]{1,0:T(8,128)(2,1)S(1)}, bf16[512,256]{1,0:T(8,128)(2,1)S(1)}, u32[]{:S(2)}, u32[]{:S(2)}) collective-permute-start(bf16[512,256]{1,0:T(8,128)(2,1)S(1)} %multiply_convert_fusion.refs_0_), channel_id=1, source_target_pairs={{0,4},{4,12},{8,0},{12,20},{16,8},{20,28},{24,16},{28,24},{1,5},{5... | collective-permute-start | bytes 786440 | tf_op jit(solution)/shard_map/ppermute | solution.py:333
  34.4 9.3 %collective-permute-start.8 = (bf16[512,256]{1,0:T(8,128)(2,1)S(1)}, bf16[512,256]{1,0:T(8,128)(2,1)S(1)}, u32[]{:S(2)}, u32[]{:S(2)}) collective-permute-start(bf16[512,256]{1,0:T(8,128)(2,1)S(1)} %multiply_convert_fusion.1.refs_3_), channel_id=1, source_target_pairs={{0,8},{4,0},{8,16},{12,4},{16,24},{20,12},{24,28},{28,20},{1,9},{5... | collective-permute-start | bytes 786440 | tf_op jit(solution)/shard_map/ppermute | solution.py:333
  36.3 9.2 %collective-permute-start.9 = (bf16[512,256]{1,0:T(8,128)(2,1)S(1)}, bf16[512,256]{1,0:T(8,128)(2,1)S(1)}, u32[]{:S(2)}, u32[]{:S(2)}) collective-permute-start(bf16[512,256]{1,0:T(8,128)(2,1)S(1)} %multiply_convert_fusion.1.refs_3_), channel_id=1, source_target_pairs={{0,4},{4,12},{8,0},{12,20},{16,8},{20,28},{24,16},{28,24},{1,5},{5... | collective-permute-start | bytes 786440 | tf_op jit(solution)/shard_map/ppermute | solution.py:333
  37.9 12.9 %collective-permute-start.19 = (bf16[512,256]{1,0:T(8,128)(2,1)S(1)}, bf16[512,256]{1,0:T(8,128)(2,1)S(1)}, u32[]{:S(2)}, u32[]{:S(2)}) collective-permute-start(bf16[512,256]{1,0:T(8,128)(2,1)S(1)} %collective-permute-done.17.refs_1_), channel_id=1, source_target_pairs={{0,8},{4,0},{8,16},{12,4},{16,24},{20,12},{24,28},{28,20},{1,9},{5... | collective-permute-start | bytes 786440 | tf_op jit(solution)/shard_map/ppermute | solution.py:333
  39.5 11.7 %collective-permute-start.20 = (bf16[512,256]{1,0:T(8,128)(2,1)S(1)}, bf16[512,256]{1,0:T(8,128)(2,1)S(1)}, u32[]{:S(2)}, u32[]{:S(2)}) collective-permute-start(bf16[512,256]{1,0:T(8,128)(2,1)S(1)} %collective-permute-done.18.refs_2_), channel_id=1, source_target_pairs={{0,4},{4,12},{8,0},{12,20},{16,8},{20,28},{24,16},{28,24},{1,5},{5... | collective-permute-start | bytes 786440 | tf_op jit(solution)/shard_map/ppermute | solution.py:333
  45.5 9.4 %collective-permute-start.10 = (bf16[512,256]{1,0:T(8,128)(2,1)S(1)}, bf16[512,256]{1,0:T(8,128)(2,1)S(1)}, u32[]{:S(2)}, u32[]{:S(2)}) collective-permute-start(bf16[512,256]{1,0:T(8,128)(2,1)S(1)} %collective-permute-done.8.refs_4_), channel_id=1, source_target_pairs={{0,8},{4,0},{8,16},{12,4},{16,24},{20,12},{24,28},{28,20},{1,9},{5... | collective-permute-start | bytes 786440 | tf_op jit(solution)/shard_map/ppermute | solution.py:333
  47.1 9.7 %collective-permute-start.11 = (bf16[512,256]{1,0:T(8,128)(2,1)S(1)}, bf16[512,256]{1,0:T(8,128)(2,1)S(1)}, u32[]{:S(2)}, u32[]{:S(2)}) collective-permute-start(bf16[512,256]{1,0:T(8,128)(2,1)S(1)} %collective-permute-done.9.refs_5_), channel_id=1, source_target_pairs={{0,4},{4,12},{8,0},{12,20},{16,8},{20,28},{24,16},{28,24},{1,5},{5... | collective-permute-start | bytes 786440 | tf_op jit(solution)/shard_map/ppermute | solution.py:333
  51.1 10.1 %collective-permute-start.21 = (bf16[512,256]{1,0:T(8,128)(2,1)S(1)}, bf16[512,256]{1,0:T(8,128)(2,1)S(1)}, u32[]{:S(2)}, u32[]{:S(2)}) collective-permute-start(bf16[512,256]{1,0:T(8,128)(2,1)S(1)} %collective-permute-done.19.refs_0_), channel_id=1, source_target_pairs={{0,8},{4,0},{8,16},{12,4},{16,24},{20,12},{24,28},{28,20},{1,9},{5... | collective-permute-start | bytes 786440 | tf_op jit(solution)/shard_map/ppermute | solution.py:333
  52.7 9.7 %collective-permute-start.22 = (bf16[512,256]{1,0:T(8,128)(2,1)S(1)}, bf16[512,256]{1,0:T(8,128)(2,1)S(1)}, u32[]{:S(2)}, u32[]{:S(2)}) collective-permute-start(bf16[512,256]{1,0:T(8,128)(2,1)S(1)} %collective-permute-done.20.refs_1_), channel_id=1, source_target_pairs={{0,4},{4,12},{8,0},{12,20},{16,8},{20,28},{24,16},{28,24},{1,5},{5... | collective-permute-start | bytes 786440 | tf_op jit(solution)/shard_map/ppermute | solution.py:333
  56.8 9.4 %collective-permute-start.12 = (bf16[512,256]{1,0:T(8,128)(2,1)S(1)}, bf16[512,256]{1,0:T(8,128)(2,1)S(1)}, u32[]{:S(2)}, u32[]{:S(2)}) collective-permute-start(bf16[512,256]{1,0:T(8,128)(2,1)S(1)} %collective-permute-done.10.refs_2_), channel_id=1, source_target_pairs={{0,8},{4,0},{8,16},{12,4},{16,24},{20,12},{24,28},{28,20},{1,9},{5... | collective-permute-start | bytes 786440 | tf_op jit(solution)/shard_map/ppermute | solution.py:333
  58.3 9.7 %collective-permute-start.14 = (bf16[512,256]{1,0:T(8,128)(2,1)S(1)}, bf16[512,256]{1,0:T(8,128)(2,1)S(1)}, u32[]{:S(2)}, u32[]{:S(2)}) collective-permute-start(bf16[512,256]{1,0:T(8,128)(2,1)S(1)} %collective-permute-done.11.refs_3_), channel_id=1, source_target_pairs={{0,4},{4,12},{8,0},{12,20},{16,8},{20,28},{24,16},{28,24},{1,5},{5... | collective-permute-start | bytes 786440 | tf_op jit(solution)/shard_map/ppermute | solution.py:333
  62.4 8.4 %collective-permute-start.23 = (bf16[256,256]{1,0:T(8,128)(2,1)S(1)}, bf16[256,256]{1,0:T(8,128)(2,1)S(1)}, u32[]{:S(2)}, u32[]{:S(2)}) collective-permute-start(bf16[256,256]{1,0:T(8,128)(2,1)S(1)} %slice.18), channel_id=1, source_target_pairs={{0,8},{4,0},{8,16},{12,4},{16,24},{20,12},{24,28},{28,20},{1,9},{5... | collective-permute-start | bytes 393224 | tf_op jit(solution)/shard_map/ppermute | solution.py:333
  64.0 6.8 %collective-permute-start.24 = (bf16[256,256]{1,0:T(8,128)(2,1)S(1)}, bf16[256,256]{1,0:T(8,128)(2,1)S(1)}, u32[]{:S(2)}, u32[]{:S(2)}) collective-permute-start(bf16[256,256]{1,0:T(8,128)(2,1)S(1)} %slice.19), channel_id=1, source_target_pairs={{0,4},{4,12},{8,0},{12,20},{16,8},{20,28},{24,16},{28,24},{1,5},{5... | collective-permute-start | bytes 393224 | tf_op jit(solution)/shard_map/ppermute | solution.py:333
  66.2 6.0 %collective-permute-start.13 = (bf16[256,256]{1,0:T(8,128)(2,1)S(1)}, bf16[256,256]{1,0:T(8,128)(2,1)S(1)}, u32[]{:S(2)}, u32[]{:S(2)}) collective-permute-start(bf16[256,256]{1,0:T(8,128)(2,1)S(1)} %slice.16), channel_id=1, source_target_pairs={{0,8},{4,0},{8,16},{12,4},{16,24},{20,12},{24,28},{28,20},{1,9},{5... | collective-permute-start | bytes 393224 | tf_op jit(solution)/shard_map/ppermute | solution.py:333
  68.1 5.0 %collective-permute-start.15 = (bf16[256,256]{1,0:T(8,128)(2,1)S(1)}, bf16[256,256]{1,0:T(8,128)(2,1)S(1)}, u32[]{:S(2)}, u32[]{:S(2)}) collective-permute-start(bf16[256,256]{1,0:T(8,128)(2,1)S(1)} %slice.17), channel_id=1, source_target_pairs={{0,4},{4,12},{8,0},{12,20},{16,8},{20,28},{24,16},{28,24},{1,5},{5... | collective-permute-start | bytes 393224 | tf_op jit(solution)/shard_map/ppermute | solution.py:333

commit v6 on v5

--- a/solution.py
+++ b/solution.py
@@ -50,10 +50,6 @@
     share, more = divmod(rows // unit, CHAINS)
     sizes = [unit * (share + (c < more)) for c in range(CHAINS)]
     return [(sum(sizes[:c]), size) for c, size in enumerate(sizes)]
-
-
-def far_share(size):
-    return size // 2
 
 
 def call(
@@ -315,32 +311,34 @@
         )
 
     held = [h.astype(bf16) for h in held]
-    group = [(0, chains[c][0], h) for c, h in enumerate(held)]
     moving = [[h, h] for h in held]
     waiting = [[(0, start, h)] for (start, _), h in zip(chains, held)]
     for step in range(1, paths // 2 + 1):
         last = 2 * step == paths
         for c, (start, size) in enumerate(chains):
             pair, starts = moving[c], [start, start]
+            ways = (1, -1) if c % 2 == 0 else (-1, 1)
             if last:
-                first = far_share(size)
-                pair = [pair[0][:first], pair[1][first:]]
-                starts = [start, start + first]
+                pair = [pair[0][: size // 2], pair[1][size // 2 :]]
+                starts = [start, start + size // 2]
+            if last and c == 0:
+                outs = apply(waiting[0], outs)
+                waiting[0] = []
             if step > 2 and c == 0:
                 pair, outs = lax.optimization_barrier((pair, outs))
             elif not last:
                 pair = lax.optimization_barrier(tuple(pair))
-            moving[c] = [lax.ppermute(b, "path", pairs[way]) for b, way in zip(pair, (1, -1))]
+            moving[c] = [lax.ppermute(b, "path", pairs[way]) for b, way in zip(pair, ways)]
             if step > 1 and c == 0 and not last:
                 outs = apply([one for group in waiting for one in group], outs)
                 waiting = [[] for _ in chains]
             waiting[c] += [
                 ((way * step) % paths, first, b)
-                for b, first, way in zip(moving[c], starts, (1, -1))
+                for b, first, way in zip(moving[c], starts, ways)
             ]
-    far = [group[-2:] for group in waiting]
-    outs = apply([one for group in waiting for one in group[:-2]], outs)
-    for group in far:
+    final = waiting[-1][-2:]
+    waiting[-1] = waiting[-1][:-2]
+    for group in (waiting[-1], *waiting[:-1], final):
         outs = apply(group, outs)
     return tuple(outs)
 

time: 74.6 us -> 74.3 us (level)
  waiting for transfers between devices: 31 us -> 29.7 us
  Pallas kernels: 16.9 us -> 17.8 us
    ppermute x16, waiting for transfers between devices: 14.5 us -> 13.4 us  [body(): lax.ppermute(b, 'path', pairs[way])]
    pallas_call x11 -> x12, Pallas kernels: 16.9 us -> 17.8 us  [call(): pl.pallas_call(kernel, in_specs=in_specs, out_specs=out_specs, out_shape=...]
  transfers between devices with their start and end apart: 25 -> 25, of which waited for: 14 -> 14; matrix products, arithmetic and copies ran while one was open for 3% -> 3% of each run, Pallas kernels for 18% -> 19%
where the time goes in v6:
time: 74.3 us; the launch traced here: 74.2 us
  waiting for transfers between devices  29.7 us (40%)
  starting transfers between devices  22.9 us (31%)
  Pallas kernels  17.8 us (24%)
  other arithmetic  1.85 us (2%)
  local copies, waits for them, and re-layouts  0.94 us (1%)
  between operations  0.89 us (1%)
    pallas_call x12, Pallas kernels, call(): pl.pallas_call(kernel, in_specs=in_specs, out_specs=out_specs, out_shape=...  17.8 us
    ppermute x16, starting transfers between devices, body(): lax.ppermute(b, 'path', pairs[way])  16.5 us
    ppermute x16, waiting for transfers between devices, body(): lax.ppermute(b, 'path', pairs[way])  13.4 us
    ppermute x2, waiting for transfers between devices, body(): lax.ppermute(gradients[s, c], 'fsdp', to_chip(s)).astype(f32)  9.14 us
    ppermute x1, waiting for transfers between devices, body(): lax.ppermute(own_weights, 'fsdp', to_chip(s))  5.57 us
    ppermute x1, starting transfers between devices, body(): lax.ppermute(own_weights, 'fsdp', to_chip(s))  3 us
    ppermute x2, starting transfers between devices, body(): lax.ppermute(gradients[s, c], 'fsdp', to_chip(s)).astype(f32)  2.16 us
    ppermute x1, waiting for transfers between devices, body(): other = lax.ppermute(partial.astype(bf16), 'fsdp', to_core)  1.52 us
  transfers between devices with their start and end apart: 25, of which 14 were waited for; matrix products, arithmetic and copies ran while one was open for 3% of the time, Pallas kernels for 19%

profile of v6, /device:TPU:0, one launch (start us, length us, event | category | flops | bytes accessed | tf_op | source)
XLA Modules:
  0.0 74.2 jit_solution(417317025323276845)
XLA Ops:
  0.7 0.8 %copy-done.3 = s32[8,1]{0,1:T(1,128)S(1)} copy-done((s32[8,1]{0,1:T(1,128)S(1)}, s32[8,1]{0,1:T(1,128)}, u32[]{:S(2)}) %copy-start.3) | copy-done | bytes 56
  1.5 1.2 %pick_rows.1.after_ref.weights_ref = bf16[1024,256]{1,0:T(8,128)(2,1)S(1)} custom-call(s32[1,8]{1,0:T(1,128)S(1)} %bitcast.7, bf16[8,1024,256]{2,1,0:T(8,128)(2,1)} %weights_ref.13), custom_call_target="tpu_custom_call" | custom-call | tf_op jit(solution)/shard_map/pick_rows/pallas_call | solution.py:58
  2.7 3.0 %collective-permute-start.5 = (bf16[1024,256]{1,0:T(8,128)(2,1)S(1)}, bf16[1024,256]{1,0:T(8,128)(2,1)S(1)}, u32[]{:S(2)}, u32[]{:S(2)}) collective-permute-start(bf16[1024,256]{1,0:T(8,128)(2,1)S(1)} %pick_rows.1.after_ref.weights_ref), channel_id=1, source_target_pairs={{0,2},{1,3},{2,0},{3,1},{4,6},{5,7},{6,4},{7,5},{8,10},{9,11},{10,... | collective-permute-start | bytes 1572872 | tf_op jit(solution)/shard_map/ppermute | solution.py:236
  5.7 1.2 %pick_columns.1 = (bf16[64,2048]{1,0:T(8,128)(2,1)}, bf16[64,2048]{1,0:T(8,128)(2,1)}, bf16[64,2048]{1,0:T(8,128)(2,1)}, bf16[64,2048]{1,0:T(8,128)(2,1)}) custom-call(bf16[1,256,4096]{2,1,0:T(8,128)(2,1)S(1)} %copy-done.1, bf16[1024,256]{1,0:T(8,128)(2,1)S(1)} %pick_rows.1.after_ref.weights_ref), custom_call_target="tpu_custom_call" | custom-call | tf_op jit(solution)/shard_map/pick_columns/pallas_call | solution.py:58
  6.9 0.1 collective-permute-start
  7.0 0.5 collective-permute-start.1
  7.5 0.1 collective-permute-start.2
  7.6 0.4 collective-permute-start.3
  8.0 0.7 fusion.5
  8.7 0.0 collective-permute-done.refs_0_
  8.8 0.1 collective-permute-start.4
  8.9 0.8 %select_reduce_fusion.1 = s32[8]{0:T(128)S(1)} fusion(s32[8]{0:T(128)S(1)} %copy-done.5, s32[]{:T(128)} %fusion.5), kind=kLoop, calls=%fused_computation.9 | loop fusion | flops 952 | bytes 68 | tf_op jit(solution)/shard_map/reduce_sum | solution.py:37
  9.7 0.2 select_reduce_fusion
  9.9 0.0 collective-permute-done.1.refs_1_
  9.9 0.0 collective-permute-done.2.refs_2_
  9.9 0.1 collective-permute-done.3.refs_3_
  10.0 2.0 %first_products.1 = (f32[512,256]{1,0:T(8,128)S(1)}, bf16[2048,512]{1,0:T(8,128)(2,1)S(1)}, bf16[256,2048]{1,0:T(8,128)(2,1)S(1)}) custom-call(bf16[1,256,4096]{2,1,0:T(8,128)(2,1)S(1)} %copy-done.1, bf16[1024,256]{1,0:T(8,128)(2,1)S(1)} %pick_rows.1.after_ref.weights_ref, bf16[64,2048]{1,0:T(8,128)(2,1)S(1)} %collective-permute-done.refs_0_, ...), custom_call_target="tpu_custom_call" | custom-call | tf_op jit(solution)/shard_map/first_products/pallas_call | solution.py:58
  12.0 0.0 collective-permute-done.4.other_up_ref
  12.0 0.1 broadcast_in_dim.31.modules_ref
  12.1 5.6 %collective-permute-done.5.weights_ref = bf16[1024,256]{1,0:T(8,128)(2,1)S(1)} collective-permute-done((bf16[1024,256]{1,0:T(8,128)(2,1)S(1)}, bf16[1024,256]{1,0:T(8,128)(2,1)S(1)}, u32[]{:S(2)}, u32[]{:S(2)}) %collective-permute-start.5) | collective-permute-done | bytes 524320 | tf_op jit(solution)/shard_map/ppermute | solution.py:236
  17.6 0.4 next_products.1.mine_ref
  18.1 0.0 slice-start.1
  18.1 0.0 copy-start
  18.1 0.1 collective-permute-start.6
  18.2 1.5 %collective-permute-done.6.other_ref = bf16[512,256]{1,0:T(8,128)(2,1)S(1)} collective-permute-done((bf16[512,256]{1,0:T(8,128)(2,1)S(1)}, bf16[512,256]{1,0:T(8,128)(2,1)S(1)}, u32[]{:S(2)}, u32[]{:S(2)}) %collective-permute-start.6) | collective-permute-done | bytes 262176 | tf_op jit(solution)/shard_map/ppermute | solution.py:260
  19.8 0.5 first_gradients.1
  20.3 1.8 %collective-permute-start.16 = (bf16[512,256]{1,0:T(8,128)(2,1)S(1)}, bf16[512,256]{1,0:T(8,128)(2,1)S(1)}, u32[]{:S(2)}, u32[]{:S(2)}) collective-permute-start(bf16[512,256]{1,0:T(8,128)(2,1)S(1)} %get-tuple-element.65), channel_id=1, source_target_pairs={{0,2},{1,3},{2,0},{3,1},{4,6},{5,7},{6,4},{7,5},{8,10},{9,11},{10,... | collective-permute-start | bytes 786440 | tf_op jit(solution)/shard_map/ppermute | solution.py:284
  22.1 0.6 more_gradients.1
  22.7 0.3 collective-permute-start.7
  23.0 6.5 %collective-permute-done.16 = bf16[512,256]{1,0:T(8,128)(2,1)S(1)} collective-permute-done((bf16[512,256]{1,0:T(8,128)(2,1)S(1)}, bf16[512,256]{1,0:T(8,128)(2,1)S(1)}, u32[]{:S(2)}, u32[]{:S(2)}) %collective-permute-start.16) | collective-permute-done | bytes 262176 | tf_op jit(solution)/shard_map/ppermute | solution.py:284
  29.5 0.1 multiply_convert_fusion.refs_0_
  29.6 1.9 %collective-permute-start.17 = (bf16[512,256]{1,0:T(8,128)(2,1)S(1)}, bf16[512,256]{1,0:T(8,128)(2,1)S(1)}, u32[]{:S(2)}, u32[]{:S(2)}) collective-permute-start(bf16[512,256]{1,0:T(8,128)(2,1)S(1)} %multiply_convert_fusion.refs_0_), channel_id=1, source_target_pairs={{0,8},{4,0},{8,16},{12,4},{16,24},{20,12},{24,28},{28,20},{1,9},{5... | collective-permute-start | bytes 786440 | tf_op jit(solution)/shard_map/ppermute | solution.py:331
  31.5 0.2 collective-permute-start.18
  31.7 2.7 %collective-permute-done.7 = bf16[512,256]{1,0:T(8,128)(2,1)S(1)} collective-permute-done((bf16[512,256]{1,0:T(8,128)(2,1)S(1)}, bf16[512,256]{1,0:T(8,128)(2,1)S(1)}, u32[]{:S(2)}, u32[]{:S(2)}) %collective-permute-start.7) | collective-permute-done | bytes 262176 | tf_op jit(solution)/shard_map/ppermute | solution.py:284
  34.3 0.1 multiply_convert_fusion.1.refs_3_
  34.4 1.8 %collective-permute-start.8 = (bf16[512,256]{1,0:T(8,128)(2,1)S(1)}, bf16[512,256]{1,0:T(8,128)(2,1)S(1)}, u32[]{:S(2)}, u32[]{:S(2)}) collective-permute-start(bf16[512,256]{1,0:T(8,128)(2,1)S(1)} %multiply_convert_fusion.1.refs_3_), channel_id=1, source_target_pairs={{0,4},{4,12},{8,0},{12,20},{16,8},{20,28},{24,16},{28,24},{1,5},{5... | collective-permute-start | bytes 786440 | tf_op jit(solution)/shard_map/ppermute | solution.py:331
  36.2 0.3 collective-permute-start.9
  36.5 2.8 %collective-permute-done.18.refs_2_ = bf16[512,256]{1,0:T(8,128)(2,1)S(1)} collective-permute-done((bf16[512,256]{1,0:T(8,128)(2,1)S(1)}, bf16[512,256]{1,0:T(8,128)(2,1)S(1)}, u32[]{:S(2)}, u32[]{:S(2)}) %collective-permute-start.18) | collective-permute-done | bytes 262176 | tf_op jit(solution)/shard_map/ppermute | solution.py:331
  39.3 1.4 %collective-permute-start.19 = (bf16[512,256]{1,0:T(8,128)(2,1)S(1)}, bf16[512,256]{1,0:T(8,128)(2,1)S(1)}, u32[]{:S(2)}, u32[]{:S(2)}) collective-permute-start(bf16[512,256]{1,0:T(8,128)(2,1)S(1)} %collective-permute-done.17.refs_1_), channel_id=1, source_target_pairs={{0,8},{4,0},{8,16},{12,4},{16,24},{20,12},{24,28},{28,20},{1,9},{5... | collective-permute-start | bytes 786440 | tf_op jit(solution)/shard_map/ppermute | solution.py:331
  40.7 0.6 collective-permute-start.20
  41.3 3.6 %collective-permute-done.8.refs_4_ = bf16[512,256]{1,0:T(8,128)(2,1)S(1)} collective-permute-done((bf16[512,256]{1,0:T(8,128)(2,1)S(1)}, bf16[512,256]{1,0:T(8,128)(2,1)S(1)}, u32[]{:S(2)}, u32[]{:S(2)}) %collective-permute-start.8) | collective-permute-done | bytes 262176 | tf_op jit(solution)/shard_map/ppermute | solution.py:331
  44.9 0.5 collective-permute-done.9.refs_5_
  45.5 1.6 %collective-permute-start.10 = (bf16[512,256]{1,0:T(8,128)(2,1)S(1)}, bf16[512,256]{1,0:T(8,128)(2,1)S(1)}, u32[]{:S(2)}, u32[]{:S(2)}) collective-permute-start(bf16[512,256]{1,0:T(8,128)(2,1)S(1)} %collective-permute-done.8.refs_4_), channel_id=1, source_target_pairs={{0,4},{4,12},{8,0},{12,20},{16,8},{20,28},{24,16},{28,24},{1,5},{5... | collective-permute-start | bytes 786440 | tf_op jit(solution)/shard_map/ppermute | solution.py:331
  47.0 0.5 collective-permute-start.11
  47.5 3.3 %apply_blocks.6 = (bf16[8,1024,256]{2,1,0:T(8,128)(2,1)}, f32[8,1024,256]{2,1,0:T(8,128)}) custom-call(s32[8,128]{1,0:T(8,128)S(1)} %broadcast_in_dim.31.modules_ref, bf16[8,1024,256]{2,1,0:T(8,128)(2,1)S(1)} %copy-done, f32[8,1024,256]{2,1,0:T(8,128)S(1)} %bitcast.4, bf16[512,256]{1,0:T(8,128)(2,1)S(1)} %multiply_convert_fusion.refs_0_, ...), custom_call_target="tpu_custom_call" | custom-call | bytes 6291456 | tf_op jit(solution)/shard_map/apply_blocks/pallas_call | solution.py:58
  50.8 0.3 collective-permute-done.19.refs_0_
  51.1 0.9 %collective-permute-start.21 = (bf16[512,256]{1,0:T(8,128)(2,1)S(1)}, bf16[512,256]{1,0:T(8,128)(2,1)S(1)}, u32[]{:S(2)}, u32[]{:S(2)}) collective-permute-start(bf16[512,256]{1,0:T(8,128)(2,1)S(1)} %collective-permute-done.19.refs_0_), channel_id=1, source_target_pairs={{0,8},{4,0},{8,16},{12,4},{16,24},{20,12},{24,28},{28,20},{1,9},{5... | collective-permute-start | bytes 786440 | tf_op jit(solution)/shard_map/ppermute | solution.py:331
  52.0 1.2 %collective-permute-start.22 = (bf16[512,256]{1,0:T(8,128)(2,1)S(1)}, bf16[512,256]{1,0:T(8,128)(2,1)S(1)}, u32[]{:S(2)}, u32[]{:S(2)}) collective-permute-start(bf16[512,256]{1,0:T(8,128)(2,1)S(1)} %collective-permute-done.20.refs_1_), channel_id=1, source_target_pairs={{0,4},{4,12},{8,0},{12,20},{16,8},{20,28},{24,16},{28,24},{1,5},{5... | collective-permute-start | bytes 786440 | tf_op jit(solution)/shard_map/ppermute | solution.py:331
  53.1 3.0 %collective-permute-done.10.refs_2_ = bf16[512,256]{1,0:T(8,128)(2,1)S(1)} collective-permute-done((bf16[512,256]{1,0:T(8,128)(2,1)S(1)}, bf16[512,256]{1,0:T(8,128)(2,1)S(1)}, u32[]{:S(2)}, u32[]{:S(2)}) %collective-permute-start.10) | collective-permute-done | bytes 262176 | tf_op jit(solution)/shard_map/ppermute | solution.py:331
  56.2 0.5 collective-permute-done.11.refs_3_
  56.7 1.6 %collective-permute-start.12 = (bf16[512,256]{1,0:T(8,128)(2,1)S(1)}, bf16[512,256]{1,0:T(8,128)(2,1)S(1)}, u32[]{:S(2)}, u32[]{:S(2)}) collective-permute-start(bf16[512,256]{1,0:T(8,128)(2,1)S(1)} %collective-permute-done.10.refs_2_), channel_id=1, source_target_pairs={{0,4},{4,12},{8,0},{12,20},{16,8},{20,28},{24,16},{28,24},{1,5},{5... | collective-permute-start | bytes 786440 | tf_op jit(solution)/shard_map/ppermute | solution.py:331
  58.3 0.5 collective-permute-start.14
  58.7 2.5 %apply_blocks.7 = (bf16[8,1024,256]{2,1,0:T(8,128)(2,1)}, f32[8,1024,256]{2,1,0:T(8,128)}) custom-call(s32[8,128]{1,0:T(8,128)S(1)} %broadcast_in_dim.31.modules_ref, bf16[8,1024,256]{2,1,0:T(8,128)(2,1)S(1)} %copy-done, f32[8,1024,256]{2,1,0:T(8,128)S(1)} %bitcast.4, ...), custom_call_target="tpu_custom_call", output_to_operand_aliasing={{0}: (7, {}), {1}: (8, {})} | custom-call | bytes 4194304 | tf_op jit(solution)/shard_map/apply_blocks/pallas_call | solution.py:58
  61.2 1.1 %collective-permute-done.21.refs_0_ = bf16[512,256]{1,0:T(8,128)(2,1)S(1)} collective-permute-done((bf16[512,256]{1,0:T(8,128)(2,1)S(1)}, bf16[512,256]{1,0:T(8,128)(2,1)S(1)}, u32[]{:S(2)}, u32[]{:S(2)}) %collective-permute-start.21) | collective-permute-done | bytes 262176 | tf_op jit(solution)/shard_map/ppermute | solution.py:331
  62.4 1.7 %apply_blocks.8 = (bf16[8,1024,256]{2,1,0:T(8,128)(2,1)}, f32[8,1024,256]{2,1,0:T(8,128)}) custom-call(s32[8,128]{1,0:T(8,128)S(1)} %broadcast_in_dim.31.modules_ref, bf16[8,1024,256]{2,1,0:T(8,128)(2,1)S(1)} %copy-done, f32[8,1024,256]{2,1,0:T(8,128)S(1)} %bitcast.4, ...), custom_call_target="tpu_custom_call", output_to_operand_aliasing={{0}: (5, {}), {1}: (6, {})} | custom-call | bytes 2097152 | tf_op jit(solution)/shard_map/apply_blocks/pallas_call | solution.py:58
  64.0 0.9 %collective-permute-start.23 = (bf16[256,256]{1,0:T(8,128)(2,1)S(1)}, bf16[256,256]{1,0:T(8,128)(2,1)S(1)}, u32[]{:S(2)}, u32[]{:S(2)}) collective-permute-start(bf16[256,256]{1,0:T(8,128)(2,1)S(1)} %slice.18), channel_id=1, source_target_pairs={{0,8},{4,0},{8,16},{12,4},{16,24},{20,12},{24,28},{28,20},{1,9},{5... | collective-permute-start | bytes 393224 | tf_op jit(solution)/shard_map/ppermute | solution.py:331
  64.9 1.2 %collective-permute-start.24 = (bf16[256,256]{1,0:T(8,128)(2,1)S(1)}, bf16[256,256]{1,0:T(8,128)(2,1)S(1)}, u32[]{:S(2)}, u32[]{:S(2)}) collective-permute-start(bf16[256,256]{1,0:T(8,128)(2,1)S(1)} %slice.19), channel_id=1, source_target_pairs={{0,4},{4,12},{8,0},{12,20},{16,8},{20,28},{24,16},{28,24},{1,5},{5... | collective-permute-start | bytes 393224 | tf_op jit(solution)/shard_map/ppermute | solution.py:331
  66.1 0.9 %collective-permute-done.12.refs_0_ = bf16[512,256]{1,0:T(8,128)(2,1)S(1)} collective-permute-done((bf16[512,256]{1,0:T(8,128)(2,1)S(1)}, bf16[512,256]{1,0:T(8,128)(2,1)S(1)}, u32[]{:S(2)}, u32[]{:S(2)}) %collective-permute-start.12) | collective-permute-done | bytes 262176 | tf_op jit(solution)/shard_map/ppermute | solution.py:331
  67.0 0.7 %collective-permute-start.13 = (bf16[256,256]{1,0:T(8,128)(2,1)S(1)}, bf16[256,256]{1,0:T(8,128)(2,1)S(1)}, u32[]{:S(2)}, u32[]{:S(2)}) collective-permute-start(bf16[256,256]{1,0:T(8,128)(2,1)S(1)} %slice.16), channel_id=1, source_target_pairs={{0,4},{4,12},{8,0},{12,20},{16,8},{20,28},{24,16},{28,24},{1,5},{5... | collective-permute-start | bytes 393224 | tf_op jit(solution)/shard_map/ppermute | solution.py:331
  67.8 1.4 %collective-permute-start.15 = (bf16[256,256]{1,0:T(8,128)(2,1)S(1)}, bf16[256,256]{1,0:T(8,128)(2,1)S(1)}, u32[]{:S(2)}, u32[]{:S(2)}) collective-permute-start(bf16[256,256]{1,0:T(8,128)(2,1)S(1)} %slice.17), channel_id=1, source_target_pairs={{0,8},{4,0},{8,16},{12,4},{16,24},{20,12},{24,28},{28,20},{1,9},{5... | collective-permute-start | bytes 393224 | tf_op jit(solution)/shard_map/ppermute | solution.py:331
  69.2 1.7 %apply_blocks.9 = (bf16[8,1024,256]{2,1,0:T(8,128)(2,1)}, f32[8,1024,256]{2,1,0:T(8,128)}) custom-call(s32[8,128]{1,0:T(8,128)S(1)} %broadcast_in_dim.31.modules_ref, bf16[8,1024,256]{2,1,0:T(8,128)(2,1)S(1)} %copy-done, f32[8,1024,256]{2,1,0:T(8,128)S(1)} %bitcast.4, ...), custom_call_target="tpu_custom_call", output_to_operand_aliasing={{0}: (5, {}), {1}: (6, {})} | custom-call | bytes 2097152 | tf_op jit(solution)/shard_map/apply_blocks/pallas_call | solution.py:58
  70.9 1.4 %apply_blocks.10 = (bf16[8,1024,256]{2,1,0:T(8,128)(2,1)}, f32[8,1024,256]{2,1,0:T(8,128)}) custom-call(s32[8,128]{1,0:T(8,128)S(1)} %broadcast_in_dim.31.modules_ref, bf16[8,1024,256]{2,1,0:T(8,128)(2,1)S(1)} %copy-done, f32[8,1024,256]{2,1,0:T(8,128)S(1)} %bitcast.4, ...), custom_call_target="tpu_custom_call", output_to_operand_aliasing={{0}: (5, {}), {1}: (6, {})} | custom-call | bytes 1048576 | tf_op jit(solution)/shard_map/apply_blocks/pallas_call | solution.py:58
  72.3 0.5 collective-permute-done.15.refs_1_
  72.8 1.4 %apply_blocks.11 = (bf16[8,1024,256]{2,1,0:T(8,128)(2,1)}, f32[8,1024,256]{2,1,0:T(8,128)}) custom-call(s32[8,128]{1,0:T(8,128)S(1)} %broadcast_in_dim.31.modules_ref, bf16[8,1024,256]{2,1,0:T(8,128)(2,1)S(1)} %copy-done, f32[8,1024,256]{2,1,0:T(8,128)S(1)} %bitcast.4, ...), custom_call_target="tpu_custom_call", output_to_operand_aliasing={{0}: (5, {}), {1}: (6, {})} | custom-call | bytes 1048576 | tf_op jit(solution)/shard_map/apply_blocks/pallas_call | solution.py:58
  (26 shorter events, 0.1 us)
Async XLA Ops:
  0.6 5.1 %copy-start.1 = (bf16[1,256,4096]{2,1,0:T(8,128)(2,1)S(1)}, bf16[1,256,4096]{2,1,0:T(8,128)(2,1)}, u32[]{:S(2)}) copy-start(bf16[1,256,4096]{2,1,0:T(8,128)(2,1)} %tokens_ref.5) | copy-start | bytes 6291460
  0.6 8.1 %copy-start.2 = (bf16[1,256,256]{2,1,0:T(8,128)(2,1)S(1)}, bf16[1,256,256]{2,1,0:T(8,128)(2,1)}, u32[]{:S(2)}) copy-start(bf16[1,256,256]{2,1,0:T(8,128)(2,1)} %param.7) | copy-start | bytes 393220
  0.6 0.8 %copy-start.3 = (s32[8,1]{0,1:T(1,128)S(1)}, s32[8,1]{0,1:T(1,128)}, u32[]{:S(2)}) copy-start(s32[8,1]{0,1:T(1,128)} %param.8) | copy-start | bytes 100
  1.5 6.6 %copy-start.5 = (s32[8]{0:T(128)S(1)}, s32[8]{0:T(128)}, u32[]{:S(2)}) copy-start(s32[8]{0:T(128)} %constant.28.clone) | copy-start | bytes 100
  1.5 8.2 %copy-start.4 = (s32[8,1]{0,1:T(1,128)S(1)}, s32[8,1]{0,1:T(1,128)}, u32[]{:S(2)}) copy-start(s32[8,1]{0,1:T(1,128)} %param.8) | copy-start | bytes 100
  2.7 14.9 %collective-permute-start.5 = (bf16[1024,256]{1,0:T(8,128)(2,1)S(1)}, bf16[1024,256]{1,0:T(8,128)(2,1)S(1)}, u32[]{:S(2)}, u32[]{:S(2)}) collective-permute-start(bf16[1024,256]{1,0:T(8,128)(2,1)S(1)} %pick_rows.1.after_ref.weights_ref), channel_id=1, source_target_pairs={{0,2},{1,3},{2,0},{3,1},{4,6},{5,7},{6,4},{7,5},{8,10},{9,11},{10,... | collective-permute-start | bytes 1572872 | tf_op jit(solution)/shard_map/ppermute | solution.py:236
  6.9 1.8 %collective-permute-start = (bf16[64,2048]{1,0:T(8,128)(2,1)}, bf16[64,2048]{1,0:T(8,128)(2,1)S(1)}, u32[]{:S(2)}, u32[]{:S(2)}) collective-permute-start(bf16[64,2048]{1,0:T(8,128)(2,1)} %get-tuple-element.45), channel_id=1, source_target_pairs={{0,1},{1,0},{2,3},{3,2},{4,5},{5,4},{6,7},{7,6},{8,9},{9,8},{10,11... | collective-permute-start | bytes 786440 | tf_op jit(solution)/shard_map/ppermute | solution.py:243
  7.0 2.9 %collective-permute-start.1 = (bf16[64,2048]{1,0:T(8,128)(2,1)}, bf16[64,2048]{1,0:T(8,128)(2,1)}, u32[]{:S(2)}, u32[]{:S(2)}) collective-permute-start(bf16[64,2048]{1,0:T(8,128)(2,1)} %get-tuple-element.46), channel_id=1, source_target_pairs={{0,1},{1,0},{2,3},{3,2},{4,5},{5,4},{6,7},{7,6},{8,9},{9,8},{10,11... | collective-permute-start | bytes 786440 | tf_op jit(solution)/shard_map/ppermute | solution.py:243
  7.5 2.4 %collective-permute-start.2 = (bf16[64,2048]{1,0:T(8,128)(2,1)}, bf16[64,2048]{1,0:T(8,128)(2,1)}, u32[]{:S(2)}, u32[]{:S(2)}) collective-permute-start(bf16[64,2048]{1,0:T(8,128)(2,1)} %get-tuple-element.47), channel_id=1, source_target_pairs={{0,1},{1,0},{2,3},{3,2},{4,5},{5,4},{6,7},{7,6},{8,9},{9,8},{10,11... | collective-permute-start | bytes 786440 | tf_op jit(solution)/shard_map/ppermute | solution.py:243
  7.6 2.4 %collective-permute-start.3 = (bf16[64,2048]{1,0:T(8,128)(2,1)}, bf16[64,2048]{1,0:T(8,128)(2,1)}, u32[]{:S(2)}, u32[]{:S(2)}) collective-permute-start(bf16[64,2048]{1,0:T(8,128)(2,1)} %get-tuple-element.48), channel_id=1, source_target_pairs={{0,1},{1,0},{2,3},{3,2},{4,5},{5,4},{6,7},{7,6},{8,9},{9,8},{10,11... | collective-permute-start | bytes 786440 | tf_op jit(solution)/shard_map/ppermute | solution.py:243
  8.8 3.2 %collective-permute-start.4 = (bf16[256,256]{1,0:T(8,128)(2,1)S(1)}, bf16[256,256]{1,0:T(8,128)(2,1)S(1)}, u32[]{:S(2)}, u32[]{:S(2)}) collective-permute-start(bf16[256,256]{1,0:T(8,128)(2,1)S(1)} %bitcast.5), channel_id=1, source_target_pairs={{0,1},{1,0},{2,3},{3,2},{4,5},{5,4},{6,7},{7,6},{8,9},{9,8},{10,11... | collective-permute-start | bytes 393224 | tf_op jit(solution)/shard_map/ppermute | solution.py:242
  10.0 37.5 %slice-start = ((s8[8388608]{0:T(1024)(128)(4,1)}), s8[4194304]{0:T(1024)(128)(4,1)S(1)}, s32[]{:S(2)}) async-start(s8[8388608]{0:T(1024)(128)(4,1)} %bitcast.3), calls=%async_computation | async-start | bytes 8388608
  18.1 29.4 %slice-start.1 = ((s8[8388608]{0:T(1024)(128)(4,1)}), s8[4194304]{0:T(1024)(128)(4,1)S(1)}, s32[]{:S(2)}) async-start(s8[8388608]{0:T(1024)(128)(4,1)} %bitcast.3), calls=%async_computation.1 | async-start | bytes 8388608
  18.1 29.4 %copy-start = (bf16[8,1024,256]{2,1,0:T(8,128)(2,1)S(1)}, bf16[8,1024,256]{2,1,0:T(8,128)(2,1)}, u32[]{:S(2)}) copy-start(bf16[8,1024,256]{2,1,0:T(8,128)(2,1)} %weights_ref.13) | copy-start | bytes 12582916
  18.1 1.6 %collective-permute-start.6 = (bf16[512,256]{1,0:T(8,128)(2,1)S(1)}, bf16[512,256]{1,0:T(8,128)(2,1)S(1)}, u32[]{:S(2)}, u32[]{:S(2)}) collective-permute-start(bf16[512,256]{1,0:T(8,128)(2,1)S(1)} %convert_element_type.15), channel_id=1, source_target_pairs={{0,1},{1,0},{2,3},{3,2},{4,5},{5,4},{6,7},{7,6},{8,9},{9,8},{10,11... | collective-permute-start | bytes 786440 | tf_op jit(solution)/shard_map/ppermute | solution.py:260
  20.3 9.2 %collective-permute-start.16 = (bf16[512,256]{1,0:T(8,128)(2,1)S(1)}, bf16[512,256]{1,0:T(8,128)(2,1)S(1)}, u32[]{:S(2)}, u32[]{:S(2)}) collective-permute-start(bf16[512,256]{1,0:T(8,128)(2,1)S(1)} %get-tuple-element.65), channel_id=1, source_target_pairs={{0,2},{1,3},{2,0},{3,1},{4,6},{5,7},{6,4},{7,5},{8,10},{9,11},{10,... | collective-permute-start | bytes 786440 | tf_op jit(solution)/shard_map/ppermute | solution.py:284
  22.7 11.7 %collective-permute-start.7 = (bf16[512,256]{1,0:T(8,128)(2,1)S(1)}, bf16[512,256]{1,0:T(8,128)(2,1)S(1)}, u32[]{:S(2)}, u32[]{:S(2)}) collective-permute-start(bf16[512,256]{1,0:T(8,128)(2,1)S(1)} %get-tuple-element.57), channel_id=1, source_target_pairs={{0,2},{1,3},{2,0},{3,1},{4,6},{5,7},{6,4},{7,5},{8,10},{9,11},{10,... | collective-permute-start | bytes 786440 | tf_op jit(solution)/shard_map/ppermute | solution.py:284
  29.6 6.9 %collective-permute-start.17 = (bf16[512,256]{1,0:T(8,128)(2,1)S(1)}, bf16[512,256]{1,0:T(8,128)(2,1)S(1)}, u32[]{:S(2)}, u32[]{:S(2)}) collective-permute-start(bf16[512,256]{1,0:T(8,128)(2,1)S(1)} %multiply_convert_fusion.refs_0_), channel_id=1, source_target_pairs={{0,8},{4,0},{8,16},{12,4},{16,24},{20,12},{24,28},{28,20},{1,9},{5... | collective-permute-start | bytes 786440 | tf_op jit(solution)/shard_map/ppermute | solution.py:331
  31.5 7.8 %collective-permute-start.18 = (bf16[512,256]{1,0:T(8,128)(2,1)S(1)}, bf16[512,256]{1,0:T(8,128)(2,1)S(1)}, u32[]{:S(2)}, u32[]{:S(2)}) collective-permute-start(bf16[512,256]{1,0:T(8,128)(2,1)S(1)} %multiply_convert_fusion.refs_0_), channel_id=1, source_target_pairs={{0,4},{4,12},{8,0},{12,20},{16,8},{20,28},{24,16},{28,24},{1,5},{5... | collective-permute-start | bytes 786440 | tf_op jit(solution)/shard_map/ppermute | solution.py:331
  34.4 10.5 %collective-permute-start.8 = (bf16[512,256]{1,0:T(8,128)(2,1)S(1)}, bf16[512,256]{1,0:T(8,128)(2,1)S(1)}, u32[]{:S(2)}, u32[]{:S(2)}) collective-permute-start(bf16[512,256]{1,0:T(8,128)(2,1)S(1)} %multiply_convert_fusion.1.refs_3_), channel_id=1, source_target_pairs={{0,4},{4,12},{8,0},{12,20},{16,8},{20,28},{24,16},{28,24},{1,5},{5... | collective-permute-start | bytes 786440 | tf_op jit(solution)/shard_map/ppermute | solution.py:331
  36.2 9.2 %collective-permute-start.9 = (bf16[512,256]{1,0:T(8,128)(2,1)S(1)}, bf16[512,256]{1,0:T(8,128)(2,1)S(1)}, u32[]{:S(2)}, u32[]{:S(2)}) collective-permute-start(bf16[512,256]{1,0:T(8,128)(2,1)S(1)} %multiply_convert_fusion.1.refs_3_), channel_id=1, source_target_pairs={{0,8},{4,0},{8,16},{12,4},{16,24},{20,12},{24,28},{28,20},{1,9},{5... | collective-permute-start | bytes 786440 | tf_op jit(solution)/shard_map/ppermute | solution.py:331
  39.3 11.8 %collective-permute-start.19 = (bf16[512,256]{1,0:T(8,128)(2,1)S(1)}, bf16[512,256]{1,0:T(8,128)(2,1)S(1)}, u32[]{:S(2)}, u32[]{:S(2)}) collective-permute-start(bf16[512,256]{1,0:T(8,128)(2,1)S(1)} %collective-permute-done.17.refs_1_), channel_id=1, source_target_pairs={{0,8},{4,0},{8,16},{12,4},{16,24},{20,12},{24,28},{28,20},{1,9},{5... | collective-permute-start | bytes 786440 | tf_op jit(solution)/shard_map/ppermute | solution.py:331
  40.7 10.4 %collective-permute-start.20 = (bf16[512,256]{1,0:T(8,128)(2,1)S(1)}, bf16[512,256]{1,0:T(8,128)(2,1)S(1)}, u32[]{:S(2)}, u32[]{:S(2)}) collective-permute-start(bf16[512,256]{1,0:T(8,128)(2,1)S(1)} %collective-permute-done.18.refs_2_), channel_id=1, source_target_pairs={{0,4},{4,12},{8,0},{12,20},{16,8},{20,28},{24,16},{28,24},{1,5},{5... | collective-permute-start | bytes 786440 | tf_op jit(solution)/shard_map/ppermute | solution.py:331
  45.5 10.7 %collective-permute-start.10 = (bf16[512,256]{1,0:T(8,128)(2,1)S(1)}, bf16[512,256]{1,0:T(8,128)(2,1)S(1)}, u32[]{:S(2)}, u32[]{:S(2)}) collective-permute-start(bf16[512,256]{1,0:T(8,128)(2,1)S(1)} %collective-permute-done.8.refs_4_), channel_id=1, source_target_pairs={{0,4},{4,12},{8,0},{12,20},{16,8},{20,28},{24,16},{28,24},{1,5},{5... | collective-permute-start | bytes 786440 | tf_op jit(solution)/shard_map/ppermute | solution.py:331
  47.0 9.7 %collective-permute-start.11 = (bf16[512,256]{1,0:T(8,128)(2,1)S(1)}, bf16[512,256]{1,0:T(8,128)(2,1)S(1)}, u32[]{:S(2)}, u32[]{:S(2)}) collective-permute-start(bf16[512,256]{1,0:T(8,128)(2,1)S(1)} %collective-permute-done.9.refs_5_), channel_id=1, source_target_pairs={{0,8},{4,0},{8,16},{12,4},{16,24},{20,12},{24,28},{28,20},{1,9},{5... | collective-permute-start | bytes 786440 | tf_op jit(solution)/shard_map/ppermute | solution.py:331
  51.1 11.2 %collective-permute-start.21 = (bf16[512,256]{1,0:T(8,128)(2,1)S(1)}, bf16[512,256]{1,0:T(8,128)(2,1)S(1)}, u32[]{:S(2)}, u32[]{:S(2)}) collective-permute-start(bf16[512,256]{1,0:T(8,128)(2,1)S(1)} %collective-permute-done.19.refs_0_), channel_id=1, source_target_pairs={{0,8},{4,0},{8,16},{12,4},{16,24},{20,12},{24,28},{28,20},{1,9},{5... | collective-permute-start | bytes 786440 | tf_op jit(solution)/shard_map/ppermute | solution.py:331
  52.0 10.4 %collective-permute-start.22 = (bf16[512,256]{1,0:T(8,128)(2,1)S(1)}, bf16[512,256]{1,0:T(8,128)(2,1)S(1)}, u32[]{:S(2)}, u32[]{:S(2)}) collective-permute-start(bf16[512,256]{1,0:T(8,128)(2,1)S(1)} %collective-permute-done.20.refs_1_), channel_id=1, source_target_pairs={{0,4},{4,12},{8,0},{12,20},{16,8},{20,28},{24,16},{28,24},{1,5},{5... | collective-permute-start | bytes 786440 | tf_op jit(solution)/shard_map/ppermute | solution.py:331
  56.7 10.3 %collective-permute-start.12 = (bf16[512,256]{1,0:T(8,128)(2,1)S(1)}, bf16[512,256]{1,0:T(8,128)(2,1)S(1)}, u32[]{:S(2)}, u32[]{:S(2)}) collective-permute-start(bf16[512,256]{1,0:T(8,128)(2,1)S(1)} %collective-permute-done.10.refs_2_), channel_id=1, source_target_pairs={{0,4},{4,12},{8,0},{12,20},{16,8},{20,28},{24,16},{28,24},{1,5},{5... | collective-permute-start | bytes 786440 | tf_op jit(solution)/shard_map/ppermute | solution.py:331
  58.3 9.5 %collective-permute-start.14 = (bf16[512,256]{1,0:T(8,128)(2,1)S(1)}, bf16[512,256]{1,0:T(8,128)(2,1)S(1)}, u32[]{:S(2)}, u32[]{:S(2)}) collective-permute-start(bf16[512,256]{1,0:T(8,128)(2,1)S(1)} %collective-permute-done.11.refs_3_), channel_id=1, source_target_pairs={{0,8},{4,0},{8,16},{12,4},{16,24},{20,12},{24,28},{28,20},{1,9},{5... | collective-permute-start | bytes 786440 | tf_op jit(solution)/shard_map/ppermute | solution.py:331
  64.0 6.8 %collective-permute-start.23 = (bf16[256,256]{1,0:T(8,128)(2,1)S(1)}, bf16[256,256]{1,0:T(8,128)(2,1)S(1)}, u32[]{:S(2)}, u32[]{:S(2)}) collective-permute-start(bf16[256,256]{1,0:T(8,128)(2,1)S(1)} %slice.18), channel_id=1, source_target_pairs={{0,8},{4,0},{8,16},{12,4},{16,24},{20,12},{24,28},{28,20},{1,9},{5... | collective-permute-start | bytes 393224 | tf_op jit(solution)/shard_map/ppermute | solution.py:331
  64.9 5.9 %collective-permute-start.24 = (bf16[256,256]{1,0:T(8,128)(2,1)S(1)}, bf16[256,256]{1,0:T(8,128)(2,1)S(1)}, u32[]{:S(2)}, u32[]{:S(2)}) collective-permute-start(bf16[256,256]{1,0:T(8,128)(2,1)S(1)} %slice.19), channel_id=1, source_target_pairs={{0,4},{4,12},{8,0},{12,20},{16,8},{20,28},{24,16},{28,24},{1,5},{5... | collective-permute-start | bytes 393224 | tf_op jit(solution)/shard_map/ppermute | solution.py:331
  67.0 5.2 %collective-permute-start.13 = (bf16[256,256]{1,0:T(8,128)(2,1)S(1)}, bf16[256,256]{1,0:T(8,128)(2,1)S(1)}, u32[]{:S(2)}, u32[]{:S(2)}) collective-permute-start(bf16[256,256]{1,0:T(8,128)(2,1)S(1)} %slice.16), channel_id=1, source_target_pairs={{0,4},{4,12},{8,0},{12,20},{16,8},{20,28},{24,16},{28,24},{1,5},{5... | collective-permute-start | bytes 393224 | tf_op jit(solution)/shard_map/ppermute | solution.py:331
  67.8 5.0 %collective-permute-start.15 = (bf16[256,256]{1,0:T(8,128)(2,1)S(1)}, bf16[256,256]{1,0:T(8,128)(2,1)S(1)}, u32[]{:S(2)}, u32[]{:S(2)}) collective-permute-start(bf16[256,256]{1,0:T(8,128)(2,1)S(1)} %slice.17), channel_id=1, source_target_pairs={{0,8},{4,0},{8,16},{12,4},{16,24},{20,12},{24,28},{28,20},{1,9},{5... | collective-permute-start | bytes 393224 | tf_op jit(solution)/shard_map/ppermute | solution.py:331

commit v7 on v6

--- a/solution.py
+++ b/solution.py
@@ -133,13 +133,16 @@
         turned_ref[spot, tok:] = taken_ref[:, spot].T
 
 
-def next_products(step, tokens_ref, taken_ref, weights_ref, sum_ref, out_ref):
+def next_products(step, tokens_ref, taken_ref, weights_ref, sum_ref, out_ref, rounded_ref):
     tok = taken_ref.shape[0]
     chips = taken_ref.shape[1] // weights_ref.shape[0]
     block = lax.rem(core_and_chip()[1] + chips - step, chips)
     a, b = products(tokens_ref, taken_ref, weights_ref, block)
-    out_ref[:tok] = sum_ref[:tok] + a
-    out_ref[tok:] = sum_ref[tok:] + b
+    a, b = sum_ref[:tok] + a, sum_ref[tok:] + b
+    out_ref[:tok] = a
+    out_ref[tok:] = b
+    rounded_ref[:tok] = a.astype(rounded_ref.dtype)
+    rounded_ref[tok:] = b.astype(rounded_ref.dtype)
 
 
 def cotangent_of(latent, upstream):
@@ -252,12 +255,14 @@
     )
     modules = modules_on_ring(table, path_id)
     partial, modules, other_up = lax.optimization_barrier((partial, modules, other_up))
+    rounded = partial.astype(bf16)
     for s in range(1, chips):
-        partial = call(
-            functools.partial(next_products, s), shape(partial.shape, f32),
-            [VMEM] * 4, VMEM, (tokens, taken, lent_weights[s - 1], partial),
+        partial, rounded = call(
+            functools.partial(next_products, s),
+            [shape(partial.shape, f32), shape(partial.shape, bf16)],
+            [VMEM] * 4, [VMEM] * 2, (tokens, taken, lent_weights[s - 1], partial),
         )
-    other = lax.ppermute(partial.astype(bf16), "fsdp", to_core)
+    other = lax.ppermute(rounded, "fsdp", to_core)
     chains = cuts(rows)
 
     def outputs(wanted):
@@ -326,7 +331,7 @@
                 waiting[0] = []
             if step > 2 and c == 0:
                 pair, outs = lax.optimization_barrier((pair, outs))
-            elif not last:
+            elif step < 2:
                 pair = lax.optimization_barrier(tuple(pair))
             moving[c] = [lax.ppermute(b, "path", pairs[way]) for b, way in zip(pair, ways)]
             if step > 1 and c == 0 and not last:

time: 74.3 us -> 74.3 us (level)
  transfers between devices with their start and end apart: 25 -> 25, of which waited for: 14 -> 13; matrix products, arithmetic and copies ran while one was open for 3% -> 2% of each run, Pallas kernels for 19% -> 19%
where the time goes in v7:
time: 74.3 us; the launch traced here: 74.1 us
  waiting for transfers between devices  30.2 us (41%)
  starting transfers between devices  22.7 us (31%)
  Pallas kernels  17.8 us (24%)
  other arithmetic  1.59 us (2%)
  local copies, waits for them, and re-layouts  0.94 us (1%)
  between operations  0.87 us (1%)
    pallas_call x12, Pallas kernels, call(): pl.pallas_call(kernel, in_specs=in_specs, out_specs=out_specs, out_shape=...  17.8 us
    ppermute x16, starting transfers between devices, body(): lax.ppermute(b, 'path', pairs[way])  16.3 us
    ppermute x16, waiting for transfers between devices, body(): lax.ppermute(b, 'path', pairs[way])  13.6 us
    ppermute x2, waiting for transfers between devices, body(): lax.ppermute(gradients[s, c], 'fsdp', to_chip(s)).astype(f32)  9.14 us
    ppermute x1, waiting for transfers between devices, body(): lax.ppermute(own_weights, 'fsdp', to_chip(s))  5.58 us
    ppermute x1, starting transfers between devices, body(): lax.ppermute(own_weights, 'fsdp', to_chip(s))  3 us
    ppermute x2, starting transfers between devices, body(): lax.ppermute(gradients[s, c], 'fsdp', to_chip(s)).astype(f32)  2.16 us
    ppermute x1, waiting for transfers between devices, body(): other = lax.ppermute(rounded, 'fsdp', to_core)  1.52 us
  transfers between devices with their start and end apart: 25, of which 13 were waited for; matrix products, arithmetic and copies ran while one was open for 2% of the time, Pallas kernels for 19%

profile of v7, /device:TPU:0, one launch (start us, length us, event | category | flops | bytes accessed | tf_op | source)
XLA Modules:
  0.0 74.1 jit_solution(5834644551152947024)
XLA Ops:
  0.7 0.8 %copy-done.3 = s32[8,1]{0,1:T(1,128)S(1)} copy-done((s32[8,1]{0,1:T(1,128)S(1)}, s32[8,1]{0,1:T(1,128)}, u32[]{:S(2)}) %copy-start.3) | copy-done | bytes 56
  1.5 1.2 %pick_rows.1.after_ref.weights_ref = bf16[1024,256]{1,0:T(8,128)(2,1)S(1)} custom-call(s32[1,8]{1,0:T(1,128)S(1)} %bitcast.7, bf16[8,1024,256]{2,1,0:T(8,128)(2,1)} %weights_ref.13), custom_call_target="tpu_custom_call" | custom-call | tf_op jit(solution)/shard_map/pick_rows/pallas_call | solution.py:58
  2.7 3.0 %collective-permute-start.5 = (bf16[1024,256]{1,0:T(8,128)(2,1)S(1)}, bf16[1024,256]{1,0:T(8,128)(2,1)S(1)}, u32[]{:S(2)}, u32[]{:S(2)}) collective-permute-start(bf16[1024,256]{1,0:T(8,128)(2,1)S(1)} %pick_rows.1.after_ref.weights_ref), channel_id=1, source_target_pairs={{0,2},{1,3},{2,0},{3,1},{4,6},{5,7},{6,4},{7,5},{8,10},{9,11},{10,... | collective-permute-start | bytes 1572872 | tf_op jit(solution)/shard_map/ppermute | solution.py:239
  5.7 1.2 %pick_columns.1 = (bf16[64,2048]{1,0:T(8,128)(2,1)}, bf16[64,2048]{1,0:T(8,128)(2,1)}, bf16[64,2048]{1,0:T(8,128)(2,1)}, bf16[64,2048]{1,0:T(8,128)(2,1)}) custom-call(bf16[1,256,4096]{2,1,0:T(8,128)(2,1)S(1)} %copy-done.1, bf16[1024,256]{1,0:T(8,128)(2,1)S(1)} %pick_rows.1.after_ref.weights_ref), custom_call_target="tpu_custom_call" | custom-call | tf_op jit(solution)/shard_map/pick_columns/pallas_call | solution.py:58
  7.0 0.1 collective-permute-start
  7.0 0.5 collective-permute-start.1
  7.5 0.1 collective-permute-start.2
  7.6 0.4 collective-permute-start.3
  8.0 0.6 fusion.5
  8.6 0.1 collective-permute-done.refs_0_
  8.8 0.1 collective-permute-start.4
  8.9 0.7 select_reduce_fusion.1
  9.6 0.2 select_reduce_fusion
  9.8 0.0 collective-permute-done.1.refs_1_
  9.8 0.0 collective-permute-done.2.refs_2_
  9.8 0.3 collective-permute-done.3.refs_3_
  10.0 2.0 %first_products.1 = (f32[512,256]{1,0:T(8,128)S(1)}, bf16[2048,512]{1,0:T(8,128)(2,1)S(1)}, bf16[256,2048]{1,0:T(8,128)(2,1)S(1)}) custom-call(bf16[1,256,4096]{2,1,0:T(8,128)(2,1)S(1)} %copy-done.1, bf16[1024,256]{1,0:T(8,128)(2,1)S(1)} %pick_rows.1.after_ref.weights_ref, bf16[64,2048]{1,0:T(8,128)(2,1)S(1)} %collective-permute-done.refs_0_, ...), custom_call_target="tpu_custom_call" | custom-call | tf_op jit(solution)/shard_map/first_products/pallas_call | solution.py:58
  12.0 0.0 collective-permute-done.4.other_up_ref
  12.0 0.1 broadcast_in_dim.31.modules_ref
  12.1 5.6 %collective-permute-done.5.weights_ref = bf16[1024,256]{1,0:T(8,128)(2,1)S(1)} collective-permute-done((bf16[1024,256]{1,0:T(8,128)(2,1)S(1)}, bf16[1024,256]{1,0:T(8,128)(2,1)S(1)}, u32[]{:S(2)}, u32[]{:S(2)}) %collective-permute-start.5) | collective-permute-done | bytes 524320 | tf_op jit(solution)/shard_map/ppermute | solution.py:239
  17.6 0.4 next_products.1
  18.1 0.0 copy-start
  18.1 0.1 collective-permute-start.6
  18.2 1.5 %collective-permute-done.6.other_ref = bf16[512,256]{1,0:T(8,128)(2,1)S(1)} collective-permute-done((bf16[512,256]{1,0:T(8,128)(2,1)S(1)}, bf16[512,256]{1,0:T(8,128)(2,1)S(1)}, u32[]{:S(2)}, u32[]{:S(2)}) %collective-permute-start.6) | collective-permute-done | bytes 262176 | tf_op jit(solution)/shard_map/ppermute | solution.py:265
  19.7 0.5 first_gradients.1
  20.2 1.8 %collective-permute-start.16 = (bf16[512,256]{1,0:T(8,128)(2,1)S(1)}, bf16[512,256]{1,0:T(8,128)(2,1)S(1)}, u32[]{:S(2)}, u32[]{:S(2)}) collective-permute-start(bf16[512,256]{1,0:T(8,128)(2,1)S(1)} %get-tuple-element.59), channel_id=1, source_target_pairs={{0,2},{1,3},{2,0},{3,1},{4,6},{5,7},{6,4},{7,5},{8,10},{9,11},{10,... | collective-permute-start | bytes 786440 | tf_op jit(solution)/shard_map/ppermute | solution.py:289
  22.1 0.6 more_gradients.1
  22.6 0.3 collective-permute-start.7
  23.0 6.5 %collective-permute-done.16 = bf16[512,256]{1,0:T(8,128)(2,1)S(1)} collective-permute-done((bf16[512,256]{1,0:T(8,128)(2,1)S(1)}, bf16[512,256]{1,0:T(8,128)(2,1)S(1)}, u32[]{:S(2)}, u32[]{:S(2)}) %collective-permute-start.16) | collective-permute-done | bytes 262176 | tf_op jit(solution)/shard_map/ppermute | solution.py:289
  29.5 0.1 multiply_convert_fusion.refs_0_
  29.5 1.9 %collective-permute-start.17 = (bf16[512,256]{1,0:T(8,128)(2,1)S(1)}, bf16[512,256]{1,0:T(8,128)(2,1)S(1)}, u32[]{:S(2)}, u32[]{:S(2)}) collective-permute-start(bf16[512,256]{1,0:T(8,128)(2,1)S(1)} %multiply_convert_fusion.refs_0_), channel_id=1, source_target_pairs={{0,8},{4,0},{8,16},{12,4},{16,24},{20,12},{24,28},{28,20},{1,9},{5... | collective-permute-start | bytes 786440 | tf_op jit(solution)/shard_map/ppermute | solution.py:336
  31.4 0.2 collective-permute-start.19
  31.6 2.7 %collective-permute-done.7 = bf16[512,256]{1,0:T(8,128)(2,1)S(1)} collective-permute-done((bf16[512,256]{1,0:T(8,128)(2,1)S(1)}, bf16[512,256]{1,0:T(8,128)(2,1)S(1)}, u32[]{:S(2)}, u32[]{:S(2)}) %collective-permute-start.7) | collective-permute-done | bytes 262176 | tf_op jit(solution)/shard_map/ppermute | solution.py:289
  34.3 0.1 multiply_convert_fusion.1.refs_3_
  34.4 1.8 %collective-permute-start.8 = (bf16[512,256]{1,0:T(8,128)(2,1)S(1)}, bf16[512,256]{1,0:T(8,128)(2,1)S(1)}, u32[]{:S(2)}, u32[]{:S(2)}) collective-permute-start(bf16[512,256]{1,0:T(8,128)(2,1)S(1)} %multiply_convert_fusion.1.refs_3_), channel_id=1, source_target_pairs={{0,4},{4,12},{8,0},{12,20},{16,8},{20,28},{24,16},{28,24},{1,5},{5... | collective-permute-start | bytes 786440 | tf_op jit(solution)/shard_map/ppermute | solution.py:336
  36.2 0.3 collective-permute-start.12
  36.4 0.0 collective-permute-done.17.refs_1_
  36.4 1.8 %collective-permute-start.18 = (bf16[512,256]{1,0:T(8,128)(2,1)S(1)}, bf16[512,256]{1,0:T(8,128)(2,1)S(1)}, u32[]{:S(2)}, u32[]{:S(2)}) collective-permute-start(bf16[512,256]{1,0:T(8,128)(2,1)S(1)} %collective-permute-done.17.refs_1_), channel_id=1, source_target_pairs={{0,8},{4,0},{8,16},{12,4},{16,24},{20,12},{24,28},{28,20},{1,9},{5... | collective-permute-start | bytes 786440 | tf_op jit(solution)/shard_map/ppermute | solution.py:336
  38.3 1.0 %collective-permute-done.19.refs_2_ = bf16[512,256]{1,0:T(8,128)(2,1)S(1)} collective-permute-done((bf16[512,256]{1,0:T(8,128)(2,1)S(1)}, bf16[512,256]{1,0:T(8,128)(2,1)S(1)}, u32[]{:S(2)}, u32[]{:S(2)}) %collective-permute-start.19) | collective-permute-done | bytes 262176 | tf_op jit(solution)/shard_map/ppermute | solution.py:336
  39.3 0.0 collective-permute-start.20
  39.3 5.6 %collective-permute-done.8.refs_4_ = bf16[512,256]{1,0:T(8,128)(2,1)S(1)} collective-permute-done((bf16[512,256]{1,0:T(8,128)(2,1)S(1)}, bf16[512,256]{1,0:T(8,128)(2,1)S(1)}, u32[]{:S(2)}, u32[]{:S(2)}) %collective-permute-start.8) | collective-permute-done | bytes 262176 | tf_op jit(solution)/shard_map/ppermute | solution.py:336
  44.9 0.5 collective-permute-start.9
  45.4 0.0 collective-permute-done.12.refs_5_
  45.4 1.5 %collective-permute-start.13 = (bf16[512,256]{1,0:T(8,128)(2,1)S(1)}, bf16[512,256]{1,0:T(8,128)(2,1)S(1)}, u32[]{:S(2)}, u32[]{:S(2)}) collective-permute-start(bf16[512,256]{1,0:T(8,128)(2,1)S(1)} %collective-permute-done.12.refs_5_), channel_id=1, source_target_pairs={{0,8},{4,0},{8,16},{12,4},{16,24},{20,12},{24,28},{28,20},{1,9},{5... | collective-permute-start | bytes 786440 | tf_op jit(solution)/shard_map/ppermute | solution.py:336
  46.9 3.3 %apply_blocks.6 = (bf16[8,1024,256]{2,1,0:T(8,128)(2,1)}, f32[8,1024,256]{2,1,0:T(8,128)}) custom-call(s32[8,128]{1,0:T(8,128)S(1)} %broadcast_in_dim.31.modules_ref, bf16[8,1024,256]{2,1,0:T(8,128)(2,1)S(1)} %copy-done, f32[8,1024,256]{2,1,0:T(8,128)S(1)} %bitcast.4, bf16[512,256]{1,0:T(8,128)(2,1)S(1)} %multiply_convert_fusion.refs_0_, ...), custom_call_target="tpu_custom_call" | custom-call | bytes 6291456 | tf_op jit(solution)/shard_map/apply_blocks/pallas_call | solution.py:58
  50.2 0.8 %collective-permute-done.18.refs_0_ = bf16[512,256]{1,0:T(8,128)(2,1)S(1)} collective-permute-done((bf16[512,256]{1,0:T(8,128)(2,1)S(1)}, bf16[512,256]{1,0:T(8,128)(2,1)S(1)}, u32[]{:S(2)}, u32[]{:S(2)}) %collective-permute-start.18) | collective-permute-done | bytes 262176 | tf_op jit(solution)/shard_map/ppermute | solution.py:336
  51.0 0.9 %collective-permute-start.21 = (bf16[512,256]{1,0:T(8,128)(2,1)S(1)}, bf16[512,256]{1,0:T(8,128)(2,1)S(1)}, u32[]{:S(2)}, u32[]{:S(2)}) collective-permute-start(bf16[512,256]{1,0:T(8,128)(2,1)S(1)} %collective-permute-done.18.refs_0_), channel_id=1, source_target_pairs={{0,8},{4,0},{8,16},{12,4},{16,24},{20,12},{24,28},{28,20},{1,9},{5... | collective-permute-start | bytes 786440 | tf_op jit(solution)/shard_map/ppermute | solution.py:336
  51.9 1.2 %collective-permute-start.22 = (bf16[512,256]{1,0:T(8,128)(2,1)S(1)}, bf16[512,256]{1,0:T(8,128)(2,1)S(1)}, u32[]{:S(2)}, u32[]{:S(2)}) collective-permute-start(bf16[512,256]{1,0:T(8,128)(2,1)S(1)} %collective-permute-done.20.refs_1_), channel_id=1, source_target_pairs={{0,4},{4,12},{8,0},{12,20},{16,8},{20,28},{24,16},{28,24},{1,5},{5... | collective-permute-start | bytes 786440 | tf_op jit(solution)/shard_map/ppermute | solution.py:336
  53.1 3.0 %collective-permute-done.9.refs_2_ = bf16[512,256]{1,0:T(8,128)(2,1)S(1)} collective-permute-done((bf16[512,256]{1,0:T(8,128)(2,1)S(1)}, bf16[512,256]{1,0:T(8,128)(2,1)S(1)}, u32[]{:S(2)}, u32[]{:S(2)}) %collective-permute-start.9) | collective-permute-done | bytes 262176 | tf_op jit(solution)/shard_map/ppermute | solution.py:336
  56.1 0.5 collective-permute-start.10
  56.7 1.5 %collective-permute-start.14 = (bf16[512,256]{1,0:T(8,128)(2,1)S(1)}, bf16[512,256]{1,0:T(8,128)(2,1)S(1)}, u32[]{:S(2)}, u32[]{:S(2)}) collective-permute-start(bf16[512,256]{1,0:T(8,128)(2,1)S(1)} %collective-permute-done.13.refs_3_), channel_id=1, source_target_pairs={{0,8},{4,0},{8,16},{12,4},{16,24},{20,12},{24,28},{28,20},{1,9},{5... | collective-permute-start | bytes 786440 | tf_op jit(solution)/shard_map/ppermute | solution.py:336
  58.1 2.5 %apply_blocks.7 = (bf16[8,1024,256]{2,1,0:T(8,128)(2,1)}, f32[8,1024,256]{2,1,0:T(8,128)}) custom-call(s32[8,128]{1,0:T(8,128)S(1)} %broadcast_in_dim.31.modules_ref, bf16[8,1024,256]{2,1,0:T(8,128)(2,1)S(1)} %copy-done, f32[8,1024,256]{2,1,0:T(8,128)S(1)} %bitcast.4, ...), custom_call_target="tpu_custom_call", output_to_operand_aliasing={{0}: (7, {}), {1}: (8, {})} | custom-call | bytes 4194304 | tf_op jit(solution)/shard_map/apply_blocks/pallas_call | solution.py:58
  60.6 1.6 %collective-permute-done.21.refs_0_ = bf16[512,256]{1,0:T(8,128)(2,1)S(1)} collective-permute-done((bf16[512,256]{1,0:T(8,128)(2,1)S(1)}, bf16[512,256]{1,0:T(8,128)(2,1)S(1)}, u32[]{:S(2)}, u32[]{:S(2)}) %collective-permute-start.21) | collective-permute-done | bytes 262176 | tf_op jit(solution)/shard_map/ppermute | solution.py:336
  62.3 1.7 %apply_blocks.8 = (bf16[8,1024,256]{2,1,0:T(8,128)(2,1)}, f32[8,1024,256]{2,1,0:T(8,128)}) custom-call(s32[8,128]{1,0:T(8,128)S(1)} %broadcast_in_dim.31.modules_ref, bf16[8,1024,256]{2,1,0:T(8,128)(2,1)S(1)} %copy-done, f32[8,1024,256]{2,1,0:T(8,128)S(1)} %bitcast.4, ...), custom_call_target="tpu_custom_call", output_to_operand_aliasing={{0}: (5, {}), {1}: (6, {})} | custom-call | bytes 2097152 | tf_op jit(solution)/shard_map/apply_blocks/pallas_call | solution.py:58
  64.0 0.9 %collective-permute-start.23 = (bf16[256,256]{1,0:T(8,128)(2,1)S(1)}, bf16[256,256]{1,0:T(8,128)(2,1)S(1)}, u32[]{:S(2)}, u32[]{:S(2)}) collective-permute-start(bf16[256,256]{1,0:T(8,128)(2,1)S(1)} %slice.18), channel_id=1, source_target_pairs={{0,8},{4,0},{8,16},{12,4},{16,24},{20,12},{24,28},{28,20},{1,9},{5... | collective-permute-start | bytes 393224 | tf_op jit(solution)/shard_map/ppermute | solution.py:336
  64.9 1.2 %collective-permute-start.24 = (bf16[256,256]{1,0:T(8,128)(2,1)S(1)}, bf16[256,256]{1,0:T(8,128)(2,1)S(1)}, u32[]{:S(2)}, u32[]{:S(2)}) collective-permute-start(bf16[256,256]{1,0:T(8,128)(2,1)S(1)} %slice.19), channel_id=1, source_target_pairs={{0,4},{4,12},{8,0},{12,20},{16,8},{20,28},{24,16},{28,24},{1,5},{5... | collective-permute-start | bytes 393224 | tf_op jit(solution)/shard_map/ppermute | solution.py:336
  66.1 0.9 %collective-permute-done.10.refs_0_ = bf16[512,256]{1,0:T(8,128)(2,1)S(1)} collective-permute-done((bf16[512,256]{1,0:T(8,128)(2,1)S(1)}, bf16[512,256]{1,0:T(8,128)(2,1)S(1)}, u32[]{:S(2)}, u32[]{:S(2)}) %collective-permute-start.10) | collective-permute-done | bytes 262176 | tf_op jit(solution)/shard_map/ppermute | solution.py:336
  67.0 0.8 %collective-permute-start.11 = (bf16[256,256]{1,0:T(8,128)(2,1)S(1)}, bf16[256,256]{1,0:T(8,128)(2,1)S(1)}, u32[]{:S(2)}, u32[]{:S(2)}) collective-permute-start(bf16[256,256]{1,0:T(8,128)(2,1)S(1)} %slice.16), channel_id=1, source_target_pairs={{0,4},{4,12},{8,0},{12,20},{16,8},{20,28},{24,16},{28,24},{1,5},{5... | collective-permute-start | bytes 393224 | tf_op jit(solution)/shard_map/ppermute | solution.py:336
  67.7 0.0 collective-permute-done.14.refs_1_
  67.7 1.4 %collective-permute-start.15 = (bf16[256,256]{1,0:T(8,128)(2,1)S(1)}, bf16[256,256]{1,0:T(8,128)(2,1)S(1)}, u32[]{:S(2)}, u32[]{:S(2)}) collective-permute-start(bf16[256,256]{1,0:T(8,128)(2,1)S(1)} %slice.17), channel_id=1, source_target_pairs={{0,8},{4,0},{8,16},{12,4},{16,24},{20,12},{24,28},{28,20},{1,9},{5... | collective-permute-start | bytes 393224 | tf_op jit(solution)/shard_map/ppermute | solution.py:336
  69.1 1.7 %apply_blocks.9 = (bf16[8,1024,256]{2,1,0:T(8,128)(2,1)}, f32[8,1024,256]{2,1,0:T(8,128)}) custom-call(s32[8,128]{1,0:T(8,128)S(1)} %broadcast_in_dim.31.modules_ref, bf16[8,1024,256]{2,1,0:T(8,128)(2,1)S(1)} %copy-done, f32[8,1024,256]{2,1,0:T(8,128)S(1)} %bitcast.4, ...), custom_call_target="tpu_custom_call", output_to_operand_aliasing={{0}: (5, {}), {1}: (6, {})} | custom-call | bytes 2097152 | tf_op jit(solution)/shard_map/apply_blocks/pallas_call | solution.py:58
  70.8 1.4 %apply_blocks.10 = (bf16[8,1024,256]{2,1,0:T(8,128)(2,1)}, f32[8,1024,256]{2,1,0:T(8,128)}) custom-call(s32[8,128]{1,0:T(8,128)S(1)} %broadcast_in_dim.31.modules_ref, bf16[8,1024,256]{2,1,0:T(8,128)(2,1)S(1)} %copy-done, f32[8,1024,256]{2,1,0:T(8,128)S(1)} %bitcast.4, ...), custom_call_target="tpu_custom_call", output_to_operand_aliasing={{0}: (5, {}), {1}: (6, {})} | custom-call | bytes 1048576 | tf_op jit(solution)/shard_map/apply_blocks/pallas_call | solution.py:58
  72.2 0.5 collective-permute-done.15.refs_1_
  72.8 1.4 %apply_blocks.11 = (bf16[8,1024,256]{2,1,0:T(8,128)(2,1)}, f32[8,1024,256]{2,1,0:T(8,128)}) custom-call(s32[8,128]{1,0:T(8,128)S(1)} %broadcast_in_dim.31.modules_ref, bf16[8,1024,256]{2,1,0:T(8,128)(2,1)S(1)} %copy-done, f32[8,1024,256]{2,1,0:T(8,128)S(1)} %bitcast.4, ...), custom_call_target="tpu_custom_call", output_to_operand_aliasing={{0}: (5, {}), {1}: (6, {})} | custom-call | bytes 1048576 | tf_op jit(solution)/shard_map/apply_blocks/pallas_call | solution.py:58
  (25 shorter events, 0.1 us)
Async XLA Ops:
  0.6 5.1 %copy-start.1 = (bf16[1,256,4096]{2,1,0:T(8,128)(2,1)S(1)}, bf16[1,256,4096]{2,1,0:T(8,128)(2,1)}, u32[]{:S(2)}) copy-start(bf16[1,256,4096]{2,1,0:T(8,128)(2,1)} %tokens_ref.5) | copy-start | bytes 6291460
  0.6 8.1 %copy-start.2 = (bf16[1,256,256]{2,1,0:T(8,128)(2,1)S(1)}, bf16[1,256,256]{2,1,0:T(8,128)(2,1)}, u32[]{:S(2)}) copy-start(bf16[1,256,256]{2,1,0:T(8,128)(2,1)} %param.7) | copy-start | bytes 393220
  0.6 0.8 %copy-start.3 = (s32[8,1]{0,1:T(1,128)S(1)}, s32[8,1]{0,1:T(1,128)}, u32[]{:S(2)}) copy-start(s32[8,1]{0,1:T(1,128)} %param.8) | copy-start | bytes 100
  1.5 6.6 %copy-start.5 = (s32[8]{0:T(128)S(1)}, s32[8]{0:T(128)}, u32[]{:S(2)}) copy-start(s32[8]{0:T(128)} %constant.28.clone) | copy-start | bytes 100
  1.5 8.1 %copy-start.4 = (s32[8,1]{0,1:T(1,128)S(1)}, s32[8,1]{0,1:T(1,128)}, u32[]{:S(2)}) copy-start(s32[8,1]{0,1:T(1,128)} %param.8) | copy-start | bytes 100
  2.7 14.9 %collective-permute-start.5 = (bf16[1024,256]{1,0:T(8,128)(2,1)S(1)}, bf16[1024,256]{1,0:T(8,128)(2,1)S(1)}, u32[]{:S(2)}, u32[]{:S(2)}) collective-permute-start(bf16[1024,256]{1,0:T(8,128)(2,1)S(1)} %pick_rows.1.after_ref.weights_ref), channel_id=1, source_target_pairs={{0,2},{1,3},{2,0},{3,1},{4,6},{5,7},{6,4},{7,5},{8,10},{9,11},{10,... | collective-permute-start | bytes 1572872 | tf_op jit(solution)/shard_map/ppermute | solution.py:239
  7.0 1.8 %collective-permute-start = (bf16[64,2048]{1,0:T(8,128)(2,1)}, bf16[64,2048]{1,0:T(8,128)(2,1)S(1)}, u32[]{:S(2)}, u32[]{:S(2)}) collective-permute-start(bf16[64,2048]{1,0:T(8,128)(2,1)} %get-tuple-element.41), channel_id=1, source_target_pairs={{0,1},{1,0},{2,3},{3,2},{4,5},{5,4},{6,7},{7,6},{8,9},{9,8},{10,11... | collective-permute-start | bytes 786440 | tf_op jit(solution)/shard_map/ppermute | solution.py:246
  7.0 2.7 %collective-permute-start.1 = (bf16[64,2048]{1,0:T(8,128)(2,1)}, bf16[64,2048]{1,0:T(8,128)(2,1)}, u32[]{:S(2)}, u32[]{:S(2)}) collective-permute-start(bf16[64,2048]{1,0:T(8,128)(2,1)} %get-tuple-element.42), channel_id=1, source_target_pairs={{0,1},{1,0},{2,3},{3,2},{4,5},{5,4},{6,7},{7,6},{8,9},{9,8},{10,11... | collective-permute-start | bytes 786440 | tf_op jit(solution)/shard_map/ppermute | solution.py:246
  7.5 2.2 %collective-permute-start.2 = (bf16[64,2048]{1,0:T(8,128)(2,1)}, bf16[64,2048]{1,0:T(8,128)(2,1)}, u32[]{:S(2)}, u32[]{:S(2)}) collective-permute-start(bf16[64,2048]{1,0:T(8,128)(2,1)} %get-tuple-element.43), channel_id=1, source_target_pairs={{0,1},{1,0},{2,3},{3,2},{4,5},{5,4},{6,7},{7,6},{8,9},{9,8},{10,11... | collective-permute-start | bytes 786440 | tf_op jit(solution)/shard_map/ppermute | solution.py:246
  7.6 2.4 %collective-permute-start.3 = (bf16[64,2048]{1,0:T(8,128)(2,1)}, bf16[64,2048]{1,0:T(8,128)(2,1)}, u32[]{:S(2)}, u32[]{:S(2)}) collective-permute-start(bf16[64,2048]{1,0:T(8,128)(2,1)} %get-tuple-element.44), channel_id=1, source_target_pairs={{0,1},{1,0},{2,3},{3,2},{4,5},{5,4},{6,7},{7,6},{8,9},{9,8},{10,11... | collective-permute-start | bytes 786440 | tf_op jit(solution)/shard_map/ppermute | solution.py:246
  8.8 3.2 %collective-permute-start.4 = (bf16[256,256]{1,0:T(8,128)(2,1)S(1)}, bf16[256,256]{1,0:T(8,128)(2,1)S(1)}, u32[]{:S(2)}, u32[]{:S(2)}) collective-permute-start(bf16[256,256]{1,0:T(8,128)(2,1)S(1)} %bitcast.5), channel_id=1, source_target_pairs={{0,1},{1,0},{2,3},{3,2},{4,5},{5,4},{6,7},{7,6},{8,9},{9,8},{10,11... | collective-permute-start | bytes 393224 | tf_op jit(solution)/shard_map/ppermute | solution.py:245
  10.0 36.9 %slice-start = ((s8[8388608]{0:T(1024)(128)(4,1)}), s8[4194304]{0:T(1024)(128)(4,1)S(1)}, s32[]{:S(2)}) async-start(s8[8388608]{0:T(1024)(128)(4,1)} %bitcast.3), calls=%async_computation | async-start | bytes 8388608
  17.6 29.3 %slice-start.1 = ((s8[8388608]{0:T(1024)(128)(4,1)}), s8[4194304]{0:T(1024)(128)(4,1)S(1)}, s32[]{:S(2)}) async-start(s8[8388608]{0:T(1024)(128)(4,1)} %bitcast.3), calls=%async_computation.1 | async-start | bytes 8388608
  18.1 28.8 %copy-start = (bf16[8,1024,256]{2,1,0:T(8,128)(2,1)S(1)}, bf16[8,1024,256]{2,1,0:T(8,128)(2,1)}, u32[]{:S(2)}) copy-start(bf16[8,1024,256]{2,1,0:T(8,128)(2,1)} %weights_ref.13) | copy-start | bytes 12582916
  18.1 1.6 %collective-permute-start.6 = (bf16[512,256]{1,0:T(8,128)(2,1)S(1)}, bf16[512,256]{1,0:T(8,128)(2,1)S(1)}, u32[]{:S(2)}, u32[]{:S(2)}) collective-permute-start(bf16[512,256]{1,0:T(8,128)(2,1)S(1)} %get-tuple-element.51), channel_id=1, source_target_pairs={{0,1},{1,0},{2,3},{3,2},{4,5},{5,4},{6,7},{7,6},{8,9},{9,8},{10,11... | collective-permute-start | bytes 786440 | tf_op jit(solution)/shard_map/ppermute | solution.py:265
  20.2 9.2 %collective-permute-start.16 = (bf16[512,256]{1,0:T(8,128)(2,1)S(1)}, bf16[512,256]{1,0:T(8,128)(2,1)S(1)}, u32[]{:S(2)}, u32[]{:S(2)}) collective-permute-start(bf16[512,256]{1,0:T(8,128)(2,1)S(1)} %get-tuple-element.59), channel_id=1, source_target_pairs={{0,2},{1,3},{2,0},{3,1},{4,6},{5,7},{6,4},{7,5},{8,10},{9,11},{10,... | collective-permute-start | bytes 786440 | tf_op jit(solution)/shard_map/ppermute | solution.py:289
  22.6 11.6 %collective-permute-start.7 = (bf16[512,256]{1,0:T(8,128)(2,1)S(1)}, bf16[512,256]{1,0:T(8,128)(2,1)S(1)}, u32[]{:S(2)}, u32[]{:S(2)}) collective-permute-start(bf16[512,256]{1,0:T(8,128)(2,1)S(1)} %get-tuple-element.55), channel_id=1, source_target_pairs={{0,2},{1,3},{2,0},{3,1},{4,6},{5,7},{6,4},{7,5},{8,10},{9,11},{10,... | collective-permute-start | bytes 786440 | tf_op jit(solution)/shard_map/ppermute | solution.py:289
  29.5 6.9 %collective-permute-start.17 = (bf16[512,256]{1,0:T(8,128)(2,1)S(1)}, bf16[512,256]{1,0:T(8,128)(2,1)S(1)}, u32[]{:S(2)}, u32[]{:S(2)}) collective-permute-start(bf16[512,256]{1,0:T(8,128)(2,1)S(1)} %multiply_convert_fusion.refs_0_), channel_id=1, source_target_pairs={{0,8},{4,0},{8,16},{12,4},{16,24},{20,12},{24,28},{28,20},{1,9},{5... | collective-permute-start | bytes 786440 | tf_op jit(solution)/shard_map/ppermute | solution.py:336
  31.4 7.8 %collective-permute-start.19 = (bf16[512,256]{1,0:T(8,128)(2,1)S(1)}, bf16[512,256]{1,0:T(8,128)(2,1)S(1)}, u32[]{:S(2)}, u32[]{:S(2)}) collective-permute-start(bf16[512,256]{1,0:T(8,128)(2,1)S(1)} %multiply_convert_fusion.refs_0_), channel_id=1, source_target_pairs={{0,4},{4,12},{8,0},{12,20},{16,8},{20,28},{24,16},{28,24},{1,5},{5... | collective-permute-start | bytes 786440 | tf_op jit(solution)/shard_map/ppermute | solution.py:336
  34.4 10.5 %collective-permute-start.8 = (bf16[512,256]{1,0:T(8,128)(2,1)S(1)}, bf16[512,256]{1,0:T(8,128)(2,1)S(1)}, u32[]{:S(2)}, u32[]{:S(2)}) collective-permute-start(bf16[512,256]{1,0:T(8,128)(2,1)S(1)} %multiply_convert_fusion.1.refs_3_), channel_id=1, source_target_pairs={{0,4},{4,12},{8,0},{12,20},{16,8},{20,28},{24,16},{28,24},{1,5},{5... | collective-permute-start | bytes 786440 | tf_op jit(solution)/shard_map/ppermute | solution.py:336
  36.2 9.2 %collective-permute-start.12 = (bf16[512,256]{1,0:T(8,128)(2,1)S(1)}, bf16[512,256]{1,0:T(8,128)(2,1)S(1)}, u32[]{:S(2)}, u32[]{:S(2)}) collective-permute-start(bf16[512,256]{1,0:T(8,128)(2,1)S(1)} %multiply_convert_fusion.1.refs_3_), channel_id=1, source_target_pairs={{0,8},{4,0},{8,16},{12,4},{16,24},{20,12},{24,28},{28,20},{1,9},{5... | collective-permute-start | bytes 786440 | tf_op jit(solution)/shard_map/ppermute | solution.py:336
  36.4 14.6 %collective-permute-start.18 = (bf16[512,256]{1,0:T(8,128)(2,1)S(1)}, bf16[512,256]{1,0:T(8,128)(2,1)S(1)}, u32[]{:S(2)}, u32[]{:S(2)}) collective-permute-start(bf16[512,256]{1,0:T(8,128)(2,1)S(1)} %collective-permute-done.17.refs_1_), channel_id=1, source_target_pairs={{0,8},{4,0},{8,16},{12,4},{16,24},{20,12},{24,28},{28,20},{1,9},{5... | collective-permute-start | bytes 786440 | tf_op jit(solution)/shard_map/ppermute | solution.py:336
  39.3 11.8 %collective-permute-start.20 = (bf16[512,256]{1,0:T(8,128)(2,1)S(1)}, bf16[512,256]{1,0:T(8,128)(2,1)S(1)}, u32[]{:S(2)}, u32[]{:S(2)}) collective-permute-start(bf16[512,256]{1,0:T(8,128)(2,1)S(1)} %collective-permute-done.19.refs_2_), channel_id=1, source_target_pairs={{0,4},{4,12},{8,0},{12,20},{16,8},{20,28},{24,16},{28,24},{1,5},{5... | collective-permute-start | bytes 786440 | tf_op jit(solution)/shard_map/ppermute | solution.py:336
  44.9 11.2 %collective-permute-start.9 = (bf16[512,256]{1,0:T(8,128)(2,1)S(1)}, bf16[512,256]{1,0:T(8,128)(2,1)S(1)}, u32[]{:S(2)}, u32[]{:S(2)}) collective-permute-start(bf16[512,256]{1,0:T(8,128)(2,1)S(1)} %collective-permute-done.8.refs_4_), channel_id=1, source_target_pairs={{0,4},{4,12},{8,0},{12,20},{16,8},{20,28},{24,16},{28,24},{1,5},{5... | collective-permute-start | bytes 786440 | tf_op jit(solution)/shard_map/ppermute | solution.py:336
  45.4 11.2 %collective-permute-start.13 = (bf16[512,256]{1,0:T(8,128)(2,1)S(1)}, bf16[512,256]{1,0:T(8,128)(2,1)S(1)}, u32[]{:S(2)}, u32[]{:S(2)}) collective-permute-start(bf16[512,256]{1,0:T(8,128)(2,1)S(1)} %collective-permute-done.12.refs_5_), channel_id=1, source_target_pairs={{0,8},{4,0},{8,16},{12,4},{16,24},{20,12},{24,28},{28,20},{1,9},{5... | collective-permute-start | bytes 786440 | tf_op jit(solution)/shard_map/ppermute | solution.py:336
  51.0 11.2 %collective-permute-start.21 = (bf16[512,256]{1,0:T(8,128)(2,1)S(1)}, bf16[512,256]{1,0:T(8,128)(2,1)S(1)}, u32[]{:S(2)}, u32[]{:S(2)}) collective-permute-start(bf16[512,256]{1,0:T(8,128)(2,1)S(1)} %collective-permute-done.18.refs_0_), channel_id=1, source_target_pairs={{0,8},{4,0},{8,16},{12,4},{16,24},{20,12},{24,28},{28,20},{1,9},{5... | collective-permute-start | bytes 786440 | tf_op jit(solution)/shard_map/ppermute | solution.py:336
  51.9 10.4 %collective-permute-start.22 = (bf16[512,256]{1,0:T(8,128)(2,1)S(1)}, bf16[512,256]{1,0:T(8,128)(2,1)S(1)}, u32[]{:S(2)}, u32[]{:S(2)}) collective-permute-start(bf16[512,256]{1,0:T(8,128)(2,1)S(1)} %collective-permute-done.20.refs_1_), channel_id=1, source_target_pairs={{0,4},{4,12},{8,0},{12,20},{16,8},{20,28},{24,16},{28,24},{1,5},{5... | collective-permute-start | bytes 786440 | tf_op jit(solution)/shard_map/ppermute | solution.py:336
  56.1 10.9 %collective-permute-start.10 = (bf16[512,256]{1,0:T(8,128)(2,1)S(1)}, bf16[512,256]{1,0:T(8,128)(2,1)S(1)}, u32[]{:S(2)}, u32[]{:S(2)}) collective-permute-start(bf16[512,256]{1,0:T(8,128)(2,1)S(1)} %collective-permute-done.9.refs_2_), channel_id=1, source_target_pairs={{0,4},{4,12},{8,0},{12,20},{16,8},{20,28},{24,16},{28,24},{1,5},{5... | collective-permute-start | bytes 786440 | tf_op jit(solution)/shard_map/ppermute | solution.py:336
  56.7 11.1 %collective-permute-start.14 = (bf16[512,256]{1,0:T(8,128)(2,1)S(1)}, bf16[512,256]{1,0:T(8,128)(2,1)S(1)}, u32[]{:S(2)}, u32[]{:S(2)}) collective-permute-start(bf16[512,256]{1,0:T(8,128)(2,1)S(1)} %collective-permute-done.13.refs_3_), channel_id=1, source_target_pairs={{0,8},{4,0},{8,16},{12,4},{16,24},{20,12},{24,28},{28,20},{1,9},{5... | collective-permute-start | bytes 786440 | tf_op jit(solution)/shard_map/ppermute | solution.py:336
  64.0 6.8 %collective-permute-start.23 = (bf16[256,256]{1,0:T(8,128)(2,1)S(1)}, bf16[256,256]{1,0:T(8,128)(2,1)S(1)}, u32[]{:S(2)}, u32[]{:S(2)}) collective-permute-start(bf16[256,256]{1,0:T(8,128)(2,1)S(1)} %slice.18), channel_id=1, source_target_pairs={{0,8},{4,0},{8,16},{12,4},{16,24},{20,12},{24,28},{28,20},{1,9},{5... | collective-permute-start | bytes 393224 | tf_op jit(solution)/shard_map/ppermute | solution.py:336
  64.9 5.9 %collective-permute-start.24 = (bf16[256,256]{1,0:T(8,128)(2,1)S(1)}, bf16[256,256]{1,0:T(8,128)(2,1)S(1)}, u32[]{:S(2)}, u32[]{:S(2)}) collective-permute-start(bf16[256,256]{1,0:T(8,128)(2,1)S(1)} %slice.19), channel_id=1, source_target_pairs={{0,4},{4,12},{8,0},{12,20},{16,8},{20,28},{24,16},{28,24},{1,5},{5... | collective-permute-start | bytes 393224 | tf_op jit(solution)/shard_map/ppermute | solution.py:336
  67.0 5.2 %collective-permute-start.11 = (bf16[256,256]{1,0:T(8,128)(2,1)S(1)}, bf16[256,256]{1,0:T(8,128)(2,1)S(1)}, u32[]{:S(2)}, u32[]{:S(2)}) collective-permute-start(bf16[256,256]{1,0:T(8,128)(2,1)S(1)} %slice.16), channel_id=1, source_target_pairs={{0,4},{4,12},{8,0},{12,20},{16,8},{20,28},{24,16},{28,24},{1,5},{5... | collective-permute-start | bytes 393224 | tf_op jit(solution)/shard_map/ppermute | solution.py:336
  67.7 5.0 %collective-permute-start.15 = (bf16[256,256]{1,0:T(8,128)(2,1)S(1)}, bf16[256,256]{1,0:T(8,128)(2,1)S(1)}, u32[]{:S(2)}, u32[]{:S(2)}) collective-permute-start(bf16[256,256]{1,0:T(8,128)(2,1)S(1)} %slice.17), channel_id=1, source_target_pairs={{0,8},{4,0},{8,16},{12,4},{16,24},{20,12},{24,28},{28,20},{1,9},{5... | collective-permute-start | bytes 393224 | tf_op jit(solution)/shard_map/ppermute | solution.py:336

commit v8 on v7

--- a/solution.py
+++ b/solution.py
@@ -207,7 +207,7 @@
 
         lax.fori_loop(0, rows // tile, work, 0)
         here, spot = pl.ds(0, rows), pl.ds(start, rows)
-        for k, (src, dst) in enumerate(((new_weights, out_weights), (new_moment, out_moment))):
+        for k, (src, dst) in enumerate(((new_moment, out_moment), (new_weights, out_weights))):
             copy = pltpu.make_async_copy(src.at[i, here], dst.at[module, spot], sems.at[i, k])
             copy.start()
             copies.append(copy)

time: 74.3 us -> 74.3 us (level)
  no operation moved by 1% of the time
where the time goes in v8:
time: 74.3 us; the launch traced here: 74.1 us
  waiting for transfers between devices  30.2 us (41%)
  starting transfers between devices  22.7 us (31%)
  Pallas kernels  17.8 us (24%)
  other arithmetic  1.59 us (2%)
  local copies, waits for them, and re-layouts  0.94 us (1%)
  between operations  0.87 us (1%)
    pallas_call x12, Pallas kernels, call(): pl.pallas_call(kernel, in_specs=in_specs, out_specs=out_specs, out_shape=...  17.8 us
    ppermute x16, starting transfers between devices, body(): lax.ppermute(b, 'path', pairs[way])  16.3 us
    ppermute x16, waiting for transfers between devices, body(): lax.ppermute(b, 'path', pairs[way])  13.6 us
    ppermute x2, waiting for transfers between devices, body(): lax.ppermute(gradients[s, c], 'fsdp', to_chip(s)).astype(f32)  9.14 us
    ppermute x1, waiting for transfers between devices, body(): lax.ppermute(own_weights, 'fsdp', to_chip(s))  5.58 us
    ppermute x1, starting transfers between devices, body(): lax.ppermute(own_weights, 'fsdp', to_chip(s))  3 us
    ppermute x2, starting transfers between devices, body(): lax.ppermute(gradients[s, c], 'fsdp', to_chip(s)).astype(f32)  2.16 us
    ppermute x1, waiting for transfers between devices, body(): other = lax.ppermute(rounded, 'fsdp', to_core)  1.52 us
  transfers between devices with their start and end apart: 25, of which 13 were waited for; matrix products, arithmetic and copies ran while one was open for 2% of the time, Pallas kernels for 19%

profile of v8, /device:TPU:0, one launch (start us, length us, event | category | flops | bytes accessed | tf_op | source)
XLA Modules:
  0.0 74.1 jit_solution(10332065907687060964)
XLA Ops:
  0.7 0.8 %copy-done.3 = s32[8,1]{0,1:T(1,128)S(1)} copy-done((s32[8,1]{0,1:T(1,128)S(1)}, s32[8,1]{0,1:T(1,128)}, u32[]{:S(2)}) %copy-start.3) | copy-done | bytes 56
  1.5 1.2 %pick_rows.1.after_ref.weights_ref = bf16[1024,256]{1,0:T(8,128)(2,1)S(1)} custom-call(s32[1,8]{1,0:T(1,128)S(1)} %bitcast.7, bf16[8,1024,256]{2,1,0:T(8,128)(2,1)} %weights_ref.13), custom_call_target="tpu_custom_call" | custom-call | tf_op jit(solution)/shard_map/pick_rows/pallas_call | solution.py:58
  2.7 3.0 %collective-permute-start.5 = (bf16[1024,256]{1,0:T(8,128)(2,1)S(1)}, bf16[1024,256]{1,0:T(8,128)(2,1)S(1)}, u32[]{:S(2)}, u32[]{:S(2)}) collective-permute-start(bf16[1024,256]{1,0:T(8,128)(2,1)S(1)} %pick_rows.1.after_ref.weights_ref), channel_id=1, source_target_pairs={{0,2},{1,3},{2,0},{3,1},{4,6},{5,7},{6,4},{7,5},{8,10},{9,11},{10,... | collective-permute-start | bytes 1572872 | tf_op jit(solution)/shard_map/ppermute | solution.py:239
  5.7 1.2 %pick_columns.1 = (bf16[64,2048]{1,0:T(8,128)(2,1)}, bf16[64,2048]{1,0:T(8,128)(2,1)}, bf16[64,2048]{1,0:T(8,128)(2,1)}, bf16[64,2048]{1,0:T(8,128)(2,1)}) custom-call(bf16[1,256,4096]{2,1,0:T(8,128)(2,1)S(1)} %copy-done.1, bf16[1024,256]{1,0:T(8,128)(2,1)S(1)} %pick_rows.1.after_ref.weights_ref), custom_call_target="tpu_custom_call" | custom-call | tf_op jit(solution)/shard_map/pick_columns/pallas_call | solution.py:58
  7.0 0.1 collective-permute-start
  7.0 0.5 collective-permute-start.1
  7.5 0.1 collective-permute-start.2
  7.6 0.4 collective-permute-start.3
  8.0 0.6 fusion.5
  8.6 0.1 collective-permute-done.refs_0_
  8.8 0.1 collective-permute-start.4
  8.9 0.7 select_reduce_fusion.1
  9.6 0.2 select_reduce_fusion
  9.8 0.0 collective-permute-done.1.refs_1_
  9.8 0.3 collective-permute-done.3.refs_3_
  10.0 2.0 %first_products.1 = (f32[512,256]{1,0:T(8,128)S(1)}, bf16[2048,512]{1,0:T(8,128)(2,1)S(1)}, bf16[256,2048]{1,0:T(8,128)(2,1)S(1)}) custom-call(bf16[1,256,4096]{2,1,0:T(8,128)(2,1)S(1)} %copy-done.1, bf16[1024,256]{1,0:T(8,128)(2,1)S(1)} %pick_rows.1.after_ref.weights_ref, bf16[64,2048]{1,0:T(8,128)(2,1)S(1)} %collective-permute-done.refs_0_, ...), custom_call_target="tpu_custom_call" | custom-call | tf_op jit(solution)/shard_map/first_products/pallas_call | solution.py:58
  12.0 0.1 broadcast_in_dim.31.modules_ref
  12.1 5.6 %collective-permute-done.5.weights_ref = bf16[1024,256]{1,0:T(8,128)(2,1)S(1)} collective-permute-done((bf16[1024,256]{1,0:T(8,128)(2,1)S(1)}, bf16[1024,256]{1,0:T(8,128)(2,1)S(1)}, u32[]{:S(2)}, u32[]{:S(2)}) %collective-permute-start.5) | collective-permute-done | bytes 524320 | tf_op jit(solution)/shard_map/ppermute | solution.py:239
  17.6 0.4 next_products.1
  18.1 0.0 copy-start
  18.1 0.1 collective-permute-start.6
  18.2 1.5 %collective-permute-done.6.other_ref = bf16[512,256]{1,0:T(8,128)(2,1)S(1)} collective-permute-done((bf16[512,256]{1,0:T(8,128)(2,1)S(1)}, bf16[512,256]{1,0:T(8,128)(2,1)S(1)}, u32[]{:S(2)}, u32[]{:S(2)}) %collective-permute-start.6) | collective-permute-done | bytes 262176 | tf_op jit(solution)/shard_map/ppermute | solution.py:265
  19.7 0.5 first_gradients.1
  20.2 1.8 %collective-permute-start.16 = (bf16[512,256]{1,0:T(8,128)(2,1)S(1)}, bf16[512,256]{1,0:T(8,128)(2,1)S(1)}, u32[]{:S(2)}, u32[]{:S(2)}) collective-permute-start(bf16[512,256]{1,0:T(8,128)(2,1)S(1)} %get-tuple-element.59), channel_id=1, source_target_pairs={{0,2},{1,3},{2,0},{3,1},{4,6},{5,7},{6,4},{7,5},{8,10},{9,11},{10,... | collective-permute-start | bytes 786440 | tf_op jit(solution)/shard_map/ppermute | solution.py:289
  22.1 0.6 more_gradients.1
  22.6 0.3 collective-permute-start.7
  23.0 6.5 %collective-permute-done.16 = bf16[512,256]{1,0:T(8,128)(2,1)S(1)} collective-permute-done((bf16[512,256]{1,0:T(8,128)(2,1)S(1)}, bf16[512,256]{1,0:T(8,128)(2,1)S(1)}, u32[]{:S(2)}, u32[]{:S(2)}) %collective-permute-start.16) | collective-permute-done | bytes 262176 | tf_op jit(solution)/shard_map/ppermute | solution.py:289
  29.5 0.1 multiply_convert_fusion.refs_0_
  29.5 1.9 %collective-permute-start.17 = (bf16[512,256]{1,0:T(8,128)(2,1)S(1)}, bf16[512,256]{1,0:T(8,128)(2,1)S(1)}, u32[]{:S(2)}, u32[]{:S(2)}) collective-permute-start(bf16[512,256]{1,0:T(8,128)(2,1)S(1)} %multiply_convert_fusion.refs_0_), channel_id=1, source_target_pairs={{0,8},{4,0},{8,16},{12,4},{16,24},{20,12},{24,28},{28,20},{1,9},{5... | collective-permute-start | bytes 786440 | tf_op jit(solution)/shard_map/ppermute | solution.py:336
  31.4 0.2 collective-permute-start.19
  31.6 2.7 %collective-permute-done.7 = bf16[512,256]{1,0:T(8,128)(2,1)S(1)} collective-permute-done((bf16[512,256]{1,0:T(8,128)(2,1)S(1)}, bf16[512,256]{1,0:T(8,128)(2,1)S(1)}, u32[]{:S(2)}, u32[]{:S(2)}) %collective-permute-start.7) | collective-permute-done | bytes 262176 | tf_op jit(solution)/shard_map/ppermute | solution.py:289
  34.3 0.1 multiply_convert_fusion.1.refs_3_
  34.4 1.8 %collective-permute-start.8 = (bf16[512,256]{1,0:T(8,128)(2,1)S(1)}, bf16[512,256]{1,0:T(8,128)(2,1)S(1)}, u32[]{:S(2)}, u32[]{:S(2)}) collective-permute-start(bf16[512,256]{1,0:T(8,128)(2,1)S(1)} %multiply_convert_fusion.1.refs_3_), channel_id=1, source_target_pairs={{0,4},{4,12},{8,0},{12,20},{16,8},{20,28},{24,16},{28,24},{1,5},{5... | collective-permute-start | bytes 786440 | tf_op jit(solution)/shard_map/ppermute | solution.py:336
  36.2 0.3 collective-permute-start.12
  36.4 1.8 %collective-permute-start.18 = (bf16[512,256]{1,0:T(8,128)(2,1)S(1)}, bf16[512,256]{1,0:T(8,128)(2,1)S(1)}, u32[]{:S(2)}, u32[]{:S(2)}) collective-permute-start(bf16[512,256]{1,0:T(8,128)(2,1)S(1)} %collective-permute-done.17.refs_1_), channel_id=1, source_target_pairs={{0,8},{4,0},{8,16},{12,4},{16,24},{20,12},{24,28},{28,20},{1,9},{5... | collective-permute-start | bytes 786440 | tf_op jit(solution)/shard_map/ppermute | solution.py:336
  38.3 1.0 %collective-permute-done.19.refs_2_ = bf16[512,256]{1,0:T(8,128)(2,1)S(1)} collective-permute-done((bf16[512,256]{1,0:T(8,128)(2,1)S(1)}, bf16[512,256]{1,0:T(8,128)(2,1)S(1)}, u32[]{:S(2)}, u32[]{:S(2)}) %collective-permute-start.19) | collective-permute-done | bytes 262176 | tf_op jit(solution)/shard_map/ppermute | solution.py:336
  39.3 0.0 collective-permute-start.20
  39.3 5.6 %collective-permute-done.8.refs_4_ = bf16[512,256]{1,0:T(8,128)(2,1)S(1)} collective-permute-done((bf16[512,256]{1,0:T(8,128)(2,1)S(1)}, bf16[512,256]{1,0:T(8,128)(2,1)S(1)}, u32[]{:S(2)}, u32[]{:S(2)}) %collective-permute-start.8) | collective-permute-done | bytes 262176 | tf_op jit(solution)/shard_map/ppermute | solution.py:336
  44.9 0.5 collective-permute-start.9
  45.4 0.0 collective-permute-done.12.refs_5_
  45.4 1.5 %collective-permute-start.13 = (bf16[512,256]{1,0:T(8,128)(2,1)S(1)}, bf16[512,256]{1,0:T(8,128)(2,1)S(1)}, u32[]{:S(2)}, u32[]{:S(2)}) collective-permute-start(bf16[512,256]{1,0:T(8,128)(2,1)S(1)} %collective-permute-done.12.refs_5_), channel_id=1, source_target_pairs={{0,8},{4,0},{8,16},{12,4},{16,24},{20,12},{24,28},{28,20},{1,9},{5... | collective-permute-start | bytes 786440 | tf_op jit(solution)/shard_map/ppermute | solution.py:336
  46.9 3.3 %apply_blocks.6 = (bf16[8,1024,256]{2,1,0:T(8,128)(2,1)}, f32[8,1024,256]{2,1,0:T(8,128)}) custom-call(s32[8,128]{1,0:T(8,128)S(1)} %broadcast_in_dim.31.modules_ref, bf16[8,1024,256]{2,1,0:T(8,128)(2,1)S(1)} %copy-done, f32[8,1024,256]{2,1,0:T(8,128)S(1)} %bitcast.4, bf16[512,256]{1,0:T(8,128)(2,1)S(1)} %multiply_convert_fusion.refs_0_, ...), custom_call_target="tpu_custom_call" | custom-call | bytes 6291456 | tf_op jit(solution)/shard_map/apply_blocks/pallas_call | solution.py:58
  50.2 0.8 %collective-permute-done.18.refs_0_ = bf16[512,256]{1,0:T(8,128)(2,1)S(1)} collective-permute-done((bf16[512,256]{1,0:T(8,128)(2,1)S(1)}, bf16[512,256]{1,0:T(8,128)(2,1)S(1)}, u32[]{:S(2)}, u32[]{:S(2)}) %collective-permute-start.18) | collective-permute-done | bytes 262176 | tf_op jit(solution)/shard_map/ppermute | solution.py:336
  51.0 0.0 collective-permute-done.20.refs_1_
  51.0 0.9 %collective-permute-start.21 = (bf16[512,256]{1,0:T(8,128)(2,1)S(1)}, bf16[512,256]{1,0:T(8,128)(2,1)S(1)}, u32[]{:S(2)}, u32[]{:S(2)}) collective-permute-start(bf16[512,256]{1,0:T(8,128)(2,1)S(1)} %collective-permute-done.18.refs_0_), channel_id=1, source_target_pairs={{0,8},{4,0},{8,16},{12,4},{16,24},{20,12},{24,28},{28,20},{1,9},{5... | collective-permute-start | bytes 786440 | tf_op jit(solution)/shard_map/ppermute | solution.py:336
  51.9 1.2 %collective-permute-start.22 = (bf16[512,256]{1,0:T(8,128)(2,1)S(1)}, bf16[512,256]{1,0:T(8,128)(2,1)S(1)}, u32[]{:S(2)}, u32[]{:S(2)}) collective-permute-start(bf16[512,256]{1,0:T(8,128)(2,1)S(1)} %collective-permute-done.20.refs_1_), channel_id=1, source_target_pairs={{0,4},{4,12},{8,0},{12,20},{16,8},{20,28},{24,16},{28,24},{1,5},{5... | collective-permute-start | bytes 786440 | tf_op jit(solution)/shard_map/ppermute | solution.py:336
  53.1 3.0 %collective-permute-done.9.refs_2_ = bf16[512,256]{1,0:T(8,128)(2,1)S(1)} collective-permute-done((bf16[512,256]{1,0:T(8,128)(2,1)S(1)}, bf16[512,256]{1,0:T(8,128)(2,1)S(1)}, u32[]{:S(2)}, u32[]{:S(2)}) %collective-permute-start.9) | collective-permute-done | bytes 262176 | tf_op jit(solution)/shard_map/ppermute | solution.py:336
  56.1 0.5 collective-permute-start.10
  56.7 0.0 collective-permute-done.13.refs_3_
  56.7 1.5 %collective-permute-start.14 = (bf16[512,256]{1,0:T(8,128)(2,1)S(1)}, bf16[512,256]{1,0:T(8,128)(2,1)S(1)}, u32[]{:S(2)}, u32[]{:S(2)}) collective-permute-start(bf16[512,256]{1,0:T(8,128)(2,1)S(1)} %collective-permute-done.13.refs_3_), channel_id=1, source_target_pairs={{0,8},{4,0},{8,16},{12,4},{16,24},{20,12},{24,28},{28,20},{1,9},{5... | collective-permute-start | bytes 786440 | tf_op jit(solution)/shard_map/ppermute | solution.py:336
  58.1 2.5 %apply_blocks.7 = (bf16[8,1024,256]{2,1,0:T(8,128)(2,1)}, f32[8,1024,256]{2,1,0:T(8,128)}) custom-call(s32[8,128]{1,0:T(8,128)S(1)} %broadcast_in_dim.31.modules_ref, bf16[8,1024,256]{2,1,0:T(8,128)(2,1)S(1)} %copy-done, f32[8,1024,256]{2,1,0:T(8,128)S(1)} %bitcast.4, ...), custom_call_target="tpu_custom_call", output_to_operand_aliasing={{0}: (7, {}), {1}: (8, {})} | custom-call | bytes 4194304 | tf_op jit(solution)/shard_map/apply_blocks/pallas_call | solution.py:58
  60.6 1.6 %collective-permute-done.21.refs_0_ = bf16[512,256]{1,0:T(8,128)(2,1)S(1)} collective-permute-done((bf16[512,256]{1,0:T(8,128)(2,1)S(1)}, bf16[512,256]{1,0:T(8,128)(2,1)S(1)}, u32[]{:S(2)}, u32[]{:S(2)}) %collective-permute-start.21) | collective-permute-done | bytes 262176 | tf_op jit(solution)/shard_map/ppermute | solution.py:336
  62.3 0.0 collective-permute-done.22.refs_1_
  62.3 1.7 %apply_blocks.8 = (bf16[8,1024,256]{2,1,0:T(8,128)(2,1)}, f32[8,1024,256]{2,1,0:T(8,128)}) custom-call(s32[8,128]{1,0:T(8,128)S(1)} %broadcast_in_dim.31.modules_ref, bf16[8,1024,256]{2,1,0:T(8,128)(2,1)S(1)} %copy-done, f32[8,1024,256]{2,1,0:T(8,128)S(1)} %bitcast.4, ...), custom_call_target="tpu_custom_call", output_to_operand_aliasing={{0}: (5, {}), {1}: (6, {})} | custom-call | bytes 2097152 | tf_op jit(solution)/shard_map/apply_blocks/pallas_call | solution.py:58
  64.0 0.9 %collective-permute-start.23 = (bf16[256,256]{1,0:T(8,128)(2,1)S(1)}, bf16[256,256]{1,0:T(8,128)(2,1)S(1)}, u32[]{:S(2)}, u32[]{:S(2)}) collective-permute-start(bf16[256,256]{1,0:T(8,128)(2,1)S(1)} %slice.18), channel_id=1, source_target_pairs={{0,8},{4,0},{8,16},{12,4},{16,24},{20,12},{24,28},{28,20},{1,9},{5... | collective-permute-start | bytes 393224 | tf_op jit(solution)/shard_map/ppermute | solution.py:336
  64.9 1.2 %collective-permute-start.24 = (bf16[256,256]{1,0:T(8,128)(2,1)S(1)}, bf16[256,256]{1,0:T(8,128)(2,1)S(1)}, u32[]{:S(2)}, u32[]{:S(2)}) collective-permute-start(bf16[256,256]{1,0:T(8,128)(2,1)S(1)} %slice.19), channel_id=1, source_target_pairs={{0,4},{4,12},{8,0},{12,20},{16,8},{20,28},{24,16},{28,24},{1,5},{5... | collective-permute-start | bytes 393224 | tf_op jit(solution)/shard_map/ppermute | solution.py:336
  66.1 0.9 %collective-permute-done.10.refs_0_ = bf16[512,256]{1,0:T(8,128)(2,1)S(1)} collective-permute-done((bf16[512,256]{1,0:T(8,128)(2,1)S(1)}, bf16[512,256]{1,0:T(8,128)(2,1)S(1)}, u32[]{:S(2)}, u32[]{:S(2)}) %collective-permute-start.10) | collective-permute-done | bytes 262176 | tf_op jit(solution)/shard_map/ppermute | solution.py:336
  67.0 0.7 collective-permute-start.11
  67.7 0.0 collective-permute-done.14.refs_1_
  67.7 1.4 %collective-permute-start.15 = (bf16[256,256]{1,0:T(8,128)(2,1)S(1)}, bf16[256,256]{1,0:T(8,128)(2,1)S(1)}, u32[]{:S(2)}, u32[]{:S(2)}) collective-permute-start(bf16[256,256]{1,0:T(8,128)(2,1)S(1)} %slice.17), channel_id=1, source_target_pairs={{0,8},{4,0},{8,16},{12,4},{16,24},{20,12},{24,28},{28,20},{1,9},{5... | collective-permute-start | bytes 393224 | tf_op jit(solution)/shard_map/ppermute | solution.py:336
  69.1 1.7 %apply_blocks.9 = (bf16[8,1024,256]{2,1,0:T(8,128)(2,1)}, f32[8,1024,256]{2,1,0:T(8,128)}) custom-call(s32[8,128]{1,0:T(8,128)S(1)} %broadcast_in_dim.31.modules_ref, bf16[8,1024,256]{2,1,0:T(8,128)(2,1)S(1)} %copy-done, f32[8,1024,256]{2,1,0:T(8,128)S(1)} %bitcast.4, ...), custom_call_target="tpu_custom_call", output_to_operand_aliasing={{0}: (5, {}), {1}: (6, {})} | custom-call | bytes 2097152 | tf_op jit(solution)/shard_map/apply_blocks/pallas_call | solution.py:58
  70.8 1.4 %apply_blocks.10 = (bf16[8,1024,256]{2,1,0:T(8,128)(2,1)}, f32[8,1024,256]{2,1,0:T(8,128)}) custom-call(s32[8,128]{1,0:T(8,128)S(1)} %broadcast_in_dim.31.modules_ref, bf16[8,1024,256]{2,1,0:T(8,128)(2,1)S(1)} %copy-done, f32[8,1024,256]{2,1,0:T(8,128)S(1)} %bitcast.4, ...), custom_call_target="tpu_custom_call", output_to_operand_aliasing={{0}: (5, {}), {1}: (6, {})} | custom-call | bytes 1048576 | tf_op jit(solution)/shard_map/apply_blocks/pallas_call | solution.py:58
  72.2 0.5 collective-permute-done.15.refs_1_
  72.8 1.3 %apply_blocks.11 = (bf16[8,1024,256]{2,1,0:T(8,128)(2,1)}, f32[8,1024,256]{2,1,0:T(8,128)}) custom-call(s32[8,128]{1,0:T(8,128)S(1)} %broadcast_in_dim.31.modules_ref, bf16[8,1024,256]{2,1,0:T(8,128)(2,1)S(1)} %copy-done, f32[8,1024,256]{2,1,0:T(8,128)S(1)} %bitcast.4, ...), custom_call_target="tpu_custom_call", output_to_operand_aliasing={{0}: (5, {}), {1}: (6, {})} | custom-call | bytes 1048576 | tf_op jit(solution)/shard_map/apply_blocks/pallas_call | solution.py:58
  (25 shorter events, 0.1 us)
Async XLA Ops:
  0.6 5.1 %copy-start.1 = (bf16[1,256,4096]{2,1,0:T(8,128)(2,1)S(1)}, bf16[1,256,4096]{2,1,0:T(8,128)(2,1)}, u32[]{:S(2)}) copy-start(bf16[1,256,4096]{2,1,0:T(8,128)(2,1)} %tokens_ref.5) | copy-start | bytes 6291460
  0.6 8.1 %copy-start.2 = (bf16[1,256,256]{2,1,0:T(8,128)(2,1)S(1)}, bf16[1,256,256]{2,1,0:T(8,128)(2,1)}, u32[]{:S(2)}) copy-start(bf16[1,256,256]{2,1,0:T(8,128)(2,1)} %param.7) | copy-start | bytes 393220
  0.6 0.8 %copy-start.3 = (s32[8,1]{0,1:T(1,128)S(1)}, s32[8,1]{0,1:T(1,128)}, u32[]{:S(2)}) copy-start(s32[8,1]{0,1:T(1,128)} %param.8) | copy-start | bytes 100
  1.5 6.6 %copy-start.5 = (s32[8]{0:T(128)S(1)}, s32[8]{0:T(128)}, u32[]{:S(2)}) copy-start(s32[8]{0:T(128)} %constant.28.clone) | copy-start | bytes 100
  1.5 8.1 %copy-start.4 = (s32[8,1]{0,1:T(1,128)S(1)}, s32[8,1]{0,1:T(1,128)}, u32[]{:S(2)}) copy-start(s32[8,1]{0,1:T(1,128)} %param.8) | copy-start | bytes 100
  2.7 14.9 %collective-permute-start.5 = (bf16[1024,256]{1,0:T(8,128)(2,1)S(1)}, bf16[1024,256]{1,0:T(8,128)(2,1)S(1)}, u32[]{:S(2)}, u32[]{:S(2)}) collective-permute-start(bf16[1024,256]{1,0:T(8,128)(2,1)S(1)} %pick_rows.1.after_ref.weights_ref), channel_id=1, source_target_pairs={{0,2},{1,3},{2,0},{3,1},{4,6},{5,7},{6,4},{7,5},{8,10},{9,11},{10,... | collective-permute-start | bytes 1572872 | tf_op jit(solution)/shard_map/ppermute | solution.py:239
  7.0 1.8 %collective-permute-start = (bf16[64,2048]{1,0:T(8,128)(2,1)}, bf16[64,2048]{1,0:T(8,128)(2,1)S(1)}, u32[]{:S(2)}, u32[]{:S(2)}) collective-permute-start(bf16[64,2048]{1,0:T(8,128)(2,1)} %get-tuple-element.41), channel_id=1, source_target_pairs={{0,1},{1,0},{2,3},{3,2},{4,5},{5,4},{6,7},{7,6},{8,9},{9,8},{10,11... | collective-permute-start | bytes 786440 | tf_op jit(solution)/shard_map/ppermute | solution.py:246
  7.0 2.7 %collective-permute-start.1 = (bf16[64,2048]{1,0:T(8,128)(2,1)}, bf16[64,2048]{1,0:T(8,128)(2,1)}, u32[]{:S(2)}, u32[]{:S(2)}) collective-permute-start(bf16[64,2048]{1,0:T(8,128)(2,1)} %get-tuple-element.42), channel_id=1, source_target_pairs={{0,1},{1,0},{2,3},{3,2},{4,5},{5,4},{6,7},{7,6},{8,9},{9,8},{10,11... | collective-permute-start | bytes 786440 | tf_op jit(solution)/shard_map/ppermute | solution.py:246
  7.5 2.2 %collective-permute-start.2 = (bf16[64,2048]{1,0:T(8,128)(2,1)}, bf16[64,2048]{1,0:T(8,128)(2,1)}, u32[]{:S(2)}, u32[]{:S(2)}) collective-permute-start(bf16[64,2048]{1,0:T(8,128)(2,1)} %get-tuple-element.43), channel_id=1, source_target_pairs={{0,1},{1,0},{2,3},{3,2},{4,5},{5,4},{6,7},{7,6},{8,9},{9,8},{10,11... | collective-permute-start | bytes 786440 | tf_op jit(solution)/shard_map/ppermute | solution.py:246
  7.6 2.4 %collective-permute-start.3 = (bf16[64,2048]{1,0:T(8,128)(2,1)}, bf16[64,2048]{1,0:T(8,128)(2,1)}, u32[]{:S(2)}, u32[]{:S(2)}) collective-permute-start(bf16[64,2048]{1,0:T(8,128)(2,1)} %get-tuple-element.44), channel_id=1, source_target_pairs={{0,1},{1,0},{2,3},{3,2},{4,5},{5,4},{6,7},{7,6},{8,9},{9,8},{10,11... | collective-permute-start | bytes 786440 | tf_op jit(solution)/shard_map/ppermute | solution.py:246
  8.8 3.2 %collective-permute-start.4 = (bf16[256,256]{1,0:T(8,128)(2,1)S(1)}, bf16[256,256]{1,0:T(8,128)(2,1)S(1)}, u32[]{:S(2)}, u32[]{:S(2)}) collective-permute-start(bf16[256,256]{1,0:T(8,128)(2,1)S(1)} %bitcast.5), channel_id=1, source_target_pairs={{0,1},{1,0},{2,3},{3,2},{4,5},{5,4},{6,7},{7,6},{8,9},{9,8},{10,11... | collective-permute-start | bytes 393224 | tf_op jit(solution)/shard_map/ppermute | solution.py:245
  10.0 36.9 %slice-start = ((s8[8388608]{0:T(1024)(128)(4,1)}), s8[4194304]{0:T(1024)(128)(4,1)S(1)}, s32[]{:S(2)}) async-start(s8[8388608]{0:T(1024)(128)(4,1)} %bitcast.3), calls=%async_computation | async-start | bytes 8388608
  17.6 29.3 %slice-start.1 = ((s8[8388608]{0:T(1024)(128)(4,1)}), s8[4194304]{0:T(1024)(128)(4,1)S(1)}, s32[]{:S(2)}) async-start(s8[8388608]{0:T(1024)(128)(4,1)} %bitcast.3), calls=%async_computation.1 | async-start | bytes 8388608
  18.1 28.8 %copy-start = (bf16[8,1024,256]{2,1,0:T(8,128)(2,1)S(1)}, bf16[8,1024,256]{2,1,0:T(8,128)(2,1)}, u32[]{:S(2)}) copy-start(bf16[8,1024,256]{2,1,0:T(8,128)(2,1)} %weights_ref.13) | copy-start | bytes 12582916
  18.1 1.6 %collective-permute-start.6 = (bf16[512,256]{1,0:T(8,128)(2,1)S(1)}, bf16[512,256]{1,0:T(8,128)(2,1)S(1)}, u32[]{:S(2)}, u32[]{:S(2)}) collective-permute-start(bf16[512,256]{1,0:T(8,128)(2,1)S(1)} %get-tuple-element.51), channel_id=1, source_target_pairs={{0,1},{1,0},{2,3},{3,2},{4,5},{5,4},{6,7},{7,6},{8,9},{9,8},{10,11... | collective-permute-start | bytes 786440 | tf_op jit(solution)/shard_map/ppermute | solution.py:265
  20.2 9.2 %collective-permute-start.16 = (bf16[512,256]{1,0:T(8,128)(2,1)S(1)}, bf16[512,256]{1,0:T(8,128)(2,1)S(1)}, u32[]{:S(2)}, u32[]{:S(2)}) collective-permute-start(bf16[512,256]{1,0:T(8,128)(2,1)S(1)} %get-tuple-element.59), channel_id=1, source_target_pairs={{0,2},{1,3},{2,0},{3,1},{4,6},{5,7},{6,4},{7,5},{8,10},{9,11},{10,... | collective-permute-start | bytes 786440 | tf_op jit(solution)/shard_map/ppermute | solution.py:289
  22.6 11.6 %collective-permute-start.7 = (bf16[512,256]{1,0:T(8,128)(2,1)S(1)}, bf16[512,256]{1,0:T(8,128)(2,1)S(1)}, u32[]{:S(2)}, u32[]{:S(2)}) collective-permute-start(bf16[512,256]{1,0:T(8,128)(2,1)S(1)} %get-tuple-element.55), channel_id=1, source_target_pairs={{0,2},{1,3},{2,0},{3,1},{4,6},{5,7},{6,4},{7,5},{8,10},{9,11},{10,... | collective-permute-start | bytes 786440 | tf_op jit(solution)/shard_map/ppermute | solution.py:289
  29.5 6.9 %collective-permute-start.17 = (bf16[512,256]{1,0:T(8,128)(2,1)S(1)}, bf16[512,256]{1,0:T(8,128)(2,1)S(1)}, u32[]{:S(2)}, u32[]{:S(2)}) collective-permute-start(bf16[512,256]{1,0:T(8,128)(2,1)S(1)} %multiply_convert_fusion.refs_0_), channel_id=1, source_target_pairs={{0,8},{4,0},{8,16},{12,4},{16,24},{20,12},{24,28},{28,20},{1,9},{5... | collective-permute-start | bytes 786440 | tf_op jit(solution)/shard_map/ppermute | solution.py:336
  31.4 7.8 %collective-permute-start.19 = (bf16[512,256]{1,0:T(8,128)(2,1)S(1)}, bf16[512,256]{1,0:T(8,128)(2,1)S(1)}, u32[]{:S(2)}, u32[]{:S(2)}) collective-permute-start(bf16[512,256]{1,0:T(8,128)(2,1)S(1)} %multiply_convert_fusion.refs_0_), channel_id=1, source_target_pairs={{0,4},{4,12},{8,0},{12,20},{16,8},{20,28},{24,16},{28,24},{1,5},{5... | collective-permute-start | bytes 786440 | tf_op jit(solution)/shard_map/ppermute | solution.py:336
  34.4 10.5 %collective-permute-start.8 = (bf16[512,256]{1,0:T(8,128)(2,1)S(1)}, bf16[512,256]{1,0:T(8,128)(2,1)S(1)}, u32[]{:S(2)}, u32[]{:S(2)}) collective-permute-start(bf16[512,256]{1,0:T(8,128)(2,1)S(1)} %multiply_convert_fusion.1.refs_3_), channel_id=1, source_target_pairs={{0,4},{4,12},{8,0},{12,20},{16,8},{20,28},{24,16},{28,24},{1,5},{5... | collective-permute-start | bytes 786440 | tf_op jit(solution)/shard_map/ppermute | solution.py:336
  36.2 9.2 %collective-permute-start.12 = (bf16[512,256]{1,0:T(8,128)(2,1)S(1)}, bf16[512,256]{1,0:T(8,128)(2,1)S(1)}, u32[]{:S(2)}, u32[]{:S(2)}) collective-permute-start(bf16[512,256]{1,0:T(8,128)(2,1)S(1)} %multiply_convert_fusion.1.refs_3_), channel_id=1, source_target_pairs={{0,8},{4,0},{8,16},{12,4},{16,24},{20,12},{24,28},{28,20},{1,9},{5... | collective-permute-start | bytes 786440 | tf_op jit(solution)/shard_map/ppermute | solution.py:336
  36.4 14.6 %collective-permute-start.18 = (bf16[512,256]{1,0:T(8,128)(2,1)S(1)}, bf16[512,256]{1,0:T(8,128)(2,1)S(1)}, u32[]{:S(2)}, u32[]{:S(2)}) collective-permute-start(bf16[512,256]{1,0:T(8,128)(2,1)S(1)} %collective-permute-done.17.refs_1_), channel_id=1, source_target_pairs={{0,8},{4,0},{8,16},{12,4},{16,24},{20,12},{24,28},{28,20},{1,9},{5... | collective-permute-start | bytes 786440 | tf_op jit(solution)/shard_map/ppermute | solution.py:336
  39.3 11.8 %collective-permute-start.20 = (bf16[512,256]{1,0:T(8,128)(2,1)S(1)}, bf16[512,256]{1,0:T(8,128)(2,1)S(1)}, u32[]{:S(2)}, u32[]{:S(2)}) collective-permute-start(bf16[512,256]{1,0:T(8,128)(2,1)S(1)} %collective-permute-done.19.refs_2_), channel_id=1, source_target_pairs={{0,4},{4,12},{8,0},{12,20},{16,8},{20,28},{24,16},{28,24},{1,5},{5... | collective-permute-start | bytes 786440 | tf_op jit(solution)/shard_map/ppermute | solution.py:336
  44.9 11.2 %collective-permute-start.9 = (bf16[512,256]{1,0:T(8,128)(2,1)S(1)}, bf16[512,256]{1,0:T(8,128)(2,1)S(1)}, u32[]{:S(2)}, u32[]{:S(2)}) collective-permute-start(bf16[512,256]{1,0:T(8,128)(2,1)S(1)} %collective-permute-done.8.refs_4_), channel_id=1, source_target_pairs={{0,4},{4,12},{8,0},{12,20},{16,8},{20,28},{24,16},{28,24},{1,5},{5... | collective-permute-start | bytes 786440 | tf_op jit(solution)/shard_map/ppermute | solution.py:336
  45.4 11.2 %collective-permute-start.13 = (bf16[512,256]{1,0:T(8,128)(2,1)S(1)}, bf16[512,256]{1,0:T(8,128)(2,1)S(1)}, u32[]{:S(2)}, u32[]{:S(2)}) collective-permute-start(bf16[512,256]{1,0:T(8,128)(2,1)S(1)} %collective-permute-done.12.refs_5_), channel_id=1, source_target_pairs={{0,8},{4,0},{8,16},{12,4},{16,24},{20,12},{24,28},{28,20},{1,9},{5... | collective-permute-start | bytes 786440 | tf_op jit(solution)/shard_map/ppermute | solution.py:336
  51.0 11.2 %collective-permute-start.21 = (bf16[512,256]{1,0:T(8,128)(2,1)S(1)}, bf16[512,256]{1,0:T(8,128)(2,1)S(1)}, u32[]{:S(2)}, u32[]{:S(2)}) collective-permute-start(bf16[512,256]{1,0:T(8,128)(2,1)S(1)} %collective-permute-done.18.refs_0_), channel_id=1, source_target_pairs={{0,8},{4,0},{8,16},{12,4},{16,24},{20,12},{24,28},{28,20},{1,9},{5... | collective-permute-start | bytes 786440 | tf_op jit(solution)/shard_map/ppermute | solution.py:336
  51.9 10.4 %collective-permute-start.22 = (bf16[512,256]{1,0:T(8,128)(2,1)S(1)}, bf16[512,256]{1,0:T(8,128)(2,1)S(1)}, u32[]{:S(2)}, u32[]{:S(2)}) collective-permute-start(bf16[512,256]{1,0:T(8,128)(2,1)S(1)} %collective-permute-done.20.refs_1_), channel_id=1, source_target_pairs={{0,4},{4,12},{8,0},{12,20},{16,8},{20,28},{24,16},{28,24},{1,5},{5... | collective-permute-start | bytes 786440 | tf_op jit(solution)/shard_map/ppermute | solution.py:336
  56.1 10.9 %collective-permute-start.10 = (bf16[512,256]{1,0:T(8,128)(2,1)S(1)}, bf16[512,256]{1,0:T(8,128)(2,1)S(1)}, u32[]{:S(2)}, u32[]{:S(2)}) collective-permute-start(bf16[512,256]{1,0:T(8,128)(2,1)S(1)} %collective-permute-done.9.refs_2_), channel_id=1, source_target_pairs={{0,4},{4,12},{8,0},{12,20},{16,8},{20,28},{24,16},{28,24},{1,5},{5... | collective-permute-start | bytes 786440 | tf_op jit(solution)/shard_map/ppermute | solution.py:336
  56.7 11.1 %collective-permute-start.14 = (bf16[512,256]{1,0:T(8,128)(2,1)S(1)}, bf16[512,256]{1,0:T(8,128)(2,1)S(1)}, u32[]{:S(2)}, u32[]{:S(2)}) collective-permute-start(bf16[512,256]{1,0:T(8,128)(2,1)S(1)} %collective-permute-done.13.refs_3_), channel_id=1, source_target_pairs={{0,8},{4,0},{8,16},{12,4},{16,24},{20,12},{24,28},{28,20},{1,9},{5... | collective-permute-start | bytes 786440 | tf_op jit(solution)/shard_map/ppermute | solution.py:336
  64.0 6.8 %collective-permute-start.23 = (bf16[256,256]{1,0:T(8,128)(2,1)S(1)}, bf16[256,256]{1,0:T(8,128)(2,1)S(1)}, u32[]{:S(2)}, u32[]{:S(2)}) collective-permute-start(bf16[256,256]{1,0:T(8,128)(2,1)S(1)} %slice.18), channel_id=1, source_target_pairs={{0,8},{4,0},{8,16},{12,4},{16,24},{20,12},{24,28},{28,20},{1,9},{5... | collective-permute-start | bytes 393224 | tf_op jit(solution)/shard_map/ppermute | solution.py:336
  64.9 6.0 %collective-permute-start.24 = (bf16[256,256]{1,0:T(8,128)(2,1)S(1)}, bf16[256,256]{1,0:T(8,128)(2,1)S(1)}, u32[]{:S(2)}, u32[]{:S(2)}) collective-permute-start(bf16[256,256]{1,0:T(8,128)(2,1)S(1)} %slice.19), channel_id=1, source_target_pairs={{0,4},{4,12},{8,0},{12,20},{16,8},{20,28},{24,16},{28,24},{1,5},{5... | collective-permute-start | bytes 393224 | tf_op jit(solution)/shard_map/ppermute | solution.py:336
  67.0 5.2 %collective-permute-start.11 = (bf16[256,256]{1,0:T(8,128)(2,1)S(1)}, bf16[256,256]{1,0:T(8,128)(2,1)S(1)}, u32[]{:S(2)}, u32[]{:S(2)}) collective-permute-start(bf16[256,256]{1,0:T(8,128)(2,1)S(1)} %slice.16), channel_id=1, source_target_pairs={{0,4},{4,12},{8,0},{12,20},{16,8},{20,28},{24,16},{28,24},{1,5},{5... | collective-permute-start | bytes 393224 | tf_op jit(solution)/shard_map/ppermute | solution.py:336
  67.7 5.0 %collective-permute-start.15 = (bf16[256,256]{1,0:T(8,128)(2,1)S(1)}, bf16[256,256]{1,0:T(8,128)(2,1)S(1)}, u32[]{:S(2)}, u32[]{:S(2)}) collective-permute-start(bf16[256,256]{1,0:T(8,128)(2,1)S(1)} %slice.17), channel_id=1, source_target_pairs={{0,8},{4,0},{8,16},{12,4},{16,24},{20,12},{24,28},{28,20},{1,9},{5... | collective-permute-start | bytes 393224 | tf_op jit(solution)/shard_map/ppermute | solution.py:336
